TPU v7x, 32 devices: a whole 2x2x4 slice. The times are simulated.
32 devices in a mesh: gx: 4 (over z), gy: 8 (over y, x, core).
Axes of the slice: x: 2, y: 2, z: 4, core: 2. Of those that a mesh axis runs over, the one named last changes fastest.
Arguments:
- coords: float32 [1, 3, 8, 16, 128], P(None, None, 'gx', 'gy'), may hold values from 0 to 1
- kinds: int32 [8, 16, 128], P('gx', 'gy'), may hold values from 0 to 2
- forces: bfloat16 [1, 3, 8, 16, 128], P(None, None, 'gx', 'gy'), may hold values from -4 to 4
- tile_offsets: int32 [1, 8, 16, 8], P(None, 'gx', 'gy'), may hold values from 0 to 8, as said below
- tile_mask: int32 [1, 8, 16, 8], P(None, 'gx', 'gy'), may hold values 0 or 1
Outputs:
- gram: float32 [1, 1536, 1536], P(None, 'gy')
- rhs: float32 [1, 1536], P(None, 'gy')
Inputs may be any that keep to these rules, and one draw needn't show every extreme that they name: `tile_offsets`: for one frame and block the 8 entries are distinct; entry o names the block o // 3 - 1 steps along the first direction and o % 3 - 1 along the second, periodically.
All inputs are finite; a program needn't handle non-finite values. No bound on the sum of `tile_mask` on one device may be relied on, other than what follows from the above.
Results may differ from a plain program's by a relative error of at most 0.0013.
Values sent between devices are 32-bit elements; how exact they have to be, the bound alone decides.
No kernel may reach another device: no remote copies, remote signals or barrier semaphores. Data moves between devices by JAX's collectives and lax.ppermute only.
A program may use at most 128 MiB of HBM per device.

v0:
```python
import jax
import jax.numpy as jnp
from jax import lax
from jax.sharding import PartitionSpec as P

K = 256
PAIRS = 6


RCUT = 1.0
SOFT = 0.05


def extended(cells, sides, width):
    for axis, dim in sides:
        count = lax.axis_size(axis)
        head = lax.slice_in_dim(cells, 0, width, axis=dim)
        tail = lax.slice_in_dim(cells, cells.shape[dim] - width, cells.shape[dim], axis=dim)
        cells = jnp.concatenate(
            [
                lax.ppermute(tail, axis, [(i, (i + 1) % count) for i in range(count)]),
                cells,
                lax.ppermute(head, axis, [((i + 1) % count, i) for i in range(count)]),
            ],
            axis=dim,
        )
    return cells


def radial(r2):
    dist = jnp.sqrt(r2)
    centers = RCUT * (jnp.arange(K, dtype=jnp.float32) + 0.5) / K
    spread = RCUT / K
    taper = jnp.square(jnp.maximum(1.0 - r2 / (RCUT * RCUT), 0.0))
    scaled = (dist[..., None] - centers) / spread
    return (jnp.exp(-0.5 * scaled * scaled) * taper[..., None]).astype(jnp.bfloat16)


def couplings(center, source, kind_center, kind_source, offset, live):
    beads = center.shape[1]
    shift = jnp.stack([offset // 3 - 1, offset % 3 - 1, 0 * offset]).astype(jnp.float32)
    delta = center[:, :, None] - source[:, None, :] - shift[:, None, None]
    r2 = jnp.sum(delta * delta, axis=0)
    lower_kind = jnp.minimum(kind_center[:, None], kind_source[None, :])
    upper_kind = jnp.maximum(kind_center[:, None], kind_source[None, :])
    pair_kind = lower_kind * (5 - lower_kind) // 2 + upper_kind
    select = (pair_kind[None] == jnp.arange(PAIRS, dtype=jnp.int32)[:, None, None]).astype(
        jnp.float32
    )
    scale = live.astype(jnp.float32) / jnp.sqrt(r2 + SOFT)
    weight = (delta[:, None] * select[None] * scale[None, None]).reshape(3 * PAIRS, beads, beads)
    return (weight.astype(jnp.bfloat16), radial(r2))


def shards(coords, kinds, forces, tile_offsets, tile_mask):
    frames = coords.shape[0]
    blocks_x = coords.shape[2]
    blocks_y = coords.shape[3]
    beads = coords.shape[4]
    slots = tile_offsets.shape[3]
    width = PAIRS * K
    size_x = lax.axis_size("gx")
    size_y = lax.axis_size("gy")
    frame_rows = 3 * beads * blocks_x * blocks_y * size_x * size_y
    beside_all = extended(coords, (("gx", 2), ("gy", 3)), 1)
    kind_around = extended(kinds, (("gx", 0), ("gy", 1)), 1)

    def frame_terms(carry, frame):
        field = lax.dynamic_index_in_dim(beside_all, frame, 0, keepdims=False)
        force_now = lax.dynamic_index_in_dim(forces, frame, 0, keepdims=False)
        stacked = []
        targets = []
        for block_x in range(blocks_x):
            for block_y in range(blocks_y):
                nearby = field[:, block_x : block_x + 3, block_y : block_y + 3, :].reshape(
                    3, 9, beads
                )
                kind_near = kind_around[block_x : block_x + 3, block_y : block_y + 3, :].reshape(
                    9, beads
                )
                center = nearby[:, 4]
                kind_center = kind_near[4]
                design = jnp.zeros((beads, 3 * PAIRS, K), jnp.float32)
                for slot in range(slots):
                    offset = tile_offsets[frame, block_x, block_y, slot]
                    source = lax.dynamic_index_in_dim(nearby, offset, 1, keepdims=False)
                    kind_source = lax.dynamic_index_in_dim(kind_near, offset, 0, keepdims=False)
                    weight, basis = couplings(
                        center,
                        source,
                        kind_center,
                        kind_source,
                        offset,
                        tile_mask[frame, block_x, block_y, slot],
                    )
                    design = design + jnp.einsum(
                        "cij,ijk->ick", weight, basis, preferred_element_type=jnp.float32
                    )
                stacked.append(design.astype(jnp.bfloat16).reshape(beads * 3, width))
                targets.append(force_now[:, block_x, block_y, :].T.reshape(beads * 3))
        design_rows = jnp.concatenate(stacked, axis=0)
        target_force = jnp.concatenate(targets, axis=0)
        gram_frame = lax.dot_general(
            design_rows, design_rows, (((0,), (0,)), ((), ())), preferred_element_type=jnp.float32
        )
        rhs_frame = jnp.dot(target_force, design_rows, preferred_element_type=jnp.float32)
        return (carry, (gram_frame / frame_rows, rhs_frame / frame_rows))

    _, (gram, rhs) = lax.scan(frame_terms, 0, jnp.arange(frames, dtype=jnp.int32))
    gram_part, rhs_part = (
        lax.psum_scatter(gram, "gy", scatter_dimension=1, tiled=True),
        lax.psum_scatter(rhs, "gy", scatter_dimension=1, tiled=True),
    )
    gram_rows, rhs_rows = lax.psum((gram_part, rhs_part), "gx")
    return (gram_rows, rhs_rows)


def solution(mesh):
    placed = (
        P(None, None, "gx", "gy", None),
        P("gx", "gy", None),
        P(None, None, "gx", "gy", None),
        P(None, "gx", "gy", None),
        P(None, "gx", "gy", None),
    )
    return jax.shard_map(
        shards,
        mesh=mesh,
        in_specs=placed,
        out_specs=(P(None, "gy", None), P(None, "gy")),
        check_vma=False,
    )
```

profile of v0, /device:TPU:1, one launch (start us, length us, event | category | flops | bytes accessed | tf_op | source)
XLA Modules:
  0.0 579.8 jit_solution(13585154460078518301)
XLA Ops:
  7.9 2.1 collective-permute-start.4
  10.0 2.0 collective-permute-start.5
  12.8 3.3 collective-permute-start.1
  16.0 1.9 fusion.594
  25.5 1.8 fusion.595
  44.7 1.9 fusion.592
  46.7 1.8 fusion.593
  147.1 2.9 collective-permute-start.6
  174.7 1.0 fusion.279
  175.6 1.0 fusion.277
  176.7 1.0 fusion.275
  179.2 1.0 fusion.269
  180.2 1.0 fusion.267
  181.1 1.0 fusion.265
  182.2 1.8 collective-permute-start.2
  184.4 1.0 fusion.271
  185.4 2.1 collective-permute-done.3
  191.1 4.7 fusion.133
  195.7 4.7 fusion.135
  200.4 4.8 fusion.137
  205.2 4.7 fusion.139
  209.9 4.9 fusion.141
  214.7 4.7 fusion.129
  219.4 4.7 fusion.131
  224.1 9.6 %add_convert_fusion = bf16[128,18,256]{2,1,0:T(8,128)(2,1)} fusion(f32[128,18,256]{2,1,0:T(8,128)S(1)} %fusion.129, f32[128,18,256]{2,1,0:T(8,128)S(1)} %fusion.131, f32[128,18,256]{2,1,0:T(8,128)S(1)} %fusion.133, f32[128,18,256]{2,1,0:T(8,128)S(1)} %fusion.135, f32[128,18,256]{2,1,0:T(8,128)S(1)} %fusion.137, f32[128,18,256]{2,1,0:T(8,128)S(1)} %fusion.139, ...), kind=kOutput, calls=%fused_computation.226 | convolution fusion | flops 180879360 | bytes 18416640 | tf_op jit(solution)/shard_map/while/body/eval_jaxpr/cij,ijk->ick/dot_general | solution.py:96
  233.7 3.9 reshape.4060
  240.6 4.7 fusion.145
  245.2 4.7 fusion.147
  249.9 4.8 fusion.149
  254.7 4.7 fusion.151
  259.4 4.9 fusion.153
  264.3 4.7 fusion.155
  268.9 4.7 fusion.157
  273.7 8.9 %add_convert_fusion.1 = bf16[128,18,256]{2,1,0:T(8,128)(2,1)S(1)} fusion(f32[128,18,256]{2,1,0:T(8,128)S(1)} %fusion.145, f32[128,18,256]{2,1,0:T(8,128)S(1)} %fusion.147, f32[128,18,256]{2,1,0:T(8,128)S(1)} %fusion.149, f32[128,18,256]{2,1,0:T(8,128)S(1)} %fusion.151, f32[128,18,256]{2,1,0:T(8,128)S(1)} %fusion.153, f32[128,18,256]{2,1,0:T(8,128)S(1)} %fusion.155, ...), kind=kOutput, calls=%fused_computation.227 | convolution fusion | flops 180879360 | bytes 18416640 | tf_op jit(solution)/shard_map/while/body/eval_jaxpr/cij,ijk->ick/dot_general | solution.py:96
  282.7 2.3 reshape.4057
  288.1 4.7 fusion.161
  292.8 4.7 fusion.163
  297.5 4.8 fusion.165
  302.3 4.7 fusion.167
  306.9 4.9 fusion.169
  311.8 4.7 fusion.171
  316.5 4.7 fusion.173
  321.2 9.6 %add_convert_fusion.2 = bf16[128,18,256]{2,1,0:T(8,128)(2,1)} fusion(f32[128,18,256]{2,1,0:T(8,128)S(1)} %fusion.161, f32[128,18,256]{2,1,0:T(8,128)S(1)} %fusion.163, f32[128,18,256]{2,1,0:T(8,128)S(1)} %fusion.165, f32[128,18,256]{2,1,0:T(8,128)S(1)} %fusion.167, f32[128,18,256]{2,1,0:T(8,128)S(1)} %fusion.169, f32[128,18,256]{2,1,0:T(8,128)S(1)} %fusion.171, ...), kind=kOutput, calls=%fused_computation.228 | convolution fusion | flops 180879360 | bytes 18416640 | tf_op jit(solution)/shard_map/while/body/eval_jaxpr/cij,ijk->ick/dot_general | solution.py:96
  330.9 3.2 reshape.4054
  337.3 4.7 fusion.183
  341.9 4.7 fusion.185
  346.6 4.8 fusion.187
  351.4 4.7 fusion.189
  356.1 4.9 fusion.181
  360.9 4.7 fusion.179
  365.6 4.7 fusion.177
  370.3 9.6 %add_convert_fusion.3 = bf16[128,18,256]{2,1,0:T(8,128)(2,1)} fusion(f32[128,18,256]{2,1,0:T(8,128)S(1)} %fusion.177, f32[128,18,256]{2,1,0:T(8,128)S(1)} %fusion.179, f32[128,18,256]{2,1,0:T(8,128)S(1)} %fusion.181, f32[128,18,256]{2,1,0:T(8,128)S(1)} %fusion.183, f32[128,18,256]{2,1,0:T(8,128)S(1)} %fusion.185, f32[128,18,256]{2,1,0:T(8,128)S(1)} %fusion.187, ...), kind=kOutput, calls=%fused_computation.229 | convolution fusion | flops 180879360 | bytes 18416640 | tf_op jit(solution)/shard_map/while/body/eval_jaxpr/cij,ijk->ick/dot_general | solution.py:96
  379.9 3.9 reshape.4051
  383.8 1.3 constant_dynamic-update-slice_fusion.9
  385.4 2.2 copy-done
  387.6 10.3 %fusion.128 = f32[1,1536,1536]{2,1,0:T(8,128)} fusion(bf16[1536,1536]{1,0:T(8,128)(2,1)S(1)} %constant_dynamic-update-slice_fusion.6), kind=kOutput, calls=%fused_computation.193 | convolution fusion | flops 7250116608 | bytes 14155776 | tf_op jit(solution)/shard_map/while/body/eval_jaxpr/dot_general | solution.py:103
  400.2 3.1 convolution_reduce_fusion
  403.3 1.1 reshape_bitcast_fusion
  404.5 68.7 %reduce-scatter.5.cloned.1.call-done = f32[1,192,1536]{2,1,0:T(8,128)} async-done(((f32[1,1536,1536]{2,1,0:T(8,128)}), f32[1,192,1536]{2,1,0:T(8,128)}) %reduce-scatter.5.cloned.1.call-update) | async-done | bytes 1179664 | tf_op jit(solution)/shard_map/reduce_scatter | solution.py:111
  473.2 38.4 %reduce-scatter.7.cloned.1.call-done = f32[192,1]{1,0:T(8,128)} async-done(((f32[1536,1]{1,0:T(8,128)}), f32[192,1]{1,0:T(8,128)}) %reduce-scatter.7.cloned.1.call-update) | async-done | bytes 784
  511.7 1.0 copy.92
  512.6 10.3 %psum.15 = f32[1,192]{1,0:T(1,128)} all-reduce(f32[1,192]{1,0:T(1,128)S(1)} %copy.92), channel_id=1, replica_groups=mesh['gx'=4,'gy'=8] {'gx'}, use_global_device_ids=true, to_apply=%region_35.36 | all-reduce | flops 192 | bytes 1536 | tf_op jit(solution)/shard_map/psum | solution.py:114
  522.9 47.6 %all-reduce.2.cloned.1.call-done = f32[1,192,1536]{2,1,0:T(8,128)} async-done(((f32[1,192,1536]{2,1,0:T(8,128)}), f32[1,192,1536]{2,1,0:T(8,128)}) %all-reduce.2.cloned.1.call-update) | async-done | bytes 1179664 | tf_op jit(solution)/shard_map/psum | solution.py:114
  570.5 2.4 copy.173
  (269 shorter events, 26.0 us)
Async XLA Ops:
  7.2 466.0 %reduce-scatter.5.cloned.1.call-start = ((), (), s32[]{:S(2)}) async-start(), calls=%async_computation.2 | async-start | bytes 10616832 | tf_op jit(solution)/shard_map/reduce_scatter | solution.py:111
  7.9 138.5 %collective-permute-start.4 = (s32[1,2,128]{2,1,0:T(2,128)S(1)}, s32[1,2,128]{2,1,0:T(2,128)S(1)}, u32[]{:S(2)}, u32[]{:S(2)}) collective-permute-start(s32[1,2,128]{2,1,0:T(2,128)S(1)} %get-tuple-element.343), channel_id=1, source_target_pairs={{0,8},{8,16},{16,24},{24,0},{1,9},{9,17},{17,25},{25,1},{2,10},{10... | collective-permute-start | bytes 3080 | tf_op jit(solution)/shard_map/ppermute | solution.py:21
  10.0 137.1 %collective-permute-start.5 = (s32[1,2,128]{2,1,0:T(2,128)S(1)}, s32[1,2,128]{2,1,0:T(2,128)S(1)}, u32[]{:S(2)}, u32[]{:S(2)}) collective-permute-start(s32[1,2,128]{2,1,0:T(2,128)S(1)} %get-tuple-element.342), channel_id=1, source_target_pairs={{8,0},{16,8},{24,16},{0,24},{9,1},{17,9},{25,17},{1,25},{10,2},{18... | collective-permute-start | bytes 3080 | tf_op jit(solution)/shard_map/ppermute | solution.py:23
  12.8 169.4 %collective-permute-start = (f32[1,3,1,2,128]{4,3,2,1,0:T(2,128)S(1)}, f32[1,3,1,2,128]{4,3,2,1,0:T(2,128)S(1)}, u32[]{:S(2)}, u32[]{:S(2)}) collective-permute-start(f32[1,3,1,2,128]{4,3,2,1,0:T(2,128)S(1)} %get-tuple-element.237), channel_id=1, source_target_pairs={{0,8},{8,16},{16,24},{24,0},{1,9},{9,17},{17,25},{25,1},{2,10},{10... | collective-permute-start | bytes 9224 | tf_op jit(solution)/shard_map/ppermute | solution.py:21
  12.8 169.4 %collective-permute-start.1 = (f32[1,3,1,2,128]{4,3,2,1,0:T(2,128)S(1)}, f32[1,3,1,2,128]{4,3,2,1,0:T(2,128)S(1)}, u32[]{:S(2)}, u32[]{:S(2)}) collective-permute-start(f32[1,3,1,2,128]{4,3,2,1,0:T(2,128)S(1)} %get-tuple-element.236), channel_id=1, source_target_pairs={{8,0},{16,8},{24,16},{0,24},{9,1},{17,9},{25,17},{1,25},{10,2},{18... | collective-permute-start | bytes 9224 | tf_op jit(solution)/shard_map/ppermute | solution.py:23
  128.1 54.1 %copy-start.21 = (f32[1,3,2,2,128]{4,3,2,1,0:T(2,128)S(1)}, f32[1,3,2,2,128]{4,3,2,1,0:T(2,128)}, u32[]{:S(2)}) copy-start(f32[1,3,2,2,128]{4,3,2,1,0:T(2,128)} %param.5) | copy-start | bytes 18436
  147.1 25.2 %collective-permute-start.6 = (s32[4,1,128]{2,1,0:T(1,128)S(1)}, s32[4,1,128]{2,1,0:T(1,128)S(1)}, u32[]{:S(2)}, u32[]{:S(2)}) collective-permute-start(s32[4,1,128]{2,1,0:T(1,128)S(1)} %get-tuple-element.273), channel_id=1, source_target_pairs={{0,1},{1,2},{2,3},{3,4},{4,5},{5,6},{6,7},{7,0},{8,9},{9,10},{10,1... | collective-permute-start | bytes 6152 | tf_op jit(solution)/shard_map/ppermute | solution.py:21
  150.0 22.4 %collective-permute-start.7 = (s32[4,1,128]{2,1,0:T(1,128)S(1)}, s32[4,1,128]{2,1,0:T(1,128)S(1)}, u32[]{:S(2)}, u32[]{:S(2)}) collective-permute-start(s32[4,1,128]{2,1,0:T(1,128)S(1)} %get-tuple-element.272), channel_id=1, source_target_pairs={{1,0},{2,1},{3,2},{4,3},{5,4},{6,5},{7,6},{0,7},{9,8},{10,9},{11,1... | collective-permute-start | bytes 6152 | tf_op jit(solution)/shard_map/ppermute | solution.py:23
  182.2 3.2 collective-permute-start.2
  184.0 3.5 collective-permute-start.3
  273.6 11.4 %copy-start.20 = (f32[3,3,3,128]{3,2,1,0:T(4,128)S(1)}, f32[3,3,3,128]{3,2,1,0:T(4,128)}, u32[]{:S(2)}) copy-start(f32[3,3,3,128]{3,2,1,0:T(4,128)} %get-tuple-element.156) | copy-start | bytes 41476
  273.6 11.5 %copy-start.31 = (f32[3]{0:T(128)S(1)}, f32[3]{0:T(128)}, u32[]{:S(2)}) copy-start(f32[3]{0:T(128)} %get-tuple-element.388) | copy-start | bytes 40
  273.6 11.5 %copy-start.32 = (f32[3]{0:T(128)S(1)}, f32[3]{0:T(128)}, u32[]{:S(2)}) copy-start(f32[3]{0:T(128)} %get-tuple-element.389) | copy-start | bytes 40
  273.6 11.5 %copy-start.33 = (f32[3]{0:T(128)S(1)}, f32[3]{0:T(128)}, u32[]{:S(2)}) copy-start(f32[3]{0:T(128)} %get-tuple-element.390) | copy-start | bytes 40
  273.6 11.5 %copy-start.34 = (f32[3]{0:T(128)S(1)}, f32[3]{0:T(128)}, u32[]{:S(2)}) copy-start(f32[3]{0:T(128)} %get-tuple-element.391) | copy-start | bytes 40
  273.6 11.5 %copy-start.35 = (f32[3]{0:T(128)S(1)}, f32[3]{0:T(128)}, u32[]{:S(2)}) copy-start(f32[3]{0:T(128)} %get-tuple-element.386) | copy-start | bytes 40
  273.6 11.5 %copy-start.36 = (f32[3]{0:T(128)S(1)}, f32[3]{0:T(128)}, u32[]{:S(2)}) copy-start(f32[3]{0:T(128)} %get-tuple-element.387) | copy-start | bytes 40
  273.6 11.5 %copy-start.37 = (f32[3]{0:T(128)S(1)}, f32[3]{0:T(128)}, u32[]{:S(2)}) copy-start(f32[3]{0:T(128)} %get-tuple-element.384) | copy-start | bytes 40
  273.7 11.5 %copy-start.38 = (f32[3]{0:T(128)S(1)}, f32[3]{0:T(128)}, u32[]{:S(2)}) copy-start(f32[3]{0:T(128)} %get-tuple-element.385) | copy-start | bytes 40
  273.7 11.9 %copy-start.18 = (f32[6,128,128]{2,1,0:T(8,128)S(1)}, f32[6,128,128]{2,1,0:T(8,128)}, u32[]{:S(2)}) copy-start(f32[6,128,128]{2,1,0:T(8,128)} %get-tuple-element.423) | copy-start | bytes 1179652
  282.6 3.2 copy-start.17
  282.6 3.6 copy-start.16
  282.7 3.9 copy-start.15
  285.1 1.7 copy-start.14
  285.7 1.5 copy-start.13
  286.0 1.4 copy-start.12
  286.4 1.4 copy-start.11
  321.1 13.0 %copy-start.19 = (f32[3,3,3,128]{3,2,1,0:T(4,128)S(1)}, f32[3,3,3,128]{3,2,1,0:T(4,128)}, u32[]{:S(2)}) copy-start(f32[3,3,3,128]{3,2,1,0:T(4,128)} %get-tuple-element.157) | copy-start | bytes 41476
  321.1 13.0 %copy-start.23 = (f32[3]{0:T(128)S(1)}, f32[3]{0:T(128)}, u32[]{:S(2)}) copy-start(f32[3]{0:T(128)} %get-tuple-element.378) | copy-start | bytes 40
  321.2 13.0 %copy-start.24 = (f32[3]{0:T(128)S(1)}, f32[3]{0:T(128)}, u32[]{:S(2)}) copy-start(f32[3]{0:T(128)} %get-tuple-element.379) | copy-start | bytes 40
  321.2 13.0 %copy-start.25 = (f32[3]{0:T(128)S(1)}, f32[3]{0:T(128)}, u32[]{:S(2)}) copy-start(f32[3]{0:T(128)} %get-tuple-element.380) | copy-start | bytes 40
  321.2 13.0 %copy-start.26 = (f32[3]{0:T(128)S(1)}, f32[3]{0:T(128)}, u32[]{:S(2)}) copy-start(f32[3]{0:T(128)} %get-tuple-element.381) | copy-start | bytes 40
  321.2 13.0 %copy-start.27 = (f32[3]{0:T(128)S(1)}, f32[3]{0:T(128)}, u32[]{:S(2)}) copy-start(f32[3]{0:T(128)} %get-tuple-element.382) | copy-start | bytes 40
  321.2 13.0 %copy-start.28 = (f32[3]{0:T(128)S(1)}, f32[3]{0:T(128)}, u32[]{:S(2)}) copy-start(f32[3]{0:T(128)} %get-tuple-element.383) | copy-start | bytes 40
  321.2 13.0 %copy-start.29 = (f32[3]{0:T(128)S(1)}, f32[3]{0:T(128)}, u32[]{:S(2)}) copy-start(f32[3]{0:T(128)} %get-tuple-element.376) | copy-start | bytes 40
  321.2 13.0 %copy-start.30 = (f32[3]{0:T(128)S(1)}, f32[3]{0:T(128)}, u32[]{:S(2)}) copy-start(f32[3]{0:T(128)} %get-tuple-element.377) | copy-start | bytes 40
  321.2 13.4 %copy-start.10 = (f32[6,128,128]{2,1,0:T(8,128)S(1)}, f32[6,128,128]{2,1,0:T(8,128)}, u32[]{:S(2)}) copy-start(f32[6,128,128]{2,1,0:T(8,128)} %get-tuple-element.412) | copy-start | bytes 1179652
  330.9 4.1 copy-start.9
  330.9 4.4 copy-start.8
  330.9 4.8 copy-start.7
  334.3 1.7 copy-start.4
  334.8 1.5 copy-start.3
  335.2 1.5 copy-start.6
  335.5 1.4 copy-start.5
  370.3 15.0 %copy-start.2 = (bf16[384,1536]{1,0:T(8,128)(2,1)S(1)}, bf16[384,1536]{1,0:T(8,128)(2,1)}, u32[]{:S(2)}) copy-start(bf16[384,1536]{1,0:T(8,128)(2,1)} %reshape.4057) | copy-start | bytes 3538948
  379.9 5.4 copy-start.1
  385.4 2.2 copy-start
  398.0 0.7 copy-start.22
  398.0 113.6 %reduce-scatter.7.cloned.1.call-start = ((), (), s32[]{:S(2)}) async-start(), calls=%async_computation.4 | async-start | bytes 884736
  404.4 166.1 %all-reduce.2.cloned.1.call-start = ((), (), s32[]{:S(2)}) async-start(), calls=%async_computation.3 | async-start | bytes 2359296 | tf_op jit(solution)/shard_map/psum | solution.py:114
Sparse Core Ops, SparseCore 0:
  398.1 75.0 reduce-scatter.4
  476.9 34.6 reduce-scatter.6
  514.0 56.4 all-reduce.1
where the time goes:
time: 588 us; the launch traced here: 580 us
  matrix products  183 us (31%)
  waiting for transfers between devices  157 us (27%)
  between operations  156 us (27%)
  local copies, waits for them, and re-layouts  34.2 us (6%)
  other arithmetic  26.8 us (5%)
  starting transfers between devices  12.7 us (2%)
  blocking collectives  10.3 us (2%)
    dot_general x32, matrix products, frame_terms(): jnp.einsum('cij,ijk->ick', weight, basis, preferred_element_type=jnp.floa...  170 us
    reduce_scatter x1, waiting for transfers between devices, shards(): lax.psum_scatter(gram, 'gy', scatter_dimension=1, tiled=True)  68.7 us
    psum x1, waiting for transfers between devices, shards(): gram_rows, rhs_rows = lax.psum((gram_part, rhs_part), 'gx')  47.6 us
    unnamed x4, waiting for transfers between devices  38.5 us
    reshape x4, local copies, waits for them, and re-layouts, frame_terms(): stacked.append(design.astype(jnp.bfloat16).reshape(beads * 3, width))  13.3 us
  transfers between devices with their start and end apart: 11, of which 4 were waited for; matrix products, arithmetic and copies ran while one was open for 5% of the time, Pallas kernels for 0%

commit v1 on v0

v1 whole, which is shorter than its diff:
```python
import functools
import math
import jax
import jax.numpy as jnp
from jax import lax
from jax.experimental import pallas as pl
from jax.experimental.pallas import tpu as pltpu
from jax.sharding import PartitionSpec as P

K=256; PAIRS=6
STEP=32; SPAN=64
ROOT=math.sqrt(0.5*math.log2(math.e))
NEG=-1e9

def design_kernel(off_ref, mask_ref, rows_ref, kind_ref, col_ref, out_ref, pos_s, lt_s, code_s, w_s, res_s, list_s, *, by_blocks, beads, slots, unroll):
    b = pl.program_id(0)
    bx = b // by_blocks
    by = b % by_blocks
    live = jnp.int32(0)
    for t in range(slots):
        list_s[live] = off_ref[b, t]
        live = live + mask_ref[b, t]
    chunks = (live + 1) // 2
    colv = [jnp.broadcast_to(col_ref[0, :, a:a+1], (beads, beads)) for a in range(3)]
    def geom(s, c):
        o = list_s[s]
        ox = o // 3
        oy = o % 3
        src = (bx + ox) * (by_blocks + 2) + by + oy
        sx = (ox - 1).astype(jnp.float32)
        sy = (oy - 1).astype(jnp.float32)
        d0 = colv[0] - rows_ref[src, 0:1, :] - sx
        d1 = colv[1] - rows_ref[src, 1:2, :] - sy
        d2 = colv[2] - rows_ref[src, 2:3, :]
        r2 = d0 * d0 + d1 * d1 + d2 * d2
        u = jnp.sqrt(r2) * K
        m = jnp.minimum(jnp.floor(u * (1.0 / STEP)), K // STEP - 1.0)
        pos_s[s] = (u - m * STEP) * ROOT
        t = jnp.maximum(1.0 - r2, 0.0)
        lt_s[s] = jnp.where(t > 0.0, 2.0 * jnp.log2(jnp.where(t > 0.0, t, 1.0)), NEG)
        code_s[s] = kind_ref[src, 0:1, :] * 8.0 + m
        sc = 1.0 / jnp.sqrt(r2 + 0.05)
        w_s[0, s] = d0 * sc
        w_s[1, s] = d1 * sc
        w_s[2, s] = d2 * sc
        return c
    lax.fori_loop(0, live, geom, 0)
    @pl.when(live % 2 == 1)
    def _():
        z = jnp.zeros((beads, beads), jnp.float32)
        pos_s[live] = z
        lt_s[live] = z + NEG
        code_s[live] = z
        for a in range(3):
            w_s[a, live] = z

    cen = (lax.broadcasted_iota(jnp.int32, (SPAN, beads), 0).astype(jnp.float32) - 15.5) * ROOT
    row24 = lax.broadcasted_iota(jnp.int32, (24, beads), 0).astype(jnp.float32)

    def one(i, n):
        gs = []
        ws = []
        for s in range(n):
            x = pos_s[s, pl.ds(i, 1), :] - cen
            g = jnp.exp2(lt_s[s, pl.ds(i, 1), :] - x * x).astype(jnp.bfloat16)
            gs.append(g)
            hit = code_s[s, pl.ds(i, 1), :] == row24
            w = [jnp.where(hit, w_s[a, s, pl.ds(i, 1), :], 0.0) for a in range(3)]
            ws.append(jnp.concatenate(w, axis=0).astype(jnp.bfloat16))
        g = jnp.concatenate(gs, axis=1)
        w = jnp.concatenate(ws, axis=1)
        r = lax.dot_general(w, g, (((1,), (1,)), ((), ())), preferred_element_type=jnp.float32)
        res_s[pl.ds(pl.multiple_of(i * 72, 8), 72), 0:SPAN] = r

    for c in range(1, slots // 2 + 1):
        @pl.when(chunks == c)
        def _(c=c):
            def body(i, carry):
                for q in range(unroll):
                    one(i * unroll + q, 2 * c)
                return carry
            lax.fori_loop(0, beads // unroll, body, 0)
    @pl.when(chunks == 0)
    def _():
        res_s[...] = jnp.zeros_like(res_s)

    lane = lax.broadcasted_iota(jnp.int32, (8, 128), 1)
    low64 = lane < 64
    def unfold(g, carry):
        i0 = g * 16
        kt16 = jnp.broadcast_to(col_ref[0, pl.ds(pl.multiple_of(i0, 16), 16), 3:4], (16, 128))
        for a in range(3):
            d = []
            for t in range(3):
                halves = []
                for h in range(2):
                    rr = [res_s[pl.ds((i0 + h * 8) * 72 + a * 24 + t * 8 + m, 8, stride=72), :] for m in range(8)]
                    pair = lambda p, q: jnp.where(low64, p, pltpu.roll(q, 64, 1))
                    e0, e1 = pair(rr[0], rr[2]), pair(rr[4], rr[6])
                    o0, o1 = pair(rr[1], rr[3]), pair(rr[5], rr[7])
                    e0, e1 = pltpu.roll(e0, 112, 1), pltpu.roll(e1, 112, 1)
                    o0, o1 = pltpu.roll(o0, 16, 1), pltpu.roll(o1, 16, 1)
                    lo = jnp.where(lane < 112, e0, e1) + jnp.where(lane < 16, 0.0, o0)
                    hi = jnp.where(lane < 112, e1, 0.0) + jnp.where(lane < 16, o0, o1)
                    halves.append((lo, hi))
                d.append([jnp.concatenate([halves[0][v], halves[1][v]], axis=0) for v in range(2)])
            is_t = [kt16 == float(t) for t in range(3)]
            for p, (lo_t, hi_t) in enumerate([(0, 0), (0, 1), (0, 2), (1, 1), (1, 2), (2, 2)]):
                for v in range(2):
                    x = jnp.where(is_t[lo_t], d[hi_t][v], 0.0)
                    if lo_t != hi_t:
                        x = jnp.where(is_t[hi_t], d[lo_t][v], x)
                    out_ref[0, a, pl.ds(pl.multiple_of(i0, 16), 16), p * K + v * 128:p * K + (v + 1) * 128] = x.astype(jnp.bfloat16)
        return carry
    lax.fori_loop(0, beads // 16, unfold, 0)

def design(off, mask, rows, kind, cols, by_blocks, unroll=16):
    nb, slots = off.shape
    beads = rows.shape[-1]
    n_src = rows.shape[0]
    return pl.pallas_call(
        functools.partial(design_kernel, by_blocks=by_blocks, beads=beads, slots=slots, unroll=unroll),
        grid_spec=pltpu.PrefetchScalarGridSpec(
            num_scalar_prefetch=2, grid=(nb,),
            in_specs=[
                pl.BlockSpec((n_src, 3, beads), lambda b, *_: (0, 0, 0)),
                pl.BlockSpec((n_src, 1, beads), lambda b, *_: (0, 0, 0)),
                pl.BlockSpec((1, beads, 4), lambda b, *_: (b, 0, 0)),
            ],
            out_specs=pl.BlockSpec((1, 3, beads, PAIRS * K), lambda b, *_: (b, 0, 0, 0)),
            scratch_shapes=[
                pltpu.VMEM((slots, beads, beads), jnp.float32),
                pltpu.VMEM((slots, beads, beads), jnp.float32),
                pltpu.VMEM((slots, beads, beads), jnp.float32),
                pltpu.VMEM((3, slots, beads, beads), jnp.float32),
                pltpu.VMEM((beads * 72, 128), jnp.float32),
                pltpu.SMEM((slots + 1,), jnp.int32),
            ]),
        out_shape=jax.ShapeDtypeStruct((nb, 3, beads, PAIRS * K), jnp.bfloat16),
        compiler_params=pltpu.CompilerParams(vmem_limit_bytes=56 * 1024 * 1024),
    )(off, mask, rows, kind, cols)


def extended(cells, sides, width):
    for axis, dim in sides:
        count = lax.axis_size(axis)
        head = lax.slice_in_dim(cells, 0, width, axis=dim)
        tail = lax.slice_in_dim(cells, cells.shape[dim] - width, cells.shape[dim], axis=dim)
        cells = jnp.concatenate(
            [
                lax.ppermute(tail, axis, [(i, (i + 1) % count) for i in range(count)]),
                cells,
                lax.ppermute(head, axis, [((i + 1) % count, i) for i in range(count)]),
            ],
            axis=dim,
        )
    return cells


def shards(coords, kinds, forces, tile_offsets, tile_mask):
    frames, _, blocks_x, blocks_y, beads = coords.shape
    slots = tile_offsets.shape[3]
    nb = blocks_x * blocks_y
    frame_rows = 3 * beads * nb * lax.axis_size("gx") * lax.axis_size("gy")
    cells = jnp.concatenate(
        [jnp.transpose(coords[0], (1, 2, 0, 3)), kinds.astype(jnp.float32)[:, :, None, :]], axis=2
    )
    around = extended(cells, (("gx", 0), ("gy", 1)), 1)
    around = around.reshape((blocks_x + 2) * (blocks_y + 2), 4, beads)
    cols = jnp.swapaxes(cells.reshape(nb, 4, beads), 1, 2)
    rows = design(
        tile_offsets.reshape(nb, slots),
        tile_mask.reshape(nb, slots),
        around[:, :3],
        around[:, 3:],
        cols,
        blocks_y,
    ).reshape(nb * 3 * beads, PAIRS * K)
    target = jnp.transpose(forces[0], (1, 2, 0, 3)).reshape(nb * 3 * beads)
    gram = lax.dot_general(rows, rows, (((0,), (0,)), ((), ())), preferred_element_type=jnp.float32)
    rhs = jnp.dot(target, rows, preferred_element_type=jnp.float32)
    gram = lax.psum_scatter(gram / frame_rows, "gy", scatter_dimension=0, tiled=True)
    rhs = lax.psum_scatter(rhs / frame_rows, "gy", scatter_dimension=0, tiled=True)
    gram, rhs = lax.psum((gram, rhs), "gx")
    return gram[None], rhs[None]


def solution(mesh):
    placed = (
        P(None, None, "gx", "gy", None),
        P("gx", "gy", None),
        P(None, None, "gx", "gy", None),
        P(None, "gx", "gy", None),
        P(None, "gx", "gy", None),
    )
    return jax.shard_map(
        shards,
        mesh=mesh,
        in_specs=placed,
        out_specs=(P(None, "gy", None), P(None, "gy")),
        check_vma=False,
    )
```

time: 588 us -> 225 us (0.38); the launches traced: 580 us -> 226 us
  matrix products: 183 us -> 16.4 us
  between operations: 156 us -> 14.8 us
  waiting for transfers between devices: 157 us -> 114 us
  Pallas kernels: 0 us -> 41.7 us
  local copies, waits for them, and re-layouts: 34.2 us -> 4.67 us
  other arithmetic: 26.8 us -> 3.66 us
  blocking collectives: 10.3 us -> 23.4 us
    dot_general x34 -> x2, matrix products: 183 us -> 16.4 us  [the longest x1 13.3 us: shards(): lax.dot_general(rows, rows, (((0,), (0,)), ((), ())), preferred_element_t...]
    pallas_call x0 -> x1, Pallas kernels: none -> 41.7 us  [design(): pl.pallas_call(functools.partial(design_kernel, by_blocks=by_blocks, bead...]
    unnamed x4 -> x2, waiting for transfers between devices: 38.5 us -> 0.03 us
    convert_element_type x64 -> x1, other arithmetic: 18.5 us -> 0.69 us  [shards(): kinds.astype(jnp.float32)[:, :, None, :]]
    psum x1, waiting for transfers between devices: 47.6 us -> 30.9 us  [shards(): gram, rhs = lax.psum((gram, rhs), 'gx')]
    reshape x12 -> x1, local copies, waits for them, and re-layouts: 14.2 us -> 0.02 us  [shards(): target = jnp.transpose(forces[0], (1, 2, 0, 3)).reshape(nb * 3 * beads)]
    unnamed x0 -> x1, blocking collectives: none -> 12.4 us
    reduce_scatter x1, waiting for transfers between devices: 68.7 us -> 80.7 us  [shards(): lax.psum_scatter(gram / frame_rows, 'gy', scatter_dimension=0, tiled=True)]
  transfers between devices with their start and end apart: 11 -> 6, of which waited for: 4 -> 3; matrix products, arithmetic and copies ran while one was open for 5% -> 2% of each run, Pallas kernels for 0% -> 0%
where the time goes in v1:
time: 225 us; the launch traced here: 226 us
  waiting for transfers between devices  114 us (51%)
  Pallas kernels  41.7 us (19%)
  blocking collectives  23.4 us (10%)
  matrix products  16.4 us (7%)
  between operations  14.8 us (7%)
  starting transfers between devices  7.12 us (3%)
  local copies, waits for them, and re-layouts  4.67 us (2%)
  other arithmetic  3.66 us (2%)
    reduce_scatter x1, waiting for transfers between devices, shards(): lax.psum_scatter(gram / frame_rows, 'gy', scatter_dimension=0, tiled=True)  80.7 us
    pallas_call x1, Pallas kernels, design(): pl.pallas_call(functools.partial(design_kernel, by_blocks=by_blocks, bead...  41.7 us
    psum x1, waiting for transfers between devices, shards(): gram, rhs = lax.psum((gram, rhs), 'gx')  30.9 us
    dot_general x1, matrix products, shards(): lax.dot_general(rows, rows, (((0,), (0,)), ((), ())), preferred_element_t...  13.3 us
    unnamed x1, blocking collectives  12.4 us
    psum x1, blocking collectives, shards(): gram, rhs = lax.psum((gram, rhs), 'gx')  11 us
    ppermute x2, starting transfers between devices, extended(): lax.ppermute(tail, axis, [(i, (i + 1) % count) for i in range(count)])  4.96 us
  transfers between devices with their start and end apart: 6, of which 3 were waited for; matrix products, arithmetic and copies ran while one was open for 2% of the time, Pallas kernels for 0%

profile of v1, /device:TPU:1, one launch (start us, length us, event | category | flops | bytes accessed | tf_op | source)
XLA Modules:
  0.0 225.5 jit_solution(17220867042856102636)
XLA Ops:
  7.2 0.0 reduce-scatter.2.cloned.1.call-start
  7.2 0.7 fusion.2
  7.9 0.7 fusion
  8.6 2.1 collective-permute-start
  10.7 2.1 collective-permute-start.1
  12.8 0.8 copy.22
  13.6 0.1 copy.23
  13.8 0.0 collective-permute-done
  13.8 0.0 collective-permute-done.1
  13.8 0.7 pad_maximum_fusion.1
  14.5 2.8 %collective-permute-start.2 = (f32[4,1,4,128]{3,1,0,2:T(1,128)S(1)}, f32[4,1,4,128]{3,1,0,2:T(1,128)S(1)}, u32[]{:S(2)}, u32[]{:S(2)}) collective-permute-start(f32[4,1,4,128]{3,1,0,2:T(1,128)S(1)} %get-tuple-element.2), channel_id=1, source_target_pairs={{0,1},{1,2},{2,3},{3,4},{4,5},{5,6},{6,7},{7,0},{8,9},{9,10},{10,1... | collective-permute-start | bytes 24584 | tf_op jit(solution)/shard_map/ppermute | solution.py:151
  17.4 0.0 collective-permute-start.3
  17.4 0.8 maximum_bitcast_fusion.col_ref
  18.2 0.0 collective-permute-done.2
  18.2 2.2 collective-permute-done.3
  20.5 0.7 pad_maximum_fusion
  21.2 0.0 copy-start
  21.2 0.6 slice.29.kind_ref
  21.8 0.0 copy-done
  21.8 41.7 %shard_map.68 = bf16[4,3,128,1536]{3,2,1,0:T(8,128)(2,1)} custom-call(s32[4,8]{1,0:T(4,128)} %bitcast.40, s32[4,8]{1,0:T(4,128)} %bitcast.41, f32[16,3,128]{2,1,0:T(4,128)} %bitcast.32, f32[16,1,128]{2,1,0:T(1,128)} %slice.29.kind_ref, f32[4,128,4]{2,1,0:T(8,128)} %maximum_bitcast_fusion.col_ref), custom_call_target="tpu_custom_call" | custom-call | tf_op jit(solution)/shard_map/pallas_call | solution.py:121
  63.5 13.3 %bitcast_multiply_fusion = f32[1536,1536]{1,0:T(8,128)} fusion(bf16[4,3,128,1536]{3,2,1,0:T(8,128)(2,1)} %shard_map.68), kind=kOutput, calls=%fused_computation | convolution fusion | flops 7250116608 | bytes 14155776 | tf_op jit(solution)/shard_map/dot_general | solution.py:180
  76.8 0.0 copy-start.1
  76.8 0.0 copy-start.2
  76.8 0.0 reduce-scatter.2.cloned.1.call-update
  76.8 0.0 all-reduce.3.cloned.1.call-start
  76.9 80.7 %reduce-scatter.2.cloned.1.call-done = f32[192,1536]{1,0:T(8,128)} async-done(((f32[1536,1536]{1,0:T(8,128)}), f32[192,1536]{1,0:T(8,128)}) %reduce-scatter.2.cloned.1.call-update) | async-done | bytes 1179664 | tf_op jit(solution)/shard_map/reduce_scatter | solution.py:182
  157.6 0.0 all-reduce.3.cloned.1.call-update
  157.6 0.0 copy-done.1
  157.6 0.0 copy-done.2
  157.6 0.6 dynamic-slice
  158.9 3.1 %convolution_reduce_fusion = f32[1536]{0:T(1024)S(1)} fusion(bf16[1536,1536]{1,0:T(8,128)(2,1)} %bitcast.28, bf16[1536,1]{0,1:T(2,128)(2,1)S(1)} %reshape.29), kind=kOutput, calls=%fused_computation.1 | convolution fusion | flops 4718592 | bytes 4727808 | tf_op jit(solution)/shard_map/dot_general | solution.py:181
  162.0 12.4 %all-reduce = f32[1536]{0:T(1024)S(1)} all-reduce(f32[1536]{0:T(1024)S(1)} %broadcast_multiply_fusion), channel_id=3, replica_groups=mesh['gx'=4,'gy'=8] {'gy'}, use_global_device_ids=true, to_apply=%region_2.0.clone | all-reduce | flops 1536 | bytes 12288
  174.4 0.1 dynamic-slice.1
  174.5 11.0 %psum.15 = f32[1,192]{1,0:T(1,128)} all-reduce(f32[1,192]{1,0:T(1,128)S(1)} %bitcast.38), channel_id=1, replica_groups=mesh['gx'=4,'gy'=8] {'gx'}, use_global_device_ids=true, to_apply=%region_3.0 | all-reduce | flops 192 | bytes 1536 | tf_op jit(solution)/shard_map/psum | solution.py:184
  185.5 30.9 %all-reduce.3.cloned.1.call-done = f32[1,192,1536]{2,1,0:T(8,128)} async-done(((f32[1,192,1536]{2,1,0:T(8,128)}), f32[1,192,1536]{2,1,0:T(8,128)}) %all-reduce.3.cloned.1.call-update) | async-done | bytes 1179664 | tf_op jit(solution)/shard_map/psum | solution.py:184
  216.3 2.4 %copy.29 = f32[1,192,1536]{2,1,0:T(8,128)} copy(f32[1,192,1536]{2,1,0:T(8,128)} %all-reduce.3.cloned.1.call-done) | data formatting | bytes 2359296
  (5 shorter events, 0.1 us)
Async XLA Ops:
  7.2 150.4 %reduce-scatter.2.cloned.1.call-start = ((), (), s32[]{:S(2)}) async-start(), calls=%async_computation.1 | async-start | bytes 10616832 | tf_op jit(solution)/shard_map/reduce_scatter | solution.py:182
  8.6 5.2 %collective-permute-start = (f32[1,2,4,128]{3,1,0,2:T(2,128)S(1)}, f32[1,2,4,128]{3,1,0,2:T(2,128)S(1)}, u32[]{:S(2)}, u32[]{:S(2)}) collective-permute-start(f32[1,2,4,128]{3,1,0,2:T(2,128)S(1)} %get-tuple-element.4), channel_id=1, source_target_pairs={{0,8},{8,16},{16,24},{24,0},{1,9},{9,17},{17,25},{25,1},{2,10},{10... | collective-permute-start | bytes 12296 | tf_op jit(solution)/shard_map/ppermute | solution.py:151
  10.7 3.1 %collective-permute-start.1 = (f32[1,2,4,128]{3,1,0,2:T(2,128)S(1)}, f32[1,2,4,128]{3,1,0,2:T(2,128)S(1)}, u32[]{:S(2)}, u32[]{:S(2)}) collective-permute-start(f32[1,2,4,128]{3,1,0,2:T(2,128)S(1)} %get-tuple-element.5), channel_id=1, source_target_pairs={{8,0},{16,8},{24,16},{0,24},{9,1},{17,9},{25,17},{1,25},{10,2},{18... | collective-permute-start | bytes 12296 | tf_op jit(solution)/shard_map/ppermute | solution.py:153
  14.5 3.7 %collective-permute-start.2 = (f32[4,1,4,128]{3,1,0,2:T(1,128)S(1)}, f32[4,1,4,128]{3,1,0,2:T(1,128)S(1)}, u32[]{:S(2)}, u32[]{:S(2)}) collective-permute-start(f32[4,1,4,128]{3,1,0,2:T(1,128)S(1)} %get-tuple-element.2), channel_id=1, source_target_pairs={{0,1},{1,2},{2,3},{3,4},{4,5},{5,6},{6,7},{7,0},{8,9},{9,10},{10,1... | collective-permute-start | bytes 24584 | tf_op jit(solution)/shard_map/ppermute | solution.py:151
  17.4 3.1 %collective-permute-start.3 = (f32[4,1,4,128]{3,1,0,2:T(1,128)S(1)}, f32[4,1,4,128]{3,1,0,2:T(1,128)S(1)}, u32[]{:S(2)}, u32[]{:S(2)}) collective-permute-start(f32[4,1,4,128]{3,1,0,2:T(1,128)S(1)} %get-tuple-element.3), channel_id=1, source_target_pairs={{1,0},{2,1},{3,2},{4,3},{5,4},{6,5},{7,6},{0,7},{9,8},{10,9},{11,1... | collective-permute-start | bytes 24584 | tf_op jit(solution)/shard_map/ppermute | solution.py:153
  21.2 0.6 copy-start
  76.8 80.8 %copy-start.1 = (bf16[1,3,2,2,128]{4,3,2,1,0:T(2,128)(2,1)S(1)}, bf16[1,3,2,2,128]{4,3,2,1,0:T(2,128)(2,1)}, u32[]{:S(2)}) copy-start(bf16[1,3,2,2,128]{4,3,2,1,0:T(2,128)(2,1)} %param.7) | copy-start | bytes 9220
  76.8 80.8 %copy-start.2 = (u32[32]{0:T(128)S(1)}, u32[32]{0:T(128)}, u32[]{:S(2)}) copy-start(u32[32]{0:T(128)} %constant.12) | copy-start | bytes 388
  76.8 139.5 %all-reduce.3.cloned.1.call-start = ((), (), s32[]{:S(2)}) async-start(), calls=%async_computation.2 | async-start | bytes 2359296 | tf_op jit(solution)/shard_map/psum | solution.py:184
Sparse Core Ops, SparseCore 0:
  77.0 80.5 reduce-scatter.1
  159.9 56.3 all-reduce.2

commit v2 on v1

--- a/solution.py
+++ b/solution.py
@@ -2,6 +2,7 @@
 import math
 import jax
 import jax.numpy as jnp
+import numpy as np
 from jax import lax
 from jax.experimental import pallas as pl
 from jax.experimental.pallas import tpu as pltpu
@@ -12,7 +13,114 @@
 ROOT=math.sqrt(0.5*math.log2(math.e))
 NEG=-1e9
 
-def design_kernel(off_ref, mask_ref, rows_ref, kind_ref, col_ref, out_ref, pos_s, lt_s, code_s, w_s, res_s, list_s, *, by_blocks, beads, slots, unroll):
+CLASSES = ((0, 0), (0, 1), (0, 2), (1, 1), (1, 2), (2, 2))
+HALF = 128
+TILES = PAIRS * K // HALF
+CHUNKS = 2
+RHS = (-1, -1)
+
+
+def stored(r, c):
+    p, q = CLASSES[r * HALF // K], CLASSES[c * HALF // K]
+    return r <= c and bool(set(p) & set(q))
+
+
+class Plan:
+    def __init__(self, size_x, size_y):
+        self.size_x = size_x
+        self.pairs = size_y // 2
+        self.rows = PAIRS * K // size_y
+        self.part = HALF // 2 // size_x
+        pairs = range(self.pairs)
+        tiles = [(r, c) for r in range(TILES) for c in range(TILES) if stored(r, c)]
+        needs = {RHS: set(pairs)}
+        for r, c in tiles:
+            span = [(x * HALF, x * HALF + HALF) for x in (r, c)]
+            needs[(r, c)] = {
+                g for g in pairs for lo, hi in span
+                if lo < (g + 1) * 2 * self.rows and hi > g * 2 * self.rows
+            }
+        self.slots = -(-(len(tiles) + 1) // (self.pairs * CHUNKS))
+        room = self.slots * CHUNKS
+        owned = [[] for _ in pairs]
+        for tile in sorted(tiles, key=lambda t: len(needs[t])) + [RHS]:
+            free = [g for g in pairs if len(owned[g]) < room]
+            wanted = [g for g in free if g in needs[tile]] or free
+            owned[min(wanted, key=lambda g: len(owned[g]))].append(tile)
+        self.owned = owned
+        self.place = {t: (g, s) for g in pairs for s, t in enumerate(owned[g])}
+        lists = {
+            (g, k): [s for s, t in enumerate(owned[g]) if (g ^ k) in needs[t]]
+            for g in pairs for k in range(1, self.pairs)
+        }
+        self.counts = [max(1, max(len(lists[g, k]) for g in pairs)) for k in range(1, self.pairs)]
+        self.room = room
+        self.send = np.zeros((self.pairs, sum(self.counts)), np.int32)
+        self.entries = room + sum(self.counts)
+        found = []
+        for g in pairs:
+            where = {t: s for s, t in enumerate(owned[g])}
+            at = 0
+            for k in range(1, self.pairs):
+                chosen = lists[g, k]
+                self.send[g, at:at + len(chosen)] = chosen
+                for j, s in enumerate(lists[g ^ k, k]):
+                    where[owned[g ^ k][s]] = room + at + j
+                at += self.counts[k - 1]
+            found.append(where)
+        self.unit = math.gcd(self.rows, HALF)
+        units = self.rows // self.unit
+        self.table = np.zeros((size_y, units * TILES), np.int32)
+        self.rhs = np.zeros((size_y,), np.int32)
+        for d in range(size_y):
+            where = found[d // 2]
+            self.rhs[d] = where[RHS]
+            for u in range(units):
+                r = (d * self.rows + u * self.unit) // HALF
+                for c in range(TILES):
+                    if stored(r, c):
+                        self.table[d, u * TILES + c] = 2 * where[(r, c)]
+                    elif stored(c, r):
+                        self.table[d, u * TILES + c] = 2 * where[(c, r)] + 1
+                    else:
+                        self.table[d, u * TILES + c] = -1
+
+
+def gram_tiles(me_ref, force_ref, rows_s, left_s, outs, plan):
+    def put(tile, value):
+        g, s = plan.place[tile]
+        out = outs[s // plan.slots]
+        for h in range(2):
+            for z in range(plan.size_x):
+                at = h * HALF // 2 + z * plan.part
+                out[h ^ me_ref[0], g ^ me_ref[1], z ^ me_ref[2], s % plan.slots] = value[at:at + plan.part]
+
+    used = {(g, s) for g, s in plan.place.values()}
+    for g in range(plan.pairs):
+        for s in range(plan.room):
+            if (g, s) not in used:
+                plan_tile = jnp.zeros((plan.part, HALF), jnp.float32)
+                for h in range(2):
+                    for z in range(plan.size_x):
+                        outs[s // plan.slots][h ^ me_ref[0], g ^ me_ref[1], z ^ me_ref[2], s % plan.slots] = plan_tile
+    for p in range(PAIRS):
+        left_s[...] = rows_s[:, p * K:(p + 1) * K].T
+        for q in range(p, PAIRS):
+            if not stored(2 * p, 2 * q):
+                continue
+            block = jnp.dot(left_s[...], rows_s[:, q * K:(q + 1) * K], preferred_element_type=jnp.float32)
+            for r in range(2):
+                for c in range(2):
+                    if stored(2 * p + r, 2 * q + c):
+                        put((2 * p + r, 2 * q + c), block[r * HALF:(r + 1) * HALF, c * HALF:(c + 1) * HALF])
+    rhs = jnp.dot(force_ref[...], rows_s[...], preferred_element_type=jnp.float32)
+    lines = [rhs[0:1, t * HALF:(t + 1) * HALF] for t in range(TILES)]
+    put(RHS, jnp.concatenate(lines + [jnp.zeros((HALF - TILES, HALF), jnp.float32)], axis=0))
+
+
+def design_kernel(off_ref, mask_ref, me_ref, rows_ref, kind_ref, col_ref, force_ref, *refs, plan, by_blocks, beads, slots, unroll):
+    outs = refs[:CHUNKS]
+    pos_s, lt_s, code_s, w_s, res_s, rows_s, left_s, list_s = refs[CHUNKS:]
     b = pl.program_id(0)
     bx = b // by_blocks
     by = b % by_blocks
@@ -110,35 +218,128 @@
                     x = jnp.where(is_t[lo_t], d[hi_t][v], 0.0)
                     if lo_t != hi_t:
                         x = jnp.where(is_t[hi_t], d[lo_t][v], x)
-                    out_ref[0, a, pl.ds(pl.multiple_of(i0, 16), 16), p * K + v * 128:p * K + (v + 1) * 128] = x.astype(jnp.bfloat16)
+                    rows_s[pl.ds(pl.multiple_of((b * 3 + a) * beads + i0, 16), 16), p * K + v * 128:p * K + (v + 1) * 128] = x.astype(jnp.bfloat16)
         return carry
     lax.fori_loop(0, beads // 16, unfold, 0)
 
-def design(off, mask, rows, kind, cols, by_blocks, unroll=16):
+    @pl.when(b == pl.num_programs(0) - 1)
+    def _():
+        gram_tiles(me_ref, force_ref, rows_s, left_s, outs, plan)
+
+
+def design(off, mask, me, rows, kind, cols, force, plan, by_blocks, unroll=16):
     nb, slots = off.shape
     beads = rows.shape[-1]
     n_src = rows.shape[0]
+    total = nb * 3 * beads
+    share = (2, plan.pairs, plan.size_x, plan.slots, plan.part, HALF)
     return pl.pallas_call(
-        functools.partial(design_kernel, by_blocks=by_blocks, beads=beads, slots=slots, unroll=unroll),
+        functools.partial(design_kernel, plan=plan, by_blocks=by_blocks, beads=beads, slots=slots, unroll=unroll),
         grid_spec=pltpu.PrefetchScalarGridSpec(
-            num_scalar_prefetch=2, grid=(nb,),
+            num_scalar_prefetch=3,
+            grid=(nb,),
             in_specs=[
                 pl.BlockSpec((n_src, 3, beads), lambda b, *_: (0, 0, 0)),
                 pl.BlockSpec((n_src, 1, beads), lambda b, *_: (0, 0, 0)),
                 pl.BlockSpec((1, beads, 4), lambda b, *_: (b, 0, 0)),
+                pl.BlockSpec((16, total), lambda b, *_: (0, 0)),
             ],
-            out_specs=pl.BlockSpec((1, 3, beads, PAIRS * K), lambda b, *_: (b, 0, 0, 0)),
+            out_specs=[pl.BlockSpec(share, lambda b, *_: (0,) * 6)] * CHUNKS,
             scratch_shapes=[
                 pltpu.VMEM((slots, beads, beads), jnp.float32),
                 pltpu.VMEM((slots, beads, beads), jnp.float32),
                 pltpu.VMEM((slots, beads, beads), jnp.float32),
                 pltpu.VMEM((3, slots, beads, beads), jnp.float32),
                 pltpu.VMEM((beads * 72, 128), jnp.float32),
+                pltpu.VMEM((total, PAIRS * K), jnp.bfloat16),
+                pltpu.VMEM((K, total), jnp.bfloat16),
                 pltpu.SMEM((slots + 1,), jnp.int32),
-            ]),
-        out_shape=jax.ShapeDtypeStruct((nb, 3, beads, PAIRS * K), jnp.bfloat16),
+            ],
+        ),
+        out_shape=[jax.ShapeDtypeStruct(share, jnp.float32)] * CHUNKS,
         compiler_params=pltpu.CompilerParams(vmem_limit_bytes=56 * 1024 * 1024),
-    )(off, mask, rows, kind, cols)
+    )(off, mask, me, rows, kind, cols, force)
+
+
+def pack_kernel(me_ref, send_ref, parts_ref, own_ref, *msg_refs, plan, scale):
+    def fetch(ref, j, s):
+        for z in range(plan.size_x):
+            value = parts_ref[s // plan.slots, z ^ me_ref[2], s % plan.slots]
+            ref[j, z * plan.part:(z + 1) * plan.part, :] = value * scale
+
+    for s in range(plan.room):
+        fetch(own_ref, s, s)
+    at = 0
+    for ref, count in zip(msg_refs, plan.counts):
+        for j in range(count):
+            fetch(ref, j, send_ref[me_ref[1], at + j])
+        at += count
+
+
+def pack(me, parts, plan, scale):
+    shapes = [(n, HALF // 2, HALF) for n in [plan.room] + plan.counts]
+    return pl.pallas_call(
+        functools.partial(pack_kernel, plan=plan, scale=scale),
+        grid_spec=pltpu.PrefetchScalarGridSpec(
+            num_scalar_prefetch=2,
+            grid=(1,),
+            in_specs=[pl.BlockSpec(parts.shape, lambda b, *_: (0,) * parts.ndim)],
+            out_specs=[pl.BlockSpec(s, lambda b, *_: (0, 0, 0)) for s in shapes],
+        ),
+        out_shape=[jax.ShapeDtypeStruct(s, jnp.float32) for s in shapes],
+        compiler_params=pltpu.CompilerParams(vmem_limit_bytes=32 * 1024 * 1024),
+    )(me, jnp.asarray(plan.send), parts)
+
+
+def place_kernel(me_ref, table_ref, rhs_at_ref, mine_ref, other_ref, gram_ref, rhs_ref, full_s, *, plan):
+    half = HALF // 2
+    core = me_ref[0]
+    dev = me_ref[3]
+    full_s[:, pl.ds(pl.multiple_of(core * half, half), half), :] = mine_ref[...]
+    full_s[:, pl.ds(pl.multiple_of((1 - core) * half, half), half), :] = other_ref[...]
+    for u in range(plan.rows // plan.unit):
+        at = (dev * plan.rows + u * plan.unit) % HALF
+        for c in range(TILES):
+            entry = table_ref[dev, u * TILES + c]
+            cut = (slice(u * plan.unit, (u + 1) * plan.unit), slice(c * HALF, (c + 1) * HALF))
+
+            @pl.when(entry < 0)
+            def _(cut=cut):
+                gram_ref[cut] = jnp.zeros((plan.unit, HALF), jnp.float32)
+
+            @pl.when(jnp.logical_and(entry >= 0, entry % 2 == 0))
+            def _(cut=cut, entry=entry, at=at):
+                gram_ref[cut] = full_s[entry // 2, pl.ds(pl.multiple_of(at, plan.unit), plan.unit), :]
+
+            @pl.when(jnp.logical_and(entry >= 0, entry % 2 == 1))
+            def _(cut=cut, entry=entry, at=at):
+                turned = full_s[entry // 2].T
+                value = turned[0:plan.unit]
+                for v in range(1, HALF // plan.unit):
+                    value = jnp.where(at == v * plan.unit, turned[v * plan.unit:(v + 1) * plan.unit], value)
+                gram_ref[cut] = value
+    rhs_ref[...] = full_s[rhs_at_ref[dev], 0:16, :]
+
+
+def place(me, mine, other, plan):
+    return pl.pallas_call(
+        functools.partial(place_kernel, plan=plan),
+        grid_spec=pltpu.PrefetchScalarGridSpec(
+            num_scalar_prefetch=3,
+            grid=(1,),
+            in_specs=[pl.BlockSpec(mine.shape, lambda b, *_: (0, 0, 0))] * 2,
+            out_specs=[
+                pl.BlockSpec((plan.rows, PAIRS * K), lambda b, *_: (0, 0)),
+                pl.BlockSpec((16, HALF), lambda b, *_: (0, 0)),
+            ],
+            scratch_shapes=[pltpu.VMEM((plan.entries, HALF, HALF), jnp.float32)],
+        ),
+        out_shape=[
+            jax.ShapeDtypeStruct((plan.rows, PAIRS * K), jnp.float32),
+            jax.ShapeDtypeStruct((16, HALF), jnp.float32),
+        ],
+        compiler_params=pltpu.CompilerParams(vmem_limit_bytes=32 * 1024 * 1024),
+    )(me, jnp.asarray(plan.table), jnp.asarray(plan.rhs), mine, other)
 
 
 def extended(cells, sides, width):
@@ -157,31 +358,52 @@
     return cells
 
 
+def swap(x, axis, flip):
+    return lax.ppermute(x, axis, [(i, i ^ flip) for i in range(lax.axis_size(axis))])
+
+
+def summed(x, plan):
+    x = x[0] + swap(x[1], "gy", 1)
+    got = [swap(x[k], "gy", 2 * k) for k in range(1, plan.pairs)]
+    x = functools.reduce(jnp.add, got, x[0])
+    got = [swap(x[k], "gx", k) for k in range(1, plan.size_x)]
+    x = functools.reduce(jnp.add, got, x[0])
+    return jnp.stack([x] + [swap(x, "gx", k) for k in range(1, plan.size_x)])
+
+
 def shards(coords, kinds, forces, tile_offsets, tile_mask):
     frames, _, blocks_x, blocks_y, beads = coords.shape
     slots = tile_offsets.shape[3]
     nb = blocks_x * blocks_y
-    frame_rows = 3 * beads * nb * lax.axis_size("gx") * lax.axis_size("gy")
+    size_x, size_y = lax.axis_size("gx"), lax.axis_size("gy")
+    frame_rows = 3 * beads * nb * size_x * size_y
+    plan = Plan(size_x, size_y)
+    dev = lax.axis_index("gy")
+    me = jnp.stack([dev % 2, dev // 2, lax.axis_index("gx"), dev]).astype(jnp.int32)
     cells = jnp.concatenate(
         [jnp.transpose(coords[0], (1, 2, 0, 3)), kinds.astype(jnp.float32)[:, :, None, :]], axis=2
     )
     around = extended(cells, (("gx", 0), ("gy", 1)), 1)
     around = around.reshape((blocks_x + 2) * (blocks_y + 2), 4, beads)
     cols = jnp.swapaxes(cells.reshape(nb, 4, beads), 1, 2)
-    rows = design(
+    force = jnp.transpose(forces[0], (1, 2, 0, 3)).reshape(1, nb * 3 * beads)
+    chunks = design(
         tile_offsets.reshape(nb, slots),
         tile_mask.reshape(nb, slots),
+        me,
         around[:, :3],
         around[:, 3:],
         cols,
+        jnp.broadcast_to(force, (16, nb * 3 * beads)),
+        plan,
         blocks_y,
-    ).reshape(nb * 3 * beads, PAIRS * K)
-    target = jnp.transpose(forces[0], (1, 2, 0, 3)).reshape(nb * 3 * beads)
-    gram = lax.dot_general(rows, rows, (((0,), (0,)), ((), ())), preferred_element_type=jnp.float32)
-    rhs = jnp.dot(target, rows, preferred_element_type=jnp.float32)
-    gram = lax.psum_scatter(gram / frame_rows, "gy", scatter_dimension=0, tiled=True)
-    rhs = lax.psum_scatter(rhs / frame_rows, "gy", scatter_dimension=0, tiled=True)
-    gram, rhs = lax.psum((gram, rhs), "gx")
+    )
+    parts = jnp.stack([summed(x, plan) for x in chunks])
+    own, *messages = pack(me, parts, plan, 1.0 / frame_rows)
+    got = [swap(m, "gy", 2 * k) for k, m in enumerate(messages, 1)]
+    mine = jnp.concatenate([own] + got)
+    gram, lines = place(me, mine, swap(mine, "gy", 1), plan)
+    rhs = lax.dynamic_slice(lines.reshape(16 * HALF), (dev * plan.rows,), (plan.rows,))
     return gram[None], rhs[None]
 
 

time: 225 us -> 126 us (0.56)
  waiting for transfers between devices: 114 us -> 30.6 us
  starting transfers between devices: 7.12 us -> 38.4 us
  blocking collectives: 23.4 us -> 0 us
  matrix products: 16.4 us -> 0 us
  between operations: 14.8 us -> 0.87 us
  Pallas kernels: 41.7 us -> 46.8 us
    reduce_scatter x1 -> x0, waiting for transfers between devices: 80.7 us -> none  [shards(): lax.psum_scatter(gram / frame_rows, 'gy', scatter_dimension=0, tiled=True)]
    ppermute x0 -> x24, starting transfers between devices: none -> 31.9 us  [swap(): lax.ppermute(x, axis, [(i, i ^ flip) for i in range(lax.axis_size(axis))])]
    psum x1 -> x0, waiting for transfers between devices: 30.9 us -> none  [shards(): gram, rhs = lax.psum((gram, rhs), 'gx')]
    ppermute x0 -> x24, waiting for transfers between devices: none -> 28.9 us  [swap(): lax.ppermute(x, axis, [(i, i ^ flip) for i in range(lax.axis_size(axis))])]
    dot_general x2 -> x0, matrix products: 16.4 us -> none  [the longest x1 13.3 us: shards(): lax.dot_general(rows, rows, (((0,), (0,)), ((), ())), preferred_element_t...]
    unnamed x1 -> x0, blocking collectives: 12.4 us -> none
    psum x1 -> x0, blocking collectives: 11 us -> none  [shards(): gram, rhs = lax.psum((gram, rhs), 'gx')]
    pallas_call x1 -> x3, Pallas kernels: 41.7 us -> 46.8 us  [the longest x1 42.9 us: design(): pl.pallas_call(functools.partial(design_kernel, plan=plan, by_blocks=by_b...]
  transfers between devices with their start and end apart: 6 -> 28, of which waited for: 3 -> 13; matrix products, arithmetic and copies ran while one was open for 2% -> 3% of each run, Pallas kernels for 0% -> 0%
where the time goes in v2:
time: 126 us; the launch traced here: 127 us
  Pallas kernels  46.8 us (37%)
  starting transfers between devices  38.4 us (30%)
  waiting for transfers between devices  30.6 us (24%)
  local copies, waits for them, and re-layouts  5.26 us (4%)
  other arithmetic  4.74 us (4%)
    pallas_call x1, Pallas kernels, design(): pl.pallas_call(functools.partial(design_kernel, plan=plan, by_blocks=by_b...  42.9 us
    ppermute x24, starting transfers between devices, swap(): lax.ppermute(x, axis, [(i, i ^ flip) for i in range(lax.axis_size(axis))])  31.9 us
    ppermute x24, waiting for transfers between devices, swap(): lax.ppermute(x, axis, [(i, i ^ flip) for i in range(lax.axis_size(axis))])  28.9 us
    ppermute x2, starting transfers between devices, extended(): lax.ppermute(tail, axis, [(i, (i + 1) % count) for i in range(count)])  4.39 us
    pallas_call x1, Pallas kernels, place(): pl.pallas_call(functools.partial(place_kernel, plan=plan), grid_spec=pltp...  3.17 us
  transfers between devices with their start and end apart: 28, of which 13 were waited for; matrix products, arithmetic and copies ran while one was open for 3% of the time, Pallas kernels for 0%

profile of v2, /device:TPU:1, one launch (start us, length us, event | category | flops | bytes accessed | tf_op | source)
XLA Modules:
  0.0 126.7 jit_solution(3465083917144743624)
XLA Ops:
  0.6 0.7 fusion.14
  1.3 0.7 fusion.12
  2.0 2.1 %collective-permute-start = (f32[1,2,4,128]{3,1,0,2:T(2,128)S(1)}, f32[1,2,4,128]{3,1,0,2:T(2,128)S(1)}, u32[]{:S(2)}, u32[]{:S(2)}) collective-permute-start(f32[1,2,4,128]{3,1,0,2:T(2,128)S(1)} %get-tuple-element.32), channel_id=1, source_target_pairs={{0,8},{8,16},{16,24},{24,0},{1,9},{9,17},{17,25},{25,1},{2,10},{10... | collective-permute-start | bytes 12296 | tf_op jit(solution)/shard_map/ppermute | solution.py:352
  4.1 2.1 %collective-permute-start.1 = (f32[1,2,4,128]{3,1,0,2:T(2,128)S(1)}, f32[1,2,4,128]{3,1,0,2:T(2,128)S(1)}, u32[]{:S(2)}, u32[]{:S(2)}) collective-permute-start(f32[1,2,4,128]{3,1,0,2:T(2,128)S(1)} %get-tuple-element.33), channel_id=1, source_target_pairs={{8,0},{16,8},{24,16},{0,24},{9,1},{17,9},{25,17},{1,25},{10,2},{18... | collective-permute-start | bytes 12296 | tf_op jit(solution)/shard_map/ppermute | solution.py:354
  6.2 0.8 copy.22
  7.1 0.1 copy.23
  7.2 0.8 maximum_bitcast_fusion.col_ref
  8.1 0.0 collective-permute-done
  8.1 0.7 pad_maximum_fusion.2
  8.8 2.3 %collective-permute-start.2 = (f32[4,1,4,128]{3,1,0,2:T(1,128)S(1)}, f32[4,1,4,128]{3,1,0,2:T(1,128)S(1)}, u32[]{:S(2)}, u32[]{:S(2)}) collective-permute-start(f32[4,1,4,128]{3,1,0,2:T(1,128)S(1)} %get-tuple-element.30), channel_id=1, source_target_pairs={{0,1},{1,2},{2,3},{3,4},{4,5},{5,6},{6,7},{7,0},{8,9},{9,10},{10,1... | collective-permute-start | bytes 24584 | tf_op jit(solution)/shard_map/ppermute | solution.py:352
  11.1 0.0 collective-permute-start.3
  11.1 0.6 pad_add_fusion.me_ref
  11.7 0.7 copy.24
  12.4 0.0 collective-permute-done.2
  12.4 1.8 %collective-permute-done.3 = f32[4,1,4,128]{3,1,0,2:T(1,128)S(1)} collective-permute-done((f32[4,1,4,128]{3,1,0,2:T(1,128)S(1)}, f32[4,1,4,128]{3,1,0,2:T(1,128)S(1)}, u32[]{:S(2)}, u32[]{:S(2)}) %collective-permute-start.3) | collective-permute-done | bytes 8224 | tf_op jit(solution)/shard_map/ppermute | solution.py:354
  14.1 0.7 pad_maximum_fusion.1
  14.9 0.6 slice.109.kind_ref
  15.5 0.6 broadcast_in_dim.18.force_ref
  16.1 42.9 %shard_map.95 = (f32[2,4,4,7,16,128]{5,4,3,2,1,0:T(8,128)}, f32[2,4,4,7,16,128]{5,4,3,2,1,0:T(8,128)}) custom-call(s32[4,8]{1,0:T(4,128)} %bitcast.117, s32[4,8]{1,0:T(4,128)} %bitcast.118, s32[4]{0:T(128)} %pad_add_fusion.me_ref, f32[16,3,128]{2,1,0:T(4,128)} %bitcast.104, f32[16,1,128]{2,1,0:T(1,128)} %slice.109.kind_ref, ...), custom_call_target="tpu_custom_call" | custom-call | tf_op jit(solution)/shard_map/pallas_call | solution.py:236
  59.0 1.4 %slice_bitcast_fusion.1 = f32[4,4,7,16,128]{4,3,2,1,0:T(8,128)S(1)} fusion(f32[2,4,4,7,16,128]{5,4,3,2,1,0:T(8,128)} %get-tuple-element.10), kind=kLoop, calls=%fused_computation.3 | loop fusion | bytes 1835008 | tf_op jit(solution)/shard_map/squeeze | solution.py:366
  60.4 3.1 %collective-permute-start.4 = (f32[4,4,7,16,128]{4,3,2,1,0:T(8,128)S(1)}, f32[4,4,7,16,128]{4,3,2,1,0:T(8,128)S(1)}, u32[]{:S(2)}, u32[]{:S(2)}) collective-permute-start(f32[4,4,7,16,128]{4,3,2,1,0:T(8,128)S(1)} %slice_bitcast_fusion.1), channel_id=1, source_target_pairs={{0,1},{1,0},{2,3},{3,2},{4,5},{5,4},{6,7},{7,6},{8,9},{9,8},{10,11... | collective-permute-start | bytes 2752520 | tf_op jit(solution)/shard_map/ppermute | solution.py:362
  63.5 0.1 slice_bitcast_fusion
  63.6 0.4 collective-permute-start.14
  63.9 1.6 %collective-permute-done.4 = f32[4,4,7,16,128]{4,3,2,1,0:T(8,128)S(1)} collective-permute-done((f32[4,4,7,16,128]{4,3,2,1,0:T(8,128)S(1)}, f32[4,4,7,16,128]{4,3,2,1,0:T(8,128)S(1)}, u32[]{:S(2)}, u32[]{:S(2)}) %collective-permute-start.4) | collective-permute-done | bytes 917536 | tf_op jit(solution)/shard_map/ppermute | solution.py:362
  65.6 0.1 bitcast_add_fusion.1
  65.8 4.6 %collective-permute-start.5 = (f32[4,7,16,128]{3,2,1,0:T(8,128)S(1)}, f32[4,7,16,128]{3,2,1,0:T(8,128)S(1)}, u32[]{:S(2)}, u32[]{:S(2)}) collective-permute-start(f32[4,7,16,128]{3,2,1,0:T(8,128)S(1)} %get-tuple-element.18), channel_id=1, source_target_pairs={{0,2},{1,3},{2,0},{3,1},{4,6},{5,7},{6,4},{7,5},{8,10},{9,11},{10,... | collective-permute-start | bytes 688136 | tf_op jit(solution)/shard_map/ppermute | solution.py:362
  70.4 0.0 collective-permute-start.6
  70.4 1.3 collective-permute-start.7
  71.7 0.0 collective-permute-done.14
  71.7 0.1 bitcast_add_fusion
  71.9 1.5 %collective-permute-start.15 = (f32[4,7,16,128]{3,2,1,0:T(8,128)S(1)}, f32[4,7,16,128]{3,2,1,0:T(8,128)S(1)}, u32[]{:S(2)}, u32[]{:S(2)}) collective-permute-start(f32[4,7,16,128]{3,2,1,0:T(8,128)S(1)} %get-tuple-element.21), channel_id=1, source_target_pairs={{0,2},{1,3},{2,0},{3,1},{4,6},{5,7},{6,4},{7,5},{8,10},{9,11},{10,... | collective-permute-start | bytes 688136 | tf_op jit(solution)/shard_map/ppermute | solution.py:362
  73.3 0.0 collective-permute-start.16
  73.3 2.9 %collective-permute-done.5 = f32[4,7,16,128]{3,2,1,0:T(8,128)S(1)} collective-permute-done((f32[4,7,16,128]{3,2,1,0:T(8,128)S(1)}, f32[4,7,16,128]{3,2,1,0:T(8,128)S(1)}, u32[]{:S(2)}, u32[]{:S(2)}) %collective-permute-start.5) | collective-permute-done | bytes 229408 | tf_op jit(solution)/shard_map/ppermute | solution.py:362
  76.2 5.8 %collective-permute-done.6 = f32[4,7,16,128]{3,2,1,0:T(8,128)S(1)} collective-permute-done((f32[4,7,16,128]{3,2,1,0:T(8,128)S(1)}, f32[4,7,16,128]{3,2,1,0:T(8,128)S(1)}, u32[]{:S(2)}, u32[]{:S(2)}) %collective-permute-start.6) | collective-permute-done | bytes 229408 | tf_op jit(solution)/shard_map/ppermute | solution.py:362
  82.1 0.1 fusion.5
  82.2 2.6 %collective-permute-start.10 = (f32[7,16,128]{2,1,0:T(8,128)S(1)}, f32[7,16,128]{2,1,0:T(8,128)S(1)}, u32[]{:S(2)}, u32[]{:S(2)}) collective-permute-start(f32[7,16,128]{2,1,0:T(8,128)S(1)} %get-tuple-element.25), channel_id=1, source_target_pairs={{0,24},{8,16},{16,8},{24,0},{1,25},{9,17},{17,9},{25,1},{2,26},{10... | collective-permute-start | bytes 172040 | tf_op jit(solution)/shard_map/ppermute | solution.py:362
  84.7 0.0 collective-permute-start.8
  84.7 1.4 %collective-permute-done.15 = f32[4,7,16,128]{3,2,1,0:T(8,128)S(1)} collective-permute-done((f32[4,7,16,128]{3,2,1,0:T(8,128)S(1)}, f32[4,7,16,128]{3,2,1,0:T(8,128)S(1)}, u32[]{:S(2)}, u32[]{:S(2)}) %collective-permute-start.15) | collective-permute-done | bytes 229408 | tf_op jit(solution)/shard_map/ppermute | solution.py:362
  86.1 0.2 collective-permute-start.9
  86.4 5.5 %collective-permute-done.16 = f32[4,7,16,128]{3,2,1,0:T(8,128)S(1)} collective-permute-done((f32[4,7,16,128]{3,2,1,0:T(8,128)S(1)}, f32[4,7,16,128]{3,2,1,0:T(8,128)S(1)}, u32[]{:S(2)}, u32[]{:S(2)}) %collective-permute-start.16) | collective-permute-done | bytes 229408 | tf_op jit(solution)/shard_map/ppermute | solution.py:362
  91.9 0.1 fusion.2
  92.0 0.1 collective-permute-start.18
  92.1 2.8 %collective-permute-start.19 = (f32[7,16,128]{2,1,0:T(8,128)S(1)}, f32[7,16,128]{2,1,0:T(8,128)S(1)}, u32[]{:S(2)}, u32[]{:S(2)}) collective-permute-start(f32[7,16,128]{2,1,0:T(8,128)S(1)} %get-tuple-element.29), channel_id=1, source_target_pairs={{0,16},{8,24},{16,0},{24,8},{1,17},{9,25},{17,1},{25,9},{2,18},{10... | collective-permute-start | bytes 172040 | tf_op jit(solution)/shard_map/ppermute | solution.py:362
  94.9 0.7 collective-permute-start.20
  95.6 0.1 collective-permute-start.11
  95.7 2.8 %collective-permute-start.12 = (f32[7,16,128]{2,1,0:T(8,128)S(1)}, f32[7,16,128]{2,1,0:T(8,128)S(1)}, u32[]{:S(2)}, u32[]{:S(2)}) collective-permute-start(f32[7,16,128]{2,1,0:T(8,128)S(1)} %fusion.11), channel_id=1, source_target_pairs={{0,16},{8,24},{16,0},{24,8},{1,17},{9,25},{17,1},{25,9},{2,18},{10... | collective-permute-start | bytes 172040 | tf_op jit(solution)/shard_map/ppermute | solution.py:362
  98.5 0.7 collective-permute-start.13
  99.2 0.6 collective-permute-done.20
  99.9 0.1 collective-permute-start.21
  100.0 2.2 %collective-permute-start.22 = (f32[7,16,128]{2,1,0:T(8,128)S(1)}, f32[7,16,128]{2,1,0:T(8,128)S(1)}, u32[]{:S(2)}, u32[]{:S(2)}) collective-permute-start(f32[7,16,128]{2,1,0:T(8,128)S(1)} %fusion.8), channel_id=1, source_target_pairs={{0,16},{8,24},{16,0},{24,8},{1,17},{9,25},{17,1},{25,9},{2,18},{10... | collective-permute-start | bytes 172040 | tf_op jit(solution)/shard_map/ppermute | solution.py:362
  102.2 1.3 %collective-permute-start.23 = (f32[7,16,128]{2,1,0:T(8,128)S(1)}, f32[7,16,128]{2,1,0:T(8,128)S(1)}, u32[]{:S(2)}, u32[]{:S(2)}) collective-permute-start(f32[7,16,128]{2,1,0:T(8,128)S(1)} %fusion.8), channel_id=1, source_target_pairs={{0,24},{8,16},{16,8},{24,0},{1,25},{9,17},{17,9},{25,1},{2,26},{10... | collective-permute-start | bytes 172040 | tf_op jit(solution)/shard_map/ppermute | solution.py:362
  103.5 0.3 collective-permute-done.13
  103.8 0.3 collective-permute-done.21
  104.1 4.0 %collective-permute-done.22 = f32[7,16,128]{2,1,0:T(8,128)S(1)} collective-permute-done((f32[7,16,128]{2,1,0:T(8,128)S(1)}, f32[7,16,128]{2,1,0:T(8,128)S(1)}, u32[]{:S(2)}, u32[]{:S(2)}) %collective-permute-start.22) | collective-permute-done | bytes 57376 | tf_op jit(solution)/shard_map/ppermute | solution.py:362
  108.2 0.8 shard_map.96
  109.0 1.0 collective-permute-start.24
  110.0 0.1 collective-permute-start.25
  110.1 1.6 %collective-permute-start.26 = (f32[3,64,128]{2,1,0:T(8,128)S(1)}, f32[3,64,128]{2,1,0:T(8,128)S(1)}, u32[]{:S(2)}, u32[]{:S(2)}) collective-permute-start(f32[3,64,128]{2,1,0:T(8,128)S(1)} %get-tuple-element.15), channel_id=1, source_target_pairs={{0,6},{1,7},{2,4},{3,5},{4,2},{5,3},{6,0},{7,1},{8,14},{9,15},{10,... | collective-permute-start | bytes 294920 | tf_op jit(solution)/shard_map/ppermute | solution.py:362
  111.7 1.8 %collective-permute-done.24 = f32[6,64,128]{2,1,0:T(8,128)S(1)} collective-permute-done((f32[6,64,128]{2,1,0:T(8,128)S(1)}, f32[6,64,128]{2,1,0:T(8,128)S(1)}, u32[]{:S(2)}, u32[]{:S(2)}) %collective-permute-start.24) | collective-permute-done | bytes 196640 | tf_op jit(solution)/shard_map/ppermute | solution.py:362
  113.6 2.3 %collective-permute-done.25 = f32[6,64,128]{2,1,0:T(8,128)S(1)} collective-permute-done((f32[6,64,128]{2,1,0:T(8,128)S(1)}, f32[6,64,128]{2,1,0:T(8,128)S(1)}, u32[]{:S(2)}, u32[]{:S(2)}) %collective-permute-start.25) | collective-permute-done | bytes 196640 | tf_op jit(solution)/shard_map/ppermute | solution.py:362
  115.9 4.8 %collective-permute-start.27 = (f32[29,64,128]{2,1,0:T(8,128)S(1)}, f32[29,64,128]{2,1,0:T(8,128)S(1)}, u32[]{:S(2)}, u32[]{:S(2)}) collective-permute-start(f32[29,64,128]{2,1,0:T(8,128)S(1)} %constant_dynamic-update-slice_fusion.mine_ref), channel_id=1, source_target_pairs={{0,1},{1,0},{2,3},{3,2},{4,5},{5,4},{6,7},{7,6},{8,9},{9,8},{10,11... | collective-permute-start | bytes 2850824 | tf_op jit(solution)/shard_map/ppermute | solution.py:362
  120.7 2.1 %collective-permute-done.27.other_ref = f32[29,64,128]{2,1,0:T(8,128)S(1)} collective-permute-done((f32[29,64,128]{2,1,0:T(8,128)S(1)}, f32[29,64,128]{2,1,0:T(8,128)S(1)}, u32[]{:S(2)}, u32[]{:S(2)}) %collective-permute-start.27) | collective-permute-done | bytes 950304 | tf_op jit(solution)/shard_map/ppermute | solution.py:362
  122.9 3.2 %shard_map.97 = (f32[192,1536]{1,0:T(8,128)}, f32[16,128]{1,0:T(8,128)S(1)}) custom-call(s32[4]{0:T(128)S(1)} %copy-done, s32[8,36]{1,0:T(8,128)S(1)} %copy-done.1, s32[8]{0:T(128)S(1)} %copy-done.3, f32[29,64,128]{2,1,0:T(8,128)S(1)} %constant_dynamic-update-slice_fusion.mine_ref, f32[29,64,128]{2,1,0:T(8,128)S(1)} %collective-permute-done.27.other_ref), custom_call_target="tpu_custom_call" | custom-call | tf_op jit(solution)/shard_map/pallas_call | solution.py:325
  126.1 0.6 dynamic_slice.3
  (43 shorter events, 0.4 us)
Async XLA Ops:
  2.0 6.1 %collective-permute-start = (f32[1,2,4,128]{3,1,0,2:T(2,128)S(1)}, f32[1,2,4,128]{3,1,0,2:T(2,128)S(1)}, u32[]{:S(2)}, u32[]{:S(2)}) collective-permute-start(f32[1,2,4,128]{3,1,0,2:T(2,128)S(1)} %get-tuple-element.32), channel_id=1, source_target_pairs={{0,8},{8,16},{16,24},{24,0},{1,9},{9,17},{17,25},{25,1},{2,10},{10... | collective-permute-start | bytes 12296 | tf_op jit(solution)/shard_map/ppermute | solution.py:352
  4.1 3.9 %collective-permute-start.1 = (f32[1,2,4,128]{3,1,0,2:T(2,128)S(1)}, f32[1,2,4,128]{3,1,0,2:T(2,128)S(1)}, u32[]{:S(2)}, u32[]{:S(2)}) collective-permute-start(f32[1,2,4,128]{3,1,0,2:T(2,128)S(1)} %get-tuple-element.33), channel_id=1, source_target_pairs={{8,0},{16,8},{24,16},{0,24},{9,1},{17,9},{25,17},{1,25},{10,2},{18... | collective-permute-start | bytes 12296 | tf_op jit(solution)/shard_map/ppermute | solution.py:354
  8.8 3.6 %collective-permute-start.2 = (f32[4,1,4,128]{3,1,0,2:T(1,128)S(1)}, f32[4,1,4,128]{3,1,0,2:T(1,128)S(1)}, u32[]{:S(2)}, u32[]{:S(2)}) collective-permute-start(f32[4,1,4,128]{3,1,0,2:T(1,128)S(1)} %get-tuple-element.30), channel_id=1, source_target_pairs={{0,1},{1,2},{2,3},{3,4},{4,5},{5,6},{6,7},{7,0},{8,9},{9,10},{10,1... | collective-permute-start | bytes 24584 | tf_op jit(solution)/shard_map/ppermute | solution.py:352
  11.1 3.1 %collective-permute-start.3 = (f32[4,1,4,128]{3,1,0,2:T(1,128)S(1)}, f32[4,1,4,128]{3,1,0,2:T(1,128)S(1)}, u32[]{:S(2)}, u32[]{:S(2)}) collective-permute-start(f32[4,1,4,128]{3,1,0,2:T(1,128)S(1)} %get-tuple-element.31), channel_id=1, source_target_pairs={{1,0},{2,1},{3,2},{4,3},{5,4},{6,5},{7,6},{0,7},{9,8},{10,9},{11,1... | collective-permute-start | bytes 24584 | tf_op jit(solution)/shard_map/ppermute | solution.py:354
  14.9 1.2 copy-start.6
  59.0 4.5 %copy-start.4 = (f32[2,4,4,7,16,128]{5,4,3,2,1,0:T(8,128)S(1)}, f32[2,4,4,7,16,128]{5,4,3,2,1,0:T(8,128)}, u32[]{:S(2)}) copy-start(f32[2,4,4,7,16,128]{5,4,3,2,1,0:T(8,128)} %get-tuple-element.11) | copy-start | bytes 5505028
  59.0 6.6 %copy-start.5 = (f32[2,4,4,7,16,128]{5,4,3,2,1,0:T(8,128)S(1)}, f32[2,4,4,7,16,128]{5,4,3,2,1,0:T(8,128)}, u32[]{:S(2)}) copy-start(f32[2,4,4,7,16,128]{5,4,3,2,1,0:T(8,128)} %get-tuple-element.10) | copy-start | bytes 5505028
  60.4 5.2 %collective-permute-start.4 = (f32[4,4,7,16,128]{4,3,2,1,0:T(8,128)S(1)}, f32[4,4,7,16,128]{4,3,2,1,0:T(8,128)S(1)}, u32[]{:S(2)}, u32[]{:S(2)}) collective-permute-start(f32[4,4,7,16,128]{4,3,2,1,0:T(8,128)S(1)} %slice_bitcast_fusion.1), channel_id=1, source_target_pairs={{0,1},{1,0},{2,3},{3,2},{4,5},{5,4},{6,7},{7,6},{8,9},{9,8},{10,11... | collective-permute-start | bytes 2752520 | tf_op jit(solution)/shard_map/ppermute | solution.py:362
  63.6 8.1 %collective-permute-start.14 = (f32[4,4,7,16,128]{4,3,2,1,0:T(8,128)S(1)}, f32[4,4,7,16,128]{4,3,2,1,0:T(8,128)S(1)}, u32[]{:S(2)}, u32[]{:S(2)}) collective-permute-start(f32[4,4,7,16,128]{4,3,2,1,0:T(8,128)S(1)} %slice_bitcast_fusion), channel_id=1, source_target_pairs={{0,1},{1,0},{2,3},{3,2},{4,5},{5,4},{6,7},{7,6},{8,9},{9,8},{10,11... | collective-permute-start | bytes 2752520 | tf_op jit(solution)/shard_map/ppermute | solution.py:362
  65.8 10.5 %collective-permute-start.5 = (f32[4,7,16,128]{3,2,1,0:T(8,128)S(1)}, f32[4,7,16,128]{3,2,1,0:T(8,128)S(1)}, u32[]{:S(2)}, u32[]{:S(2)}) collective-permute-start(f32[4,7,16,128]{3,2,1,0:T(8,128)S(1)} %get-tuple-element.18), channel_id=1, source_target_pairs={{0,2},{1,3},{2,0},{3,1},{4,6},{5,7},{6,4},{7,5},{8,10},{9,11},{10,... | collective-permute-start | bytes 688136 | tf_op jit(solution)/shard_map/ppermute | solution.py:362
  70.4 11.7 %collective-permute-start.6 = (f32[4,7,16,128]{3,2,1,0:T(8,128)S(1)}, f32[4,7,16,128]{3,2,1,0:T(8,128)S(1)}, u32[]{:S(2)}, u32[]{:S(2)}) collective-permute-start(f32[4,7,16,128]{3,2,1,0:T(8,128)S(1)} %get-tuple-element.20), channel_id=1, source_target_pairs={{0,4},{1,5},{2,6},{3,7},{4,0},{5,1},{6,2},{7,3},{8,12},{9,13},{10,... | collective-permute-start | bytes 688136 | tf_op jit(solution)/shard_map/ppermute | solution.py:362
  70.4 11.7 %collective-permute-start.7 = (f32[4,7,16,128]{3,2,1,0:T(8,128)S(1)}, f32[4,7,16,128]{3,2,1,0:T(8,128)S(1)}, u32[]{:S(2)}, u32[]{:S(2)}) collective-permute-start(f32[4,7,16,128]{3,2,1,0:T(8,128)S(1)} %get-tuple-element.19), channel_id=1, source_target_pairs={{0,6},{1,7},{2,4},{3,5},{4,2},{5,3},{6,0},{7,1},{8,14},{9,15},{10,... | collective-permute-start | bytes 688136 | tf_op jit(solution)/shard_map/ppermute | solution.py:362
  71.9 14.3 %collective-permute-start.15 = (f32[4,7,16,128]{3,2,1,0:T(8,128)S(1)}, f32[4,7,16,128]{3,2,1,0:T(8,128)S(1)}, u32[]{:S(2)}, u32[]{:S(2)}) collective-permute-start(f32[4,7,16,128]{3,2,1,0:T(8,128)S(1)} %get-tuple-element.21), channel_id=1, source_target_pairs={{0,2},{1,3},{2,0},{3,1},{4,6},{5,7},{6,4},{7,5},{8,10},{9,11},{10,... | collective-permute-start | bytes 688136 | tf_op jit(solution)/shard_map/ppermute | solution.py:362
  73.3 18.6 %collective-permute-start.16 = (f32[4,7,16,128]{3,2,1,0:T(8,128)S(1)}, f32[4,7,16,128]{3,2,1,0:T(8,128)S(1)}, u32[]{:S(2)}, u32[]{:S(2)}) collective-permute-start(f32[4,7,16,128]{3,2,1,0:T(8,128)S(1)} %get-tuple-element.23), channel_id=1, source_target_pairs={{0,4},{1,5},{2,6},{3,7},{4,0},{5,1},{6,2},{7,3},{8,12},{9,13},{10,... | collective-permute-start | bytes 688136 | tf_op jit(solution)/shard_map/ppermute | solution.py:362
  76.2 15.7 %collective-permute-start.17 = (f32[4,7,16,128]{3,2,1,0:T(8,128)S(1)}, f32[4,7,16,128]{3,2,1,0:T(8,128)S(1)}, u32[]{:S(2)}, u32[]{:S(2)}) collective-permute-start(f32[4,7,16,128]{3,2,1,0:T(8,128)S(1)} %get-tuple-element.22), channel_id=1, source_target_pairs={{0,6},{1,7},{2,4},{3,5},{4,2},{5,3},{6,0},{7,1},{8,14},{9,15},{10,... | collective-permute-start | bytes 688136 | tf_op jit(solution)/shard_map/ppermute | solution.py:362
  82.2 12.7 %collective-permute-start.10 = (f32[7,16,128]{2,1,0:T(8,128)S(1)}, f32[7,16,128]{2,1,0:T(8,128)S(1)}, u32[]{:S(2)}, u32[]{:S(2)}) collective-permute-start(f32[7,16,128]{2,1,0:T(8,128)S(1)} %get-tuple-element.25), channel_id=1, source_target_pairs={{0,24},{8,16},{16,8},{24,0},{1,25},{9,17},{17,9},{25,1},{2,26},{10... | collective-permute-start | bytes 172040 | tf_op jit(solution)/shard_map/ppermute | solution.py:362
  84.7 10.9 %collective-permute-start.8 = (f32[7,16,128]{2,1,0:T(8,128)S(1)}, f32[7,16,128]{2,1,0:T(8,128)S(1)}, u32[]{:S(2)}, u32[]{:S(2)}) collective-permute-start(f32[7,16,128]{2,1,0:T(8,128)S(1)} %get-tuple-element.24), channel_id=1, source_target_pairs={{0,8},{8,0},{16,24},{24,16},{1,9},{9,1},{17,25},{25,17},{2,10},{10... | collective-permute-start | bytes 172040 | tf_op jit(solution)/shard_map/ppermute | solution.py:362
  86.1 22.1 %copy-start = (s32[4]{0:T(128)S(1)}, s32[4]{0:T(128)}, u32[]{:S(2)}) copy-start(s32[4]{0:T(128)} %pad_add_fusion.me_ref) | copy-start | bytes 52
  86.1 22.1 %copy-start.2 = (s32[4,15]{1,0:T(4,128)S(1)}, s32[4,15]{1,0:T(4,128)}, u32[]{:S(2)}) copy-start(s32[4,15]{1,0:T(4,128)} %constant.43.clone.send_ref) | copy-start | bytes 724
  86.1 9.5 %collective-permute-start.9 = (f32[7,16,128]{2,1,0:T(8,128)S(1)}, f32[7,16,128]{2,1,0:T(8,128)S(1)}, u32[]{:S(2)}, u32[]{:S(2)}) collective-permute-start(f32[7,16,128]{2,1,0:T(8,128)S(1)} %get-tuple-element.26), channel_id=1, source_target_pairs={{0,16},{8,24},{16,0},{24,8},{1,17},{9,25},{17,1},{25,9},{2,18},{10... | collective-permute-start | bytes 172040 | tf_op jit(solution)/shard_map/ppermute | solution.py:362
  92.0 6.5 %collective-permute-start.18 = (f32[7,16,128]{2,1,0:T(8,128)S(1)}, f32[7,16,128]{2,1,0:T(8,128)S(1)}, u32[]{:S(2)}, u32[]{:S(2)}) collective-permute-start(f32[7,16,128]{2,1,0:T(8,128)S(1)} %get-tuple-element.27), channel_id=1, source_target_pairs={{0,8},{8,0},{16,24},{24,16},{1,9},{9,1},{17,25},{25,17},{2,10},{10... | collective-permute-start | bytes 172040 | tf_op jit(solution)/shard_map/ppermute | solution.py:362
  92.1 7.2 %collective-permute-start.19 = (f32[7,16,128]{2,1,0:T(8,128)S(1)}, f32[7,16,128]{2,1,0:T(8,128)S(1)}, u32[]{:S(2)}, u32[]{:S(2)}) collective-permute-start(f32[7,16,128]{2,1,0:T(8,128)S(1)} %get-tuple-element.29), channel_id=1, source_target_pairs={{0,16},{8,24},{16,0},{24,8},{1,17},{9,25},{17,1},{25,9},{2,18},{10... | collective-permute-start | bytes 172040 | tf_op jit(solution)/shard_map/ppermute | solution.py:362
  94.9 5.0 %collective-permute-start.20 = (f32[7,16,128]{2,1,0:T(8,128)S(1)}, f32[7,16,128]{2,1,0:T(8,128)S(1)}, u32[]{:S(2)}, u32[]{:S(2)}) collective-permute-start(f32[7,16,128]{2,1,0:T(8,128)S(1)} %get-tuple-element.28), channel_id=1, source_target_pairs={{0,24},{8,16},{16,8},{24,0},{1,25},{9,17},{17,9},{25,1},{2,26},{10... | collective-permute-start | bytes 172040 | tf_op jit(solution)/shard_map/ppermute | solution.py:362
  95.6 6.5 %collective-permute-start.11 = (f32[7,16,128]{2,1,0:T(8,128)S(1)}, f32[7,16,128]{2,1,0:T(8,128)S(1)}, u32[]{:S(2)}, u32[]{:S(2)}) collective-permute-start(f32[7,16,128]{2,1,0:T(8,128)S(1)} %fusion.11), channel_id=1, source_target_pairs={{0,8},{8,0},{16,24},{24,16},{1,9},{9,1},{17,25},{25,17},{2,10},{10... | collective-permute-start | bytes 172040 | tf_op jit(solution)/shard_map/ppermute | solution.py:362
  95.7 7.8 %collective-permute-start.12 = (f32[7,16,128]{2,1,0:T(8,128)S(1)}, f32[7,16,128]{2,1,0:T(8,128)S(1)}, u32[]{:S(2)}, u32[]{:S(2)}) collective-permute-start(f32[7,16,128]{2,1,0:T(8,128)S(1)} %fusion.11), channel_id=1, source_target_pairs={{0,16},{8,24},{16,0},{24,8},{1,17},{9,25},{17,1},{25,9},{2,18},{10... | collective-permute-start | bytes 172040 | tf_op jit(solution)/shard_map/ppermute | solution.py:362
  98.5 5.2 %collective-permute-start.13 = (f32[7,16,128]{2,1,0:T(8,128)S(1)}, f32[7,16,128]{2,1,0:T(8,128)S(1)}, u32[]{:S(2)}, u32[]{:S(2)}) collective-permute-start(f32[7,16,128]{2,1,0:T(8,128)S(1)} %fusion.11), channel_id=1, source_target_pairs={{0,24},{8,16},{16,8},{24,0},{1,25},{9,17},{17,9},{25,1},{2,26},{10... | collective-permute-start | bytes 172040 | tf_op jit(solution)/shard_map/ppermute | solution.py:362
  99.9 4.2 %collective-permute-start.21 = (f32[7,16,128]{2,1,0:T(8,128)S(1)}, f32[7,16,128]{2,1,0:T(8,128)S(1)}, u32[]{:S(2)}, u32[]{:S(2)}) collective-permute-start(f32[7,16,128]{2,1,0:T(8,128)S(1)} %fusion.8), channel_id=1, source_target_pairs={{0,8},{8,0},{16,24},{24,16},{1,9},{9,1},{17,25},{25,17},{2,10},{10... | collective-permute-start | bytes 172040 | tf_op jit(solution)/shard_map/ppermute | solution.py:362
  100.0 8.1 %collective-permute-start.22 = (f32[7,16,128]{2,1,0:T(8,128)S(1)}, f32[7,16,128]{2,1,0:T(8,128)S(1)}, u32[]{:S(2)}, u32[]{:S(2)}) collective-permute-start(f32[7,16,128]{2,1,0:T(8,128)S(1)} %fusion.8), channel_id=1, source_target_pairs={{0,16},{8,24},{16,0},{24,8},{1,17},{9,25},{17,1},{25,9},{2,18},{10... | collective-permute-start | bytes 172040 | tf_op jit(solution)/shard_map/ppermute | solution.py:362
  102.2 5.9 %collective-permute-start.23 = (f32[7,16,128]{2,1,0:T(8,128)S(1)}, f32[7,16,128]{2,1,0:T(8,128)S(1)}, u32[]{:S(2)}, u32[]{:S(2)}) collective-permute-start(f32[7,16,128]{2,1,0:T(8,128)S(1)} %fusion.8), channel_id=1, source_target_pairs={{0,24},{8,16},{16,8},{24,0},{1,25},{9,17},{17,9},{25,1},{2,26},{10... | collective-permute-start | bytes 172040 | tf_op jit(solution)/shard_map/ppermute | solution.py:362
  108.1 14.8 %copy-start.1 = (s32[8,36]{1,0:T(8,128)S(1)}, s32[8,36]{1,0:T(8,128)}, u32[]{:S(2)}) copy-start(s32[8,36]{1,0:T(8,128)} %constant.44.clone.table_ref) | copy-start | bytes 3460
  108.1 14.8 %copy-start.3 = (s32[8]{0:T(128)S(1)}, s32[8]{0:T(128)}, u32[]{:S(2)}) copy-start(s32[8]{0:T(128)} %constant.45.clone.rhs_at_ref) | copy-start | bytes 100
  109.0 4.6 %collective-permute-start.24 = (f32[6,64,128]{2,1,0:T(8,128)S(1)}, f32[6,64,128]{2,1,0:T(8,128)S(1)}, u32[]{:S(2)}, u32[]{:S(2)}) collective-permute-start(f32[6,64,128]{2,1,0:T(8,128)S(1)} %get-tuple-element.13), channel_id=1, source_target_pairs={{0,2},{1,3},{2,0},{3,1},{4,6},{5,7},{6,4},{7,5},{8,10},{9,11},{10,... | collective-permute-start | bytes 589832 | tf_op jit(solution)/shard_map/ppermute | solution.py:362
  110.0 5.9 %collective-permute-start.25 = (f32[6,64,128]{2,1,0:T(8,128)S(1)}, f32[6,64,128]{2,1,0:T(8,128)S(1)}, u32[]{:S(2)}, u32[]{:S(2)}) collective-permute-start(f32[6,64,128]{2,1,0:T(8,128)S(1)} %get-tuple-element.14), channel_id=1, source_target_pairs={{0,4},{1,5},{2,6},{3,7},{4,0},{5,1},{6,2},{7,3},{8,12},{9,13},{10,... | collective-permute-start | bytes 589832 | tf_op jit(solution)/shard_map/ppermute | solution.py:362
  110.1 5.8 %collective-permute-start.26 = (f32[3,64,128]{2,1,0:T(8,128)S(1)}, f32[3,64,128]{2,1,0:T(8,128)S(1)}, u32[]{:S(2)}, u32[]{:S(2)}) collective-permute-start(f32[3,64,128]{2,1,0:T(8,128)S(1)} %get-tuple-element.15), channel_id=1, source_target_pairs={{0,6},{1,7},{2,4},{3,5},{4,2},{5,3},{6,0},{7,1},{8,14},{9,15},{10,... | collective-permute-start | bytes 294920 | tf_op jit(solution)/shard_map/ppermute | solution.py:362
  115.9 6.9 %collective-permute-start.27 = (f32[29,64,128]{2,1,0:T(8,128)S(1)}, f32[29,64,128]{2,1,0:T(8,128)S(1)}, u32[]{:S(2)}, u32[]{:S(2)}) collective-permute-start(f32[29,64,128]{2,1,0:T(8,128)S(1)} %constant_dynamic-update-slice_fusion.mine_ref), channel_id=1, source_target_pairs={{0,1},{1,0},{2,3},{3,2},{4,5},{5,4},{6,7},{7,6},{8,9},{9,8},{10,11... | collective-permute-start | bytes 2850824 | tf_op jit(solution)/shard_map/ppermute | solution.py:362

commit v3 on v2

--- a/solution.py
+++ b/solution.py
@@ -118,7 +118,7 @@
     put(RHS, jnp.concatenate(lines + [jnp.zeros((HALF - TILES, HALF), jnp.float32)], axis=0))
 
 
-def design_kernel(off_ref, mask_ref, me_ref, rows_ref, kind_ref, col_ref, force_ref, *refs, plan, by_blocks, beads, slots, unroll):
+def design_kernel(off_ref, mask_ref, me_ref, rows_ref, kind_ref, col_ref, force_ref, *refs, plan, by_blocks, beads, slots, groups):
     outs = refs[:CHUNKS]
     pos_s, lt_s, code_s, w_s, res_s, rows_s, left_s, list_s = refs[CHUNKS:]
     b = pl.program_id(0)
@@ -128,7 +128,6 @@
     for t in range(slots):
         list_s[live] = off_ref[b, t]
         live = live + mask_ref[b, t]
-    chunks = (live + 1) // 2
     colv = [jnp.broadcast_to(col_ref[0, :, a:a+1], (beads, beads)) for a in range(3)]
     def geom(s, c):
         o = list_s[s]
@@ -153,67 +152,72 @@
         w_s[2, s] = d2 * sc
         return c
     lax.fori_loop(0, live, geom, 0)
-    @pl.when(live % 2 == 1)
-    def _():
-        z = jnp.zeros((beads, beads), jnp.float32)
-        pos_s[live] = z
-        lt_s[live] = z + NEG
-        code_s[live] = z
-        for a in range(3):
-            w_s[a, live] = z
-
-    cen = (lax.broadcasted_iota(jnp.int32, (SPAN, beads), 0).astype(jnp.float32) - 15.5) * ROOT
+    first = (lax.broadcasted_iota(jnp.int32, (8, beads), 0).astype(jnp.float32) - 15.5) * ROOT
     row24 = lax.broadcasted_iota(jnp.int32, (24, beads), 0).astype(jnp.float32)
-
-    def one(i, n):
-        gs = []
-        ws = []
-        for s in range(n):
-            x = pos_s[s, pl.ds(i, 1), :] - cen
-            g = jnp.exp2(lt_s[s, pl.ds(i, 1), :] - x * x).astype(jnp.bfloat16)
-            gs.append(g)
-            hit = code_s[s, pl.ds(i, 1), :] == row24
-            w = [jnp.where(hit, w_s[a, s, pl.ds(i, 1), :], 0.0) for a in range(3)]
-            ws.append(jnp.concatenate(w, axis=0).astype(jnp.bfloat16))
-        g = jnp.concatenate(gs, axis=1)
-        w = jnp.concatenate(ws, axis=1)
+    lane = lax.broadcasted_iota(jnp.int32, (8, 128), 1)
+    low = lane < 64
+    ahead = 8.0 * ROOT
+
+    def factors(i, s):
+        x = pos_s[s, pl.ds(i, 1), :] - first
+        e = lt_s[s, pl.ds(i, 1), :] - x * x
+        d = x * (2.0 * ahead) - ahead * ahead
+        powers = [e]
+        for v in range(1, SPAN // 8):
+            e = e + d
+            d = d - 2.0 * ahead * ahead
+            powers.append(e)
+        g = jnp.exp2(jnp.concatenate(powers[2:] + powers[:2], axis=0)).astype(jnp.bfloat16)
+        hit = code_s[s, pl.ds(i, 1), :] == row24
+        w = [jnp.where(hit, w_s[a, s, pl.ds(i, 1), :], 0.0) for a in range(3)]
+        return g, jnp.concatenate(w, axis=0).astype(jnp.bfloat16)
+
+    def couple(i, at, n):
+        both = [[factors(i + 8 * k, s) for s in range(n)] for k in range(2)]
+        g = jnp.concatenate([jnp.concatenate([f[0] for f in row], axis=1) for row in both], axis=0)
+        w = jnp.concatenate([jnp.concatenate([f[1] for f in row], axis=1) for row in both], axis=0)
         r = lax.dot_general(w, g, (((1,), (1,)), ((), ())), preferred_element_type=jnp.float32)
-        res_s[pl.ds(pl.multiple_of(i * 72, 8), 72), 0:SPAN] = r
-
-    for c in range(1, slots // 2 + 1):
-        @pl.when(chunks == c)
-        def _(c=c):
-            def body(i, carry):
-                for q in range(unroll):
-                    one(i * unroll + q, 2 * c)
+        left = lax.broadcasted_iota(jnp.int32, (72, 128), 1) < 64
+        res_s[pl.ds(pl.multiple_of(at * 72, 8), 72), :] = jnp.where(left, r[0:72], r[72:144])
+
+    for n in range(1, slots + 1):
+        @pl.when(live == n)
+        def _(n=n):
+            def body(g, carry):
+                for q in range(8 * groups):
+                    couple((g * groups + q // 8) * 16 + q % 8, (g * groups + q // 8) * 8 + q % 8, n)
                 return carry
-            lax.fori_loop(0, beads // unroll, body, 0)
-    @pl.when(chunks == 0)
+            lax.fori_loop(0, beads // (16 * groups), body, 0)
+
+    @pl.when(live == 0)
     def _():
         res_s[...] = jnp.zeros_like(res_s)
 
-    lane = lax.broadcasted_iota(jnp.int32, (8, 128), 1)
-    low64 = lane < 64
+    cut = lane % 64
+
     def unfold(g, carry):
         i0 = g * 16
         kt16 = jnp.broadcast_to(col_ref[0, pl.ds(pl.multiple_of(i0, 16), 16), 3:4], (16, 128))
+        is_t = [kt16 == float(t) for t in range(3)]
         for a in range(3):
             d = []
             for t in range(3):
+                r = [res_s[pl.ds(g * 8 * 72 + a * 24 + t * 8 + m, 8, stride=72), :] for m in range(8)]
+                r = [jnp.zeros_like(lane, jnp.float32)] + r + [jnp.zeros_like(lane, jnp.float32)]
                 halves = []
-                for h in range(2):
-                    rr = [res_s[pl.ds((i0 + h * 8) * 72 + a * 24 + t * 8 + m, 8, stride=72), :] for m in range(8)]
-                    pair = lambda p, q: jnp.where(low64, p, pltpu.roll(q, 64, 1))
-                    e0, e1 = pair(rr[0], rr[2]), pair(rr[4], rr[6])
-                    o0, o1 = pair(rr[1], rr[3]), pair(rr[5], rr[7])
-                    e0, e1 = pltpu.roll(e0, 112, 1), pltpu.roll(e1, 112, 1)
-                    o0, o1 = pltpu.roll(o0, 16, 1), pltpu.roll(o1, 16, 1)
-                    lo = jnp.where(lane < 112, e0, e1) + jnp.where(lane < 16, 0.0, o0)
-                    hi = jnp.where(lane < 112, e1, 0.0) + jnp.where(lane < 16, o0, o1)
-                    halves.append((lo, hi))
-                d.append([jnp.concatenate([halves[0][v], halves[1][v]], axis=0) for v in range(2)])
-            is_t = [kt16 == float(t) for t in range(3)]
-            for p, (lo_t, hi_t) in enumerate([(0, 0), (0, 1), (0, 2), (1, 1), (1, 2), (2, 2)]):
+                for v in range(2):
+                    m = 4 * v + 1
+                    el = jnp.where(cut < 48, r[m], r[m + 2])
+                    eu = jnp.where(cut < 48, r[m + 2], r[min(m + 4, 9)])
+                    ol = jnp.where(cut < 48, r[m + 1], r[m + 3])
+                    ou = jnp.where(cut < 32, r[m + 3], jnp.where(cut < 48, r[m - 1], r[m + 1]))
+                    et = pltpu.roll(jnp.where(low, eu, el), 64, 1)
+                    ot = pltpu.roll(jnp.where(low, ou, ol), 64, 1)
+                    near = jnp.where(low, el, et) + pltpu.roll(jnp.where(low, ol, ot), 32, 1)
+                    far = jnp.where(low, et, eu) + pltpu.roll(jnp.where(low, ot, ou), 32, 1)
+                    halves.append(jnp.concatenate([near, far], axis=0))
+                d.append(halves)
+            for p, (lo_t, hi_t) in enumerate(CLASSES):
                 for v in range(2):
                     x = jnp.where(is_t[lo_t], d[hi_t][v], 0.0)
                     if lo_t != hi_t:
@@ -227,14 +231,14 @@
         gram_tiles(me_ref, force_ref, rows_s, left_s, outs, plan)
 
 
-def design(off, mask, me, rows, kind, cols, force, plan, by_blocks, unroll=16):
+def design(off, mask, me, rows, kind, cols, force, plan, by_blocks, groups=2):
     nb, slots = off.shape
     beads = rows.shape[-1]
     n_src = rows.shape[0]
     total = nb * 3 * beads
     share = (2, plan.pairs, plan.size_x, plan.slots, plan.part, HALF)
     return pl.pallas_call(
-        functools.partial(design_kernel, plan=plan, by_blocks=by_blocks, beads=beads, slots=slots, unroll=unroll),
+        functools.partial(design_kernel, plan=plan, by_blocks=by_blocks, beads=beads, slots=slots, groups=groups),
         grid_spec=pltpu.PrefetchScalarGridSpec(
             num_scalar_prefetch=3,
             grid=(nb,),
@@ -250,7 +254,7 @@
                 pltpu.VMEM((slots, beads, beads), jnp.float32),
                 pltpu.VMEM((slots, beads, beads), jnp.float32),
                 pltpu.VMEM((3, slots, beads, beads), jnp.float32),
-                pltpu.VMEM((beads * 72, 128), jnp.float32),
+                pltpu.VMEM((beads // 2 * 72, 128), jnp.float32),
                 pltpu.VMEM((total, PAIRS * K), jnp.bfloat16),
                 pltpu.VMEM((K, total), jnp.bfloat16),
                 pltpu.SMEM((slots + 1,), jnp.int32),

time: 126 us -> 123 us (0.976); the launches traced: 127 us -> 121 us
  waiting for transfers between devices: 30.6 us -> 25 us
  starting transfers between devices: 38.4 us -> 41.4 us
  Pallas kernels: 46.8 us -> 43.9 us
    ppermute x24, waiting for transfers between devices: 28.9 us -> 23.2 us  [swap(): lax.ppermute(x, axis, [(i, i ^ flip) for i in range(lax.axis_size(axis))])]
    ppermute x24, starting transfers between devices: 31.9 us -> 34.9 us  [swap(): lax.ppermute(x, axis, [(i, i ^ flip) for i in range(lax.axis_size(axis))])]
    pallas_call x1, Pallas kernels: 42.9 us -> 40 us  [design(): pl.pallas_call(functools.partial(design_kernel, plan=plan, by_blocks=by_b...]
  transfers between devices with their start and end apart: 28 -> 28, of which waited for: 13 -> 14; matrix products, arithmetic and copies ran while one was open for 3% -> 3% of each run, Pallas kernels for 0% -> 0%
where the time goes in v3:
time: 123 us; the launch traced here: 121 us
  Pallas kernels  43.9 us (36%)
  starting transfers between devices  41.4 us (34%)
  waiting for transfers between devices  25 us (20%)
  local copies, waits for them, and re-layouts  5.26 us (4%)
  other arithmetic  4.74 us (4%)
    pallas_call x1, Pallas kernels, design(): pl.pallas_call(functools.partial(design_kernel, plan=plan, by_blocks=by_b...  40 us
    ppermute x24, starting transfers between devices, swap(): lax.ppermute(x, axis, [(i, i ^ flip) for i in range(lax.axis_size(axis))])  34.9 us
    ppermute x24, waiting for transfers between devices, swap(): lax.ppermute(x, axis, [(i, i ^ flip) for i in range(lax.axis_size(axis))])  23.2 us
    ppermute x2, starting transfers between devices, extended(): lax.ppermute(tail, axis, [(i, (i + 1) % count) for i in range(count)])  4.39 us
    pallas_call x1, Pallas kernels, place(): pl.pallas_call(functools.partial(place_kernel, plan=plan), grid_spec=pltp...  3.17 us
  transfers between devices with their start and end apart: 28, of which 14 were waited for; matrix products, arithmetic and copies ran while one was open for 3% of the time, Pallas kernels for 0%

profile of v3, /device:TPU:1, one launch (start us, length us, event | category | flops | bytes accessed | tf_op | source)
XLA Modules:
  0.0 121.2 jit_solution(3649806758261210600)
XLA Ops:
  0.6 0.7 fusion.14
  1.3 0.7 fusion.12
  2.0 2.1 %collective-permute-start = (f32[1,2,4,128]{3,1,0,2:T(2,128)S(1)}, f32[1,2,4,128]{3,1,0,2:T(2,128)S(1)}, u32[]{:S(2)}, u32[]{:S(2)}) collective-permute-start(f32[1,2,4,128]{3,1,0,2:T(2,128)S(1)} %get-tuple-element.32), channel_id=1, source_target_pairs={{0,8},{8,16},{16,24},{24,0},{1,9},{9,17},{17,25},{25,1},{2,10},{10... | collective-permute-start | bytes 12296 | tf_op jit(solution)/shard_map/ppermute | solution.py:356
  4.1 2.1 %collective-permute-start.1 = (f32[1,2,4,128]{3,1,0,2:T(2,128)S(1)}, f32[1,2,4,128]{3,1,0,2:T(2,128)S(1)}, u32[]{:S(2)}, u32[]{:S(2)}) collective-permute-start(f32[1,2,4,128]{3,1,0,2:T(2,128)S(1)} %get-tuple-element.33), channel_id=1, source_target_pairs={{8,0},{16,8},{24,16},{0,24},{9,1},{17,9},{25,17},{1,25},{10,2},{18... | collective-permute-start | bytes 12296 | tf_op jit(solution)/shard_map/ppermute | solution.py:358
  6.2 0.8 copy.22
  7.1 0.1 copy.23
  7.2 0.8 maximum_bitcast_fusion.col_ref
  8.1 0.0 collective-permute-done
  8.1 0.7 pad_maximum_fusion.2
  8.8 2.3 %collective-permute-start.2 = (f32[4,1,4,128]{3,1,0,2:T(1,128)S(1)}, f32[4,1,4,128]{3,1,0,2:T(1,128)S(1)}, u32[]{:S(2)}, u32[]{:S(2)}) collective-permute-start(f32[4,1,4,128]{3,1,0,2:T(1,128)S(1)} %get-tuple-element.30), channel_id=1, source_target_pairs={{0,1},{1,2},{2,3},{3,4},{4,5},{5,6},{6,7},{7,0},{8,9},{9,10},{10,1... | collective-permute-start | bytes 24584 | tf_op jit(solution)/shard_map/ppermute | solution.py:356
  11.1 0.0 collective-permute-start.3
  11.1 0.6 pad_add_fusion.me_ref
  11.7 0.7 copy.24
  12.4 0.0 collective-permute-done.2
  12.4 1.8 %collective-permute-done.3 = f32[4,1,4,128]{3,1,0,2:T(1,128)S(1)} collective-permute-done((f32[4,1,4,128]{3,1,0,2:T(1,128)S(1)}, f32[4,1,4,128]{3,1,0,2:T(1,128)S(1)}, u32[]{:S(2)}, u32[]{:S(2)}) %collective-permute-start.3) | collective-permute-done | bytes 8224 | tf_op jit(solution)/shard_map/ppermute | solution.py:358
  14.1 0.7 pad_maximum_fusion.1
  14.9 0.6 slice.109.kind_ref
  15.5 0.6 broadcast_in_dim.18.force_ref
  16.1 40.0 %shard_map.95 = (f32[2,4,4,7,16,128]{5,4,3,2,1,0:T(8,128)}, f32[2,4,4,7,16,128]{5,4,3,2,1,0:T(8,128)}) custom-call(s32[4,8]{1,0:T(4,128)} %bitcast.117, s32[4,8]{1,0:T(4,128)} %bitcast.118, s32[4]{0:T(128)} %pad_add_fusion.me_ref, f32[16,3,128]{2,1,0:T(4,128)} %bitcast.104, f32[16,1,128]{2,1,0:T(1,128)} %slice.109.kind_ref, ...), custom_call_target="tpu_custom_call" | custom-call | tf_op jit(solution)/shard_map/pallas_call | solution.py:240
  56.1 1.4 %slice_bitcast_fusion.1 = f32[4,4,7,16,128]{4,3,2,1,0:T(8,128)S(1)} fusion(f32[2,4,4,7,16,128]{5,4,3,2,1,0:T(8,128)} %get-tuple-element.10), kind=kLoop, calls=%fused_computation.3 | loop fusion | bytes 1835008 | tf_op jit(solution)/shard_map/squeeze | solution.py:370
  57.5 1.7 %collective-permute-start.4 = (f32[4,4,7,16,128]{4,3,2,1,0:T(8,128)S(1)}, f32[4,4,7,16,128]{4,3,2,1,0:T(8,128)S(1)}, u32[]{:S(2)}, u32[]{:S(2)}) collective-permute-start(f32[4,4,7,16,128]{4,3,2,1,0:T(8,128)S(1)} %slice_bitcast_fusion.1), channel_id=1, source_target_pairs={{0,1},{1,0},{2,3},{3,2},{4,5},{5,4},{6,7},{7,6},{8,9},{9,8},{10,11... | collective-permute-start | bytes 2752520 | tf_op jit(solution)/shard_map/ppermute | solution.py:366
  59.2 0.1 slice_bitcast_fusion
  59.3 0.4 collective-permute-start.14
  59.7 1.6 %collective-permute-done.4 = f32[4,4,7,16,128]{4,3,2,1,0:T(8,128)S(1)} collective-permute-done((f32[4,4,7,16,128]{4,3,2,1,0:T(8,128)S(1)}, f32[4,4,7,16,128]{4,3,2,1,0:T(8,128)S(1)}, u32[]{:S(2)}, u32[]{:S(2)}) %collective-permute-start.4) | collective-permute-done | bytes 917536 | tf_op jit(solution)/shard_map/ppermute | solution.py:366
  61.3 0.1 bitcast_add_fusion.1
  61.5 0.6 collective-permute-start.5
  62.1 2.5 %collective-permute-start.6 = (f32[4,7,16,128]{3,2,1,0:T(8,128)S(1)}, f32[4,7,16,128]{3,2,1,0:T(8,128)S(1)}, u32[]{:S(2)}, u32[]{:S(2)}) collective-permute-start(f32[4,7,16,128]{3,2,1,0:T(8,128)S(1)} %get-tuple-element.20), channel_id=1, source_target_pairs={{0,4},{1,5},{2,6},{3,7},{4,0},{5,1},{6,2},{7,3},{8,12},{9,13},{10,... | collective-permute-start | bytes 688136 | tf_op jit(solution)/shard_map/ppermute | solution.py:366
  64.6 1.1 collective-permute-start.7
  65.7 0.1 bitcast_add_fusion
  65.9 0.3 collective-permute-start.15
  66.2 1.3 %collective-permute-start.16 = (f32[4,7,16,128]{3,2,1,0:T(8,128)S(1)}, f32[4,7,16,128]{3,2,1,0:T(8,128)S(1)}, u32[]{:S(2)}, u32[]{:S(2)}) collective-permute-start(f32[4,7,16,128]{3,2,1,0:T(8,128)S(1)} %get-tuple-element.23), channel_id=1, source_target_pairs={{0,4},{1,5},{2,6},{3,7},{4,0},{5,1},{6,2},{7,3},{8,12},{9,13},{10,... | collective-permute-start | bytes 688136 | tf_op jit(solution)/shard_map/ppermute | solution.py:366
  67.5 0.9 collective-permute-done.5
  68.4 3.1 %collective-permute-start.17 = (f32[4,7,16,128]{3,2,1,0:T(8,128)S(1)}, f32[4,7,16,128]{3,2,1,0:T(8,128)S(1)}, u32[]{:S(2)}, u32[]{:S(2)}) collective-permute-start(f32[4,7,16,128]{3,2,1,0:T(8,128)S(1)} %get-tuple-element.22), channel_id=1, source_target_pairs={{0,6},{1,7},{2,4},{3,5},{4,2},{5,3},{6,0},{7,1},{8,14},{9,15},{10,... | collective-permute-start | bytes 688136 | tf_op jit(solution)/shard_map/ppermute | solution.py:366
  71.5 2.7 %collective-permute-done.6 = f32[4,7,16,128]{3,2,1,0:T(8,128)S(1)} collective-permute-done((f32[4,7,16,128]{3,2,1,0:T(8,128)S(1)}, f32[4,7,16,128]{3,2,1,0:T(8,128)S(1)}, u32[]{:S(2)}, u32[]{:S(2)}) %collective-permute-start.6) | collective-permute-done | bytes 229408 | tf_op jit(solution)/shard_map/ppermute | solution.py:366
  74.2 2.0 %collective-permute-done.7 = f32[4,7,16,128]{3,2,1,0:T(8,128)S(1)} collective-permute-done((f32[4,7,16,128]{3,2,1,0:T(8,128)S(1)}, f32[4,7,16,128]{3,2,1,0:T(8,128)S(1)}, u32[]{:S(2)}, u32[]{:S(2)}) %collective-permute-start.7) | collective-permute-done | bytes 229408 | tf_op jit(solution)/shard_map/ppermute | solution.py:366
  76.2 0.1 fusion.5
  76.3 0.1 collective-permute-start.10
  76.4 0.9 collective-permute-start.8
  77.3 1.0 collective-permute-done.15
  78.3 3.0 %collective-permute-start.9 = (f32[7,16,128]{2,1,0:T(8,128)S(1)}, f32[7,16,128]{2,1,0:T(8,128)S(1)}, u32[]{:S(2)}, u32[]{:S(2)}) collective-permute-start(f32[7,16,128]{2,1,0:T(8,128)S(1)} %get-tuple-element.26), channel_id=1, source_target_pairs={{0,16},{8,24},{16,0},{24,8},{1,17},{9,25},{17,1},{25,9},{2,18},{10... | collective-permute-start | bytes 172040 | tf_op jit(solution)/shard_map/ppermute | solution.py:366
  81.2 2.9 %collective-permute-done.16 = f32[4,7,16,128]{3,2,1,0:T(8,128)S(1)} collective-permute-done((f32[4,7,16,128]{3,2,1,0:T(8,128)S(1)}, f32[4,7,16,128]{3,2,1,0:T(8,128)S(1)}, u32[]{:S(2)}, u32[]{:S(2)}) %collective-permute-start.16) | collective-permute-done | bytes 229408 | tf_op jit(solution)/shard_map/ppermute | solution.py:366
  84.2 1.9 %collective-permute-done.17 = f32[4,7,16,128]{3,2,1,0:T(8,128)S(1)} collective-permute-done((f32[4,7,16,128]{3,2,1,0:T(8,128)S(1)}, f32[4,7,16,128]{3,2,1,0:T(8,128)S(1)}, u32[]{:S(2)}, u32[]{:S(2)}) %collective-permute-start.17) | collective-permute-done | bytes 229408 | tf_op jit(solution)/shard_map/ppermute | solution.py:366
  86.1 0.1 fusion.2
  86.2 0.9 collective-permute-start.18
  87.0 2.8 %collective-permute-start.20 = (f32[7,16,128]{2,1,0:T(8,128)S(1)}, f32[7,16,128]{2,1,0:T(8,128)S(1)}, u32[]{:S(2)}, u32[]{:S(2)}) collective-permute-start(f32[7,16,128]{2,1,0:T(8,128)S(1)} %get-tuple-element.28), channel_id=1, source_target_pairs={{0,24},{8,16},{16,8},{24,0},{1,25},{9,17},{17,9},{25,1},{2,26},{10... | collective-permute-start | bytes 172040 | tf_op jit(solution)/shard_map/ppermute | solution.py:366
  89.8 0.1 collective-permute-start.11
  89.9 0.8 collective-permute-start.12
  90.7 2.8 %collective-permute-start.13 = (f32[7,16,128]{2,1,0:T(8,128)S(1)}, f32[7,16,128]{2,1,0:T(8,128)S(1)}, u32[]{:S(2)}, u32[]{:S(2)}) collective-permute-start(f32[7,16,128]{2,1,0:T(8,128)S(1)} %fusion.11), channel_id=1, source_target_pairs={{0,24},{8,16},{16,8},{24,0},{1,25},{9,17},{17,9},{25,1},{2,26},{10... | collective-permute-start | bytes 172040 | tf_op jit(solution)/shard_map/ppermute | solution.py:366
  93.4 1.3 %collective-permute-start.21 = (f32[7,16,128]{2,1,0:T(8,128)S(1)}, f32[7,16,128]{2,1,0:T(8,128)S(1)}, u32[]{:S(2)}, u32[]{:S(2)}) collective-permute-start(f32[7,16,128]{2,1,0:T(8,128)S(1)} %fusion.8), channel_id=1, source_target_pairs={{0,8},{8,0},{16,24},{24,16},{1,9},{9,1},{17,25},{25,17},{2,10},{10... | collective-permute-start | bytes 172040 | tf_op jit(solution)/shard_map/ppermute | solution.py:366
  94.8 0.5 collective-permute-start.22
  95.3 1.8 %collective-permute-start.23 = (f32[7,16,128]{2,1,0:T(8,128)S(1)}, f32[7,16,128]{2,1,0:T(8,128)S(1)}, u32[]{:S(2)}, u32[]{:S(2)}) collective-permute-start(f32[7,16,128]{2,1,0:T(8,128)S(1)} %fusion.8), channel_id=1, source_target_pairs={{0,24},{8,16},{16,8},{24,0},{1,25},{9,17},{17,9},{25,1},{2,26},{10... | collective-permute-start | bytes 172040 | tf_op jit(solution)/shard_map/ppermute | solution.py:366
  97.1 0.1 collective-permute-done.21
  97.1 4.6 %collective-permute-done.22 = f32[7,16,128]{2,1,0:T(8,128)S(1)} collective-permute-done((f32[7,16,128]{2,1,0:T(8,128)S(1)}, f32[7,16,128]{2,1,0:T(8,128)S(1)}, u32[]{:S(2)}, u32[]{:S(2)}) %collective-permute-start.22) | collective-permute-done | bytes 57376 | tf_op jit(solution)/shard_map/ppermute | solution.py:366
  101.9 0.8 shard_map.96
  102.6 0.5 collective-permute-start.24
  103.1 1.1 collective-permute-start.25
  104.2 1.1 collective-permute-start.26
  105.4 1.8 %collective-permute-done.24 = f32[6,64,128]{2,1,0:T(8,128)S(1)} collective-permute-done((f32[6,64,128]{2,1,0:T(8,128)S(1)}, f32[6,64,128]{2,1,0:T(8,128)S(1)}, u32[]{:S(2)}, u32[]{:S(2)}) %collective-permute-start.24) | collective-permute-done | bytes 196640 | tf_op jit(solution)/shard_map/ppermute | solution.py:366
  107.2 0.7 collective-permute-done.25
  107.9 0.8 collective-permute-done.26
  108.7 6.5 %collective-permute-start.27 = (f32[29,64,128]{2,1,0:T(8,128)S(1)}, f32[29,64,128]{2,1,0:T(8,128)S(1)}, u32[]{:S(2)}, u32[]{:S(2)}) collective-permute-start(f32[29,64,128]{2,1,0:T(8,128)S(1)} %constant_dynamic-update-slice_fusion.mine_ref), channel_id=1, source_target_pairs={{0,1},{1,0},{2,3},{3,2},{4,5},{5,4},{6,7},{7,6},{8,9},{9,8},{10,11... | collective-permute-start | bytes 2850824 | tf_op jit(solution)/shard_map/ppermute | solution.py:366
  115.2 2.1 %collective-permute-done.27.other_ref = f32[29,64,128]{2,1,0:T(8,128)S(1)} collective-permute-done((f32[29,64,128]{2,1,0:T(8,128)S(1)}, f32[29,64,128]{2,1,0:T(8,128)S(1)}, u32[]{:S(2)}, u32[]{:S(2)}) %collective-permute-start.27) | collective-permute-done | bytes 950304 | tf_op jit(solution)/shard_map/ppermute | solution.py:366
  117.4 3.2 %shard_map.97 = (f32[192,1536]{1,0:T(8,128)}, f32[16,128]{1,0:T(8,128)S(1)}) custom-call(s32[4]{0:T(128)S(1)} %copy-done, s32[8,36]{1,0:T(8,128)S(1)} %copy-done.1, s32[8]{0:T(128)S(1)} %copy-done.3, f32[29,64,128]{2,1,0:T(8,128)S(1)} %constant_dynamic-update-slice_fusion.mine_ref, f32[29,64,128]{2,1,0:T(8,128)S(1)} %collective-permute-done.27.other_ref), custom_call_target="tpu_custom_call" | custom-call | tf_op jit(solution)/shard_map/pallas_call | solution.py:329
  120.5 0.6 dynamic_slice.3
  (43 shorter events, 0.4 us)
Async XLA Ops:
  2.0 6.1 %collective-permute-start = (f32[1,2,4,128]{3,1,0,2:T(2,128)S(1)}, f32[1,2,4,128]{3,1,0,2:T(2,128)S(1)}, u32[]{:S(2)}, u32[]{:S(2)}) collective-permute-start(f32[1,2,4,128]{3,1,0,2:T(2,128)S(1)} %get-tuple-element.32), channel_id=1, source_target_pairs={{0,8},{8,16},{16,24},{24,0},{1,9},{9,17},{17,25},{25,1},{2,10},{10... | collective-permute-start | bytes 12296 | tf_op jit(solution)/shard_map/ppermute | solution.py:356
  4.1 3.9 %collective-permute-start.1 = (f32[1,2,4,128]{3,1,0,2:T(2,128)S(1)}, f32[1,2,4,128]{3,1,0,2:T(2,128)S(1)}, u32[]{:S(2)}, u32[]{:S(2)}) collective-permute-start(f32[1,2,4,128]{3,1,0,2:T(2,128)S(1)} %get-tuple-element.33), channel_id=1, source_target_pairs={{8,0},{16,8},{24,16},{0,24},{9,1},{17,9},{25,17},{1,25},{10,2},{18... | collective-permute-start | bytes 12296 | tf_op jit(solution)/shard_map/ppermute | solution.py:358
  8.8 3.6 %collective-permute-start.2 = (f32[4,1,4,128]{3,1,0,2:T(1,128)S(1)}, f32[4,1,4,128]{3,1,0,2:T(1,128)S(1)}, u32[]{:S(2)}, u32[]{:S(2)}) collective-permute-start(f32[4,1,4,128]{3,1,0,2:T(1,128)S(1)} %get-tuple-element.30), channel_id=1, source_target_pairs={{0,1},{1,2},{2,3},{3,4},{4,5},{5,6},{6,7},{7,0},{8,9},{9,10},{10,1... | collective-permute-start | bytes 24584 | tf_op jit(solution)/shard_map/ppermute | solution.py:356
  11.1 3.1 %collective-permute-start.3 = (f32[4,1,4,128]{3,1,0,2:T(1,128)S(1)}, f32[4,1,4,128]{3,1,0,2:T(1,128)S(1)}, u32[]{:S(2)}, u32[]{:S(2)}) collective-permute-start(f32[4,1,4,128]{3,1,0,2:T(1,128)S(1)} %get-tuple-element.31), channel_id=1, source_target_pairs={{1,0},{2,1},{3,2},{4,3},{5,4},{6,5},{7,6},{0,7},{9,8},{10,9},{11,1... | collective-permute-start | bytes 24584 | tf_op jit(solution)/shard_map/ppermute | solution.py:358
  14.9 1.2 %copy-start.6 = (f32[4,4,4,128]{3,2,1,0:T(4,128)}, f32[4,4,4,128]{3,2,1,0:T(4,128)S(1)}, u32[]{:S(2)}) copy-start(f32[4,4,4,128]{3,2,1,0:T(4,128)S(1)} %copy.21) | copy-start | bytes 98308
  56.1 3.1 %copy-start.4 = (f32[2,4,4,7,16,128]{5,4,3,2,1,0:T(8,128)S(1)}, f32[2,4,4,7,16,128]{5,4,3,2,1,0:T(8,128)}, u32[]{:S(2)}) copy-start(f32[2,4,4,7,16,128]{5,4,3,2,1,0:T(8,128)} %get-tuple-element.11) | copy-start | bytes 5505028
  56.1 5.2 %copy-start.5 = (f32[2,4,4,7,16,128]{5,4,3,2,1,0:T(8,128)S(1)}, f32[2,4,4,7,16,128]{5,4,3,2,1,0:T(8,128)}, u32[]{:S(2)}) copy-start(f32[2,4,4,7,16,128]{5,4,3,2,1,0:T(8,128)} %get-tuple-element.10) | copy-start | bytes 5505028
  57.5 3.8 %collective-permute-start.4 = (f32[4,4,7,16,128]{4,3,2,1,0:T(8,128)S(1)}, f32[4,4,7,16,128]{4,3,2,1,0:T(8,128)S(1)}, u32[]{:S(2)}, u32[]{:S(2)}) collective-permute-start(f32[4,4,7,16,128]{4,3,2,1,0:T(8,128)S(1)} %slice_bitcast_fusion.1), channel_id=1, source_target_pairs={{0,1},{1,0},{2,3},{3,2},{4,5},{5,4},{6,7},{7,6},{8,9},{9,8},{10,11... | collective-permute-start | bytes 2752520 | tf_op jit(solution)/shard_map/ppermute | solution.py:366
  59.3 6.4 %collective-permute-start.14 = (f32[4,4,7,16,128]{4,3,2,1,0:T(8,128)S(1)}, f32[4,4,7,16,128]{4,3,2,1,0:T(8,128)S(1)}, u32[]{:S(2)}, u32[]{:S(2)}) collective-permute-start(f32[4,4,7,16,128]{4,3,2,1,0:T(8,128)S(1)} %slice_bitcast_fusion), channel_id=1, source_target_pairs={{0,1},{1,0},{2,3},{3,2},{4,5},{5,4},{6,7},{7,6},{8,9},{9,8},{10,11... | collective-permute-start | bytes 2752520 | tf_op jit(solution)/shard_map/ppermute | solution.py:366
  61.5 6.9 %collective-permute-start.5 = (f32[4,7,16,128]{3,2,1,0:T(8,128)S(1)}, f32[4,7,16,128]{3,2,1,0:T(8,128)S(1)}, u32[]{:S(2)}, u32[]{:S(2)}) collective-permute-start(f32[4,7,16,128]{3,2,1,0:T(8,128)S(1)} %get-tuple-element.18), channel_id=1, source_target_pairs={{0,2},{1,3},{2,0},{3,1},{4,6},{5,7},{6,4},{7,5},{8,10},{9,11},{10,... | collective-permute-start | bytes 688136 | tf_op jit(solution)/shard_map/ppermute | solution.py:366
  62.1 12.1 %collective-permute-start.6 = (f32[4,7,16,128]{3,2,1,0:T(8,128)S(1)}, f32[4,7,16,128]{3,2,1,0:T(8,128)S(1)}, u32[]{:S(2)}, u32[]{:S(2)}) collective-permute-start(f32[4,7,16,128]{3,2,1,0:T(8,128)S(1)} %get-tuple-element.20), channel_id=1, source_target_pairs={{0,4},{1,5},{2,6},{3,7},{4,0},{5,1},{6,2},{7,3},{8,12},{9,13},{10,... | collective-permute-start | bytes 688136 | tf_op jit(solution)/shard_map/ppermute | solution.py:366
  64.6 11.7 %collective-permute-start.7 = (f32[4,7,16,128]{3,2,1,0:T(8,128)S(1)}, f32[4,7,16,128]{3,2,1,0:T(8,128)S(1)}, u32[]{:S(2)}, u32[]{:S(2)}) collective-permute-start(f32[4,7,16,128]{3,2,1,0:T(8,128)S(1)} %get-tuple-element.19), channel_id=1, source_target_pairs={{0,6},{1,7},{2,4},{3,5},{4,2},{5,3},{6,0},{7,1},{8,14},{9,15},{10,... | collective-permute-start | bytes 688136 | tf_op jit(solution)/shard_map/ppermute | solution.py:366
  65.9 12.4 %collective-permute-start.15 = (f32[4,7,16,128]{3,2,1,0:T(8,128)S(1)}, f32[4,7,16,128]{3,2,1,0:T(8,128)S(1)}, u32[]{:S(2)}, u32[]{:S(2)}) collective-permute-start(f32[4,7,16,128]{3,2,1,0:T(8,128)S(1)} %get-tuple-element.21), channel_id=1, source_target_pairs={{0,2},{1,3},{2,0},{3,1},{4,6},{5,7},{6,4},{7,5},{8,10},{9,11},{10,... | collective-permute-start | bytes 688136 | tf_op jit(solution)/shard_map/ppermute | solution.py:366
  66.2 18.0 %collective-permute-start.16 = (f32[4,7,16,128]{3,2,1,0:T(8,128)S(1)}, f32[4,7,16,128]{3,2,1,0:T(8,128)S(1)}, u32[]{:S(2)}, u32[]{:S(2)}) collective-permute-start(f32[4,7,16,128]{3,2,1,0:T(8,128)S(1)} %get-tuple-element.23), channel_id=1, source_target_pairs={{0,4},{1,5},{2,6},{3,7},{4,0},{5,1},{6,2},{7,3},{8,12},{9,13},{10,... | collective-permute-start | bytes 688136 | tf_op jit(solution)/shard_map/ppermute | solution.py:366
  68.4 17.7 %collective-permute-start.17 = (f32[4,7,16,128]{3,2,1,0:T(8,128)S(1)}, f32[4,7,16,128]{3,2,1,0:T(8,128)S(1)}, u32[]{:S(2)}, u32[]{:S(2)}) collective-permute-start(f32[4,7,16,128]{3,2,1,0:T(8,128)S(1)} %get-tuple-element.22), channel_id=1, source_target_pairs={{0,6},{1,7},{2,4},{3,5},{4,2},{5,3},{6,0},{7,1},{8,14},{9,15},{10,... | collective-permute-start | bytes 688136 | tf_op jit(solution)/shard_map/ppermute | solution.py:366
  76.3 10.7 %collective-permute-start.10 = (f32[7,16,128]{2,1,0:T(8,128)S(1)}, f32[7,16,128]{2,1,0:T(8,128)S(1)}, u32[]{:S(2)}, u32[]{:S(2)}) collective-permute-start(f32[7,16,128]{2,1,0:T(8,128)S(1)} %get-tuple-element.25), channel_id=1, source_target_pairs={{0,24},{8,16},{16,8},{24,0},{1,25},{9,17},{17,9},{25,1},{2,26},{10... | collective-permute-start | bytes 172040 | tf_op jit(solution)/shard_map/ppermute | solution.py:366
  76.4 13.4 %collective-permute-start.8 = (f32[7,16,128]{2,1,0:T(8,128)S(1)}, f32[7,16,128]{2,1,0:T(8,128)S(1)}, u32[]{:S(2)}, u32[]{:S(2)}) collective-permute-start(f32[7,16,128]{2,1,0:T(8,128)S(1)} %get-tuple-element.24), channel_id=1, source_target_pairs={{0,8},{8,0},{16,24},{24,16},{1,9},{9,1},{17,25},{25,17},{2,10},{10... | collective-permute-start | bytes 172040 | tf_op jit(solution)/shard_map/ppermute | solution.py:366
  78.3 23.6 %copy-start = (s32[4]{0:T(128)S(1)}, s32[4]{0:T(128)}, u32[]{:S(2)}) copy-start(s32[4]{0:T(128)} %pad_add_fusion.me_ref) | copy-start | bytes 52
  78.3 23.6 %copy-start.2 = (s32[4,15]{1,0:T(4,128)S(1)}, s32[4,15]{1,0:T(4,128)}, u32[]{:S(2)}) copy-start(s32[4,15]{1,0:T(4,128)} %constant.43.clone.send_ref) | copy-start | bytes 724
  78.3 11.5 %collective-permute-start.9 = (f32[7,16,128]{2,1,0:T(8,128)S(1)}, f32[7,16,128]{2,1,0:T(8,128)S(1)}, u32[]{:S(2)}, u32[]{:S(2)}) collective-permute-start(f32[7,16,128]{2,1,0:T(8,128)S(1)} %get-tuple-element.26), channel_id=1, source_target_pairs={{0,16},{8,24},{16,0},{24,8},{1,17},{9,25},{17,1},{25,9},{2,18},{10... | collective-permute-start | bytes 172040 | tf_op jit(solution)/shard_map/ppermute | solution.py:366
  86.2 4.5 %collective-permute-start.18 = (f32[7,16,128]{2,1,0:T(8,128)S(1)}, f32[7,16,128]{2,1,0:T(8,128)S(1)}, u32[]{:S(2)}, u32[]{:S(2)}) collective-permute-start(f32[7,16,128]{2,1,0:T(8,128)S(1)} %get-tuple-element.27), channel_id=1, source_target_pairs={{0,8},{8,0},{16,24},{24,16},{1,9},{9,1},{17,25},{25,17},{2,10},{10... | collective-permute-start | bytes 172040 | tf_op jit(solution)/shard_map/ppermute | solution.py:366
  87.0 6.4 %collective-permute-start.19 = (f32[7,16,128]{2,1,0:T(8,128)S(1)}, f32[7,16,128]{2,1,0:T(8,128)S(1)}, u32[]{:S(2)}, u32[]{:S(2)}) collective-permute-start(f32[7,16,128]{2,1,0:T(8,128)S(1)} %get-tuple-element.29), channel_id=1, source_target_pairs={{0,16},{8,24},{16,0},{24,8},{1,17},{9,25},{17,1},{25,9},{2,18},{10... | collective-permute-start | bytes 172040 | tf_op jit(solution)/shard_map/ppermute | solution.py:366
  87.0 6.4 %collective-permute-start.20 = (f32[7,16,128]{2,1,0:T(8,128)S(1)}, f32[7,16,128]{2,1,0:T(8,128)S(1)}, u32[]{:S(2)}, u32[]{:S(2)}) collective-permute-start(f32[7,16,128]{2,1,0:T(8,128)S(1)} %get-tuple-element.28), channel_id=1, source_target_pairs={{0,24},{8,16},{16,8},{24,0},{1,25},{9,17},{17,9},{25,1},{2,26},{10... | collective-permute-start | bytes 172040 | tf_op jit(solution)/shard_map/ppermute | solution.py:366
  89.8 5.5 %collective-permute-start.11 = (f32[7,16,128]{2,1,0:T(8,128)S(1)}, f32[7,16,128]{2,1,0:T(8,128)S(1)}, u32[]{:S(2)}, u32[]{:S(2)}) collective-permute-start(f32[7,16,128]{2,1,0:T(8,128)S(1)} %fusion.11), channel_id=1, source_target_pairs={{0,8},{8,0},{16,24},{24,16},{1,9},{9,1},{17,25},{25,17},{2,10},{10... | collective-permute-start | bytes 172040 | tf_op jit(solution)/shard_map/ppermute | solution.py:366
  89.9 7.2 %collective-permute-start.12 = (f32[7,16,128]{2,1,0:T(8,128)S(1)}, f32[7,16,128]{2,1,0:T(8,128)S(1)}, u32[]{:S(2)}, u32[]{:S(2)}) collective-permute-start(f32[7,16,128]{2,1,0:T(8,128)S(1)} %fusion.11), channel_id=1, source_target_pairs={{0,16},{8,24},{16,0},{24,8},{1,17},{9,25},{17,1},{25,9},{2,18},{10... | collective-permute-start | bytes 172040 | tf_op jit(solution)/shard_map/ppermute | solution.py:366
  90.7 6.4 %collective-permute-start.13 = (f32[7,16,128]{2,1,0:T(8,128)S(1)}, f32[7,16,128]{2,1,0:T(8,128)S(1)}, u32[]{:S(2)}, u32[]{:S(2)}) collective-permute-start(f32[7,16,128]{2,1,0:T(8,128)S(1)} %fusion.11), channel_id=1, source_target_pairs={{0,24},{8,16},{16,8},{24,0},{1,25},{9,17},{17,9},{25,1},{2,26},{10... | collective-permute-start | bytes 172040 | tf_op jit(solution)/shard_map/ppermute | solution.py:366
  93.4 3.7 %collective-permute-start.21 = (f32[7,16,128]{2,1,0:T(8,128)S(1)}, f32[7,16,128]{2,1,0:T(8,128)S(1)}, u32[]{:S(2)}, u32[]{:S(2)}) collective-permute-start(f32[7,16,128]{2,1,0:T(8,128)S(1)} %fusion.8), channel_id=1, source_target_pairs={{0,8},{8,0},{16,24},{24,16},{1,9},{9,1},{17,25},{25,17},{2,10},{10... | collective-permute-start | bytes 172040 | tf_op jit(solution)/shard_map/ppermute | solution.py:366
  94.8 7.0 %collective-permute-start.22 = (f32[7,16,128]{2,1,0:T(8,128)S(1)}, f32[7,16,128]{2,1,0:T(8,128)S(1)}, u32[]{:S(2)}, u32[]{:S(2)}) collective-permute-start(f32[7,16,128]{2,1,0:T(8,128)S(1)} %fusion.8), channel_id=1, source_target_pairs={{0,16},{8,24},{16,0},{24,8},{1,17},{9,25},{17,1},{25,9},{2,18},{10... | collective-permute-start | bytes 172040 | tf_op jit(solution)/shard_map/ppermute | solution.py:366
  95.3 6.5 %collective-permute-start.23 = (f32[7,16,128]{2,1,0:T(8,128)S(1)}, f32[7,16,128]{2,1,0:T(8,128)S(1)}, u32[]{:S(2)}, u32[]{:S(2)}) collective-permute-start(f32[7,16,128]{2,1,0:T(8,128)S(1)} %fusion.8), channel_id=1, source_target_pairs={{0,24},{8,16},{16,8},{24,0},{1,25},{9,17},{17,9},{25,1},{2,26},{10... | collective-permute-start | bytes 172040 | tf_op jit(solution)/shard_map/ppermute | solution.py:366
  101.8 15.6 %copy-start.1 = (s32[8,36]{1,0:T(8,128)S(1)}, s32[8,36]{1,0:T(8,128)}, u32[]{:S(2)}) copy-start(s32[8,36]{1,0:T(8,128)} %constant.44.clone.table_ref) | copy-start | bytes 3460
  101.8 15.6 %copy-start.3 = (s32[8]{0:T(128)S(1)}, s32[8]{0:T(128)}, u32[]{:S(2)}) copy-start(s32[8]{0:T(128)} %constant.45.clone.rhs_at_ref) | copy-start | bytes 100
  102.6 4.6 %collective-permute-start.24 = (f32[6,64,128]{2,1,0:T(8,128)S(1)}, f32[6,64,128]{2,1,0:T(8,128)S(1)}, u32[]{:S(2)}, u32[]{:S(2)}) collective-permute-start(f32[6,64,128]{2,1,0:T(8,128)S(1)} %get-tuple-element.13), channel_id=1, source_target_pairs={{0,2},{1,3},{2,0},{3,1},{4,6},{5,7},{6,4},{7,5},{8,10},{9,11},{10,... | collective-permute-start | bytes 589832 | tf_op jit(solution)/shard_map/ppermute | solution.py:366
  103.1 4.8 %collective-permute-start.25 = (f32[6,64,128]{2,1,0:T(8,128)S(1)}, f32[6,64,128]{2,1,0:T(8,128)S(1)}, u32[]{:S(2)}, u32[]{:S(2)}) collective-permute-start(f32[6,64,128]{2,1,0:T(8,128)S(1)} %get-tuple-element.14), channel_id=1, source_target_pairs={{0,4},{1,5},{2,6},{3,7},{4,0},{5,1},{6,2},{7,3},{8,12},{9,13},{10,... | collective-permute-start | bytes 589832 | tf_op jit(solution)/shard_map/ppermute | solution.py:366
  104.2 4.4 %collective-permute-start.26 = (f32[3,64,128]{2,1,0:T(8,128)S(1)}, f32[3,64,128]{2,1,0:T(8,128)S(1)}, u32[]{:S(2)}, u32[]{:S(2)}) collective-permute-start(f32[3,64,128]{2,1,0:T(8,128)S(1)} %get-tuple-element.15), channel_id=1, source_target_pairs={{0,6},{1,7},{2,4},{3,5},{4,2},{5,3},{6,0},{7,1},{8,14},{9,15},{10,... | collective-permute-start | bytes 294920 | tf_op jit(solution)/shard_map/ppermute | solution.py:366
  108.7 8.7 %collective-permute-start.27 = (f32[29,64,128]{2,1,0:T(8,128)S(1)}, f32[29,64,128]{2,1,0:T(8,128)S(1)}, u32[]{:S(2)}, u32[]{:S(2)}) collective-permute-start(f32[29,64,128]{2,1,0:T(8,128)S(1)} %constant_dynamic-update-slice_fusion.mine_ref), channel_id=1, source_target_pairs={{0,1},{1,0},{2,3},{3,2},{4,5},{5,4},{6,7},{7,6},{8,9},{9,8},{10,11... | collective-permute-start | bytes 2850824 | tf_op jit(solution)/shard_map/ppermute | solution.py:366

commit v4 on v3

--- a/solution.py
+++ b/solution.py
@@ -12,6 +12,7 @@
 STEP=32; SPAN=64
 ROOT=math.sqrt(0.5*math.log2(math.e))
 NEG=-1e9
+MID=3
 
 CLASSES = ((0, 0), (0, 1), (0, 2), (1, 1), (1, 2), (2, 2))
 HALF = 128
@@ -118,9 +119,9 @@
     put(RHS, jnp.concatenate(lines + [jnp.zeros((HALF - TILES, HALF), jnp.float32)], axis=0))
 
 
-def design_kernel(off_ref, mask_ref, me_ref, rows_ref, kind_ref, col_ref, force_ref, *refs, plan, by_blocks, beads, slots, groups):
+def design_kernel(off_ref, mask_ref, me_ref, strip_ref, below_ref, above_ref, force_ref, *refs, plan, by_blocks, beads, slots, groups):
     outs = refs[:CHUNKS]
-    pos_s, lt_s, code_s, w_s, res_s, rows_s, left_s, list_s = refs[CHUNKS:]
+    pos_s, lt_s, code_s, w_s, res_s, rows_s, left_s, near_s, col_s, list_s = refs[CHUNKS:]
     b = pl.program_id(0)
     bx = b // by_blocks
     by = b % by_blocks
@@ -128,7 +129,19 @@
     for t in range(slots):
         list_s[live] = off_ref[b, t]
         live = live + mask_ref[b, t]
-    colv = [jnp.broadcast_to(col_ref[0, :, a:a+1], (beads, beads)) for a in range(3)]
+
+    @pl.when(b == 0)
+    def _():
+        near_s[...] = jnp.zeros_like(near_s)
+        for x in range(strip_ref.shape[0]):
+            near_s[x * (by_blocks + 2), 0:4] = below_ref[x, by_blocks - 1]
+            for y in range(by_blocks):
+                near_s[x * (by_blocks + 2) + y + 1, 0:4] = strip_ref[x, y]
+            near_s[x * (by_blocks + 2) + by_blocks + 1, 0:4] = above_ref[x, 0]
+
+    col_s[...] = near_s[(bx + 1) * (by_blocks + 2) + by + 1].T
+    colv = [jnp.broadcast_to(col_s[:, a:a + 1], (beads, beads)) for a in range(3)]
+
     def geom(s, c):
         o = list_s[s]
         ox = o // 3
@@ -136,49 +149,58 @@
         src = (bx + ox) * (by_blocks + 2) + by + oy
         sx = (ox - 1).astype(jnp.float32)
         sy = (oy - 1).astype(jnp.float32)
-        d0 = colv[0] - rows_ref[src, 0:1, :] - sx
-        d1 = colv[1] - rows_ref[src, 1:2, :] - sy
-        d2 = colv[2] - rows_ref[src, 2:3, :]
+        d0 = colv[0] - near_s[src, 0:1, :] - sx
+        d1 = colv[1] - near_s[src, 1:2, :] - sy
+        d2 = colv[2] - near_s[src, 2:3, :]
         r2 = d0 * d0 + d1 * d1 + d2 * d2
         u = jnp.sqrt(r2) * K
         m = jnp.minimum(jnp.floor(u * (1.0 / STEP)), K // STEP - 1.0)
         pos_s[s] = (u - m * STEP) * ROOT
         t = jnp.maximum(1.0 - r2, 0.0)
         lt_s[s] = jnp.where(t > 0.0, 2.0 * jnp.log2(jnp.where(t > 0.0, t, 1.0)), NEG)
-        code_s[s] = kind_ref[src, 0:1, :] * 8.0 + m
+        code_s[s] = near_s[src, 3:4, :] * 8.0 + m
         sc = 1.0 / jnp.sqrt(r2 + 0.05)
         w_s[0, s] = d0 * sc
         w_s[1, s] = d1 * sc
         w_s[2, s] = d2 * sc
         return c
     lax.fori_loop(0, live, geom, 0)
-    first = (lax.broadcasted_iota(jnp.int32, (8, beads), 0).astype(jnp.float32) - 15.5) * ROOT
+    middle = (lax.broadcasted_iota(jnp.int32, (8, beads), 0).astype(jnp.float32) + (8 * MID - 15.5)) * ROOT
     row24 = lax.broadcasted_iota(jnp.int32, (24, beads), 0).astype(jnp.float32)
     lane = lax.broadcasted_iota(jnp.int32, (8, 128), 1)
     low = lane < 64
     ahead = 8.0 * ROOT
 
     def factors(i, s):
-        x = pos_s[s, pl.ds(i, 1), :] - first
-        e = lt_s[s, pl.ds(i, 1), :] - x * x
-        d = x * (2.0 * ahead) - ahead * ahead
-        powers = [e]
+        x = pos_s[s, pl.ds(i, 1), :] - middle
+        up = lt_s[s, pl.ds(i, 1), :] - x * x
+        down = up
+        rise = x * (2.0 * ahead) - ahead * ahead
+        fall = rise
+        powers = {MID: up}
         for v in range(1, SPAN // 8):
-            e = e + d
-            d = d - 2.0 * ahead * ahead
-            powers.append(e)
-        g = jnp.exp2(jnp.concatenate(powers[2:] + powers[:2], axis=0)).astype(jnp.bfloat16)
+            if MID + v < SPAN // 8:
+                up = up + rise
+                rise = rise - 2.0 * ahead * ahead
+                powers[MID + v] = up
+            if MID - v >= 0:
+                fall = fall + 2.0 * ahead * ahead
+                down = down - fall
+                powers[MID - v] = down
+        order = [(v + 2) % (SPAN // 8) for v in range(SPAN // 8)]
+        g = jnp.exp2(jnp.concatenate([powers[v] for v in order], axis=0)).astype(jnp.bfloat16)
         hit = code_s[s, pl.ds(i, 1), :] == row24
         w = [jnp.where(hit, w_s[a, s, pl.ds(i, 1), :], 0.0) for a in range(3)]
         return g, jnp.concatenate(w, axis=0).astype(jnp.bfloat16)
 
     def couple(i, at, n):
-        both = [[factors(i + 8 * k, s) for s in range(n)] for k in range(2)]
-        g = jnp.concatenate([jnp.concatenate([f[0] for f in row], axis=1) for row in both], axis=0)
-        w = jnp.concatenate([jnp.concatenate([f[1] for f in row], axis=1) for row in both], axis=0)
-        r = lax.dot_general(w, g, (((1,), (1,)), ((), ())), preferred_element_type=jnp.float32)
-        left = lax.broadcasted_iota(jnp.int32, (72, 128), 1) < 64
-        res_s[pl.ds(pl.multiple_of(at * 72, 8), 72), :] = jnp.where(left, r[0:72], r[72:144])
+        both = []
+        for k in range(2):
+            parts = [factors(i + 8 * k, s) for s in range(n)]
+            g = jnp.concatenate([f[0] for f in parts], axis=1)
+            w = jnp.concatenate([f[1] for f in parts], axis=1)
+            both.append(lax.dot_general(w, g, (((1,), (1,)), ((), ())), preferred_element_type=jnp.float32))
+        res_s[pl.ds(pl.multiple_of(at * 72, 8), 72), :] = jnp.concatenate(both, axis=1)
 
     for n in range(1, slots + 1):
         @pl.when(live == n)
@@ -197,7 +219,7 @@
 
     def unfold(g, carry):
         i0 = g * 16
-        kt16 = jnp.broadcast_to(col_ref[0, pl.ds(pl.multiple_of(i0, 16), 16), 3:4], (16, 128))
+        kt16 = jnp.broadcast_to(col_s[pl.ds(pl.multiple_of(i0, 16), 16), 3:4], (16, 128))
         is_t = [kt16 == float(t) for t in range(3)]
         for a in range(3):
             d = []
@@ -231,10 +253,9 @@
         gram_tiles(me_ref, force_ref, rows_s, left_s, outs, plan)
 
 
-def design(off, mask, me, rows, kind, cols, force, plan, by_blocks, groups=2):
+def design(off, mask, me, strip, below, above, force, plan, groups=2):
     nb, slots = off.shape
-    beads = rows.shape[-1]
-    n_src = rows.shape[0]
+    x_rows, by_blocks, _, beads = strip.shape
     total = nb * 3 * beads
     share = (2, plan.pairs, plan.size_x, plan.slots, plan.part, HALF)
     return pl.pallas_call(
@@ -242,12 +263,8 @@
         grid_spec=pltpu.PrefetchScalarGridSpec(
             num_scalar_prefetch=3,
             grid=(nb,),
-            in_specs=[
-                pl.BlockSpec((n_src, 3, beads), lambda b, *_: (0, 0, 0)),
-                pl.BlockSpec((n_src, 1, beads), lambda b, *_: (0, 0, 0)),
-                pl.BlockSpec((1, beads, 4), lambda b, *_: (b, 0, 0)),
-                pl.BlockSpec((16, total), lambda b, *_: (0, 0)),
-            ],
+            in_specs=[pl.BlockSpec(strip.shape, lambda b, *_: (0, 0, 0, 0))] * 3
+            + [pl.BlockSpec((16, total), lambda b, *_: (0, 0))],
             out_specs=[pl.BlockSpec(share, lambda b, *_: (0,) * 6)] * CHUNKS,
             scratch_shapes=[
                 pltpu.VMEM((slots, beads, beads), jnp.float32),
@@ -257,12 +274,14 @@
                 pltpu.VMEM((beads // 2 * 72, 128), jnp.float32),
                 pltpu.VMEM((total, PAIRS * K), jnp.bfloat16),
                 pltpu.VMEM((K, total), jnp.bfloat16),
+                pltpu.VMEM((x_rows * (by_blocks + 2), 8, beads), jnp.float32),
+                pltpu.VMEM((beads, 8), jnp.float32),
                 pltpu.SMEM((slots + 1,), jnp.int32),
             ],
         ),
         out_shape=[jax.ShapeDtypeStruct(share, jnp.float32)] * CHUNKS,
         compiler_params=pltpu.CompilerParams(vmem_limit_bytes=56 * 1024 * 1024),
-    )(off, mask, me, rows, kind, cols, force)
+    )(off, mask, me, strip, below, above, force)
 
 
 def pack_kernel(me_ref, send_ref, parts_ref, own_ref, *msg_refs, plan, scale):
@@ -322,7 +341,13 @@
                 for v in range(1, HALF // plan.unit):
                     value = jnp.where(at == v * plan.unit, turned[v * plan.unit:(v + 1) * plan.unit], value)
                 gram_ref[cut] = value
-    rhs_ref[...] = full_s[rhs_at_ref[dev], 0:16, :]
+    for u in range(plan.rows // plan.unit):
+        at = dev * plan.rows + u * plan.unit
+        line = full_s[rhs_at_ref[dev], pl.ds(at // HALF, 1), :]
+        value = line[:, 0:plan.unit]
+        for v in range(1, HALF // plan.unit):
+            value = jnp.where(at % HALF == v * plan.unit, line[:, v * plan.unit:(v + 1) * plan.unit], value)
+        rhs_ref[:, u * plan.unit:(u + 1) * plan.unit] = value
 
 
 def place(me, mine, other, plan):
@@ -334,32 +359,21 @@
             in_specs=[pl.BlockSpec(mine.shape, lambda b, *_: (0, 0, 0))] * 2,
             out_specs=[
                 pl.BlockSpec((plan.rows, PAIRS * K), lambda b, *_: (0, 0)),
-                pl.BlockSpec((16, HALF), lambda b, *_: (0, 0)),
+                pl.BlockSpec((1, plan.rows), lambda b, *_: (0, 0)),
             ],
             scratch_shapes=[pltpu.VMEM((plan.entries, HALF, HALF), jnp.float32)],
         ),
         out_shape=[
             jax.ShapeDtypeStruct((plan.rows, PAIRS * K), jnp.float32),
-            jax.ShapeDtypeStruct((16, HALF), jnp.float32),
+            jax.ShapeDtypeStruct((1, plan.rows), jnp.float32),
         ],
         compiler_params=pltpu.CompilerParams(vmem_limit_bytes=32 * 1024 * 1024),
     )(me, jnp.asarray(plan.table), jnp.asarray(plan.rhs), mine, other)
 
 
-def extended(cells, sides, width):
-    for axis, dim in sides:
-        count = lax.axis_size(axis)
-        head = lax.slice_in_dim(cells, 0, width, axis=dim)
-        tail = lax.slice_in_dim(cells, cells.shape[dim] - width, cells.shape[dim], axis=dim)
-        cells = jnp.concatenate(
-            [
-                lax.ppermute(tail, axis, [(i, (i + 1) % count) for i in range(count)]),
-                cells,
-                lax.ppermute(head, axis, [((i + 1) % count, i) for i in range(count)]),
-            ],
-            axis=dim,
-        )
-    return cells
+def shifted(x, axis, step):
+    count = lax.axis_size(axis)
+    return lax.ppermute(x, axis, [(i, (i + step) % count) for i in range(count)])
 
 
 def swap(x, axis, flip):
@@ -387,28 +401,26 @@
     cells = jnp.concatenate(
         [jnp.transpose(coords[0], (1, 2, 0, 3)), kinds.astype(jnp.float32)[:, :, None, :]], axis=2
     )
-    around = extended(cells, (("gx", 0), ("gy", 1)), 1)
-    around = around.reshape((blocks_x + 2) * (blocks_y + 2), 4, beads)
-    cols = jnp.swapaxes(cells.reshape(nb, 4, beads), 1, 2)
+    left, right = shifted(cells, "gx", 1), shifted(cells, "gx", -1)
+    strip = jnp.concatenate([left[-1:], cells, right[:1]], axis=0)
+    below, above = shifted(strip, "gy", 1), shifted(strip, "gy", -1)
     force = jnp.transpose(forces[0], (1, 2, 0, 3)).reshape(1, nb * 3 * beads)
     chunks = design(
         tile_offsets.reshape(nb, slots),
         tile_mask.reshape(nb, slots),
         me,
-        around[:, :3],
-        around[:, 3:],
-        cols,
+        strip,
+        below,
+        above,
         jnp.broadcast_to(force, (16, nb * 3 * beads)),
         plan,
-        blocks_y,
     )
     parts = jnp.stack([summed(x, plan) for x in chunks])
     own, *messages = pack(me, parts, plan, 1.0 / frame_rows)
     got = [swap(m, "gy", 2 * k) for k, m in enumerate(messages, 1)]
     mine = jnp.concatenate([own] + got)
-    gram, lines = place(me, mine, swap(mine, "gy", 1), plan)
-    rhs = lax.dynamic_slice(lines.reshape(16 * HALF), (dev * plan.rows,), (plan.rows,))
-    return gram[None], rhs[None]
+    gram, rhs = place(me, mine, swap(mine, "gy", 1), plan)
+    return gram[None], rhs
 
 
 def solution(mesh):

time: 123 us -> 119 us (0.967); the launches traced: 121 us -> 120 us
  waiting for transfers between devices: 25 us -> 30.6 us
  starting transfers between devices: 41.4 us -> 36.6 us
  other arithmetic: 4.74 us -> 1.75 us
  Pallas kernels: 43.9 us -> 45.8 us
  local copies, waits for them, and re-layouts: 5.26 us -> 4.02 us
    ppermute x24, starting transfers between devices: 34.9 us -> 29.4 us  [swap(): lax.ppermute(x, axis, [(i, i ^ flip) for i in range(lax.axis_size(axis))])]
    ppermute x24, waiting for transfers between devices: 23.2 us -> 27.7 us  [swap(): lax.ppermute(x, axis, [(i, i ^ flip) for i in range(lax.axis_size(axis))])]
    pallas_call x1, Pallas kernels: 40 us -> 41.9 us  [design(): pl.pallas_call(functools.partial(design_kernel, plan=plan, by_blocks=by_b...]
    concatenate x2 -> x1, other arithmetic: 1.42 us -> 0.01 us  [shards(): strip = jnp.concatenate([left[-1:], cells, right[:1]], axis=0)]
  transfers between devices with their start and end apart: 28 -> 28, of which waited for: 14 -> 13; matrix products, arithmetic and copies ran while one was open for 3% -> 2% of each run, Pallas kernels for 0% -> 0%
where the time goes in v4:
time: 119 us; the launch traced here: 120 us
  Pallas kernels  45.8 us (38%)
  starting transfers between devices  36.6 us (31%)
  waiting for transfers between devices  30.6 us (26%)
  local copies, waits for them, and re-layouts  4.02 us (3%)
  other arithmetic  1.75 us (1%)
    pallas_call x1, Pallas kernels, design(): pl.pallas_call(functools.partial(design_kernel, plan=plan, by_blocks=by_b...  41.9 us
    ppermute x24, starting transfers between devices, swap(): lax.ppermute(x, axis, [(i, i ^ flip) for i in range(lax.axis_size(axis))])  29.4 us
    ppermute x24, waiting for transfers between devices, swap(): lax.ppermute(x, axis, [(i, i ^ flip) for i in range(lax.axis_size(axis))])  27.7 us
    ppermute x4, starting transfers between devices, shifted(): lax.ppermute(x, axis, [(i, (i + step) % count) for i in range(count)])  7.18 us
    pallas_call x1, Pallas kernels, place(): pl.pallas_call(functools.partial(place_kernel, plan=plan), grid_spec=pltp...  3.19 us
    ppermute x4, waiting for transfers between devices, shifted(): lax.ppermute(x, axis, [(i, (i + step) % count) for i in range(count)])  2.86 us
  transfers between devices with their start and end apart: 28, of which 13 were waited for; matrix products, arithmetic and copies ran while one was open for 2% of the time, Pallas kernels for 0%

profile of v4, /device:TPU:1, one launch (start us, length us, event | category | flops | bytes accessed | tf_op | source)
XLA Modules:
  0.0 119.6 jit_solution(17203812767526550589)
XLA Ops:
  0.6 0.7 copy.14
  1.3 0.7 convert_element_type.3
  2.0 2.2 %collective-permute-start = (f32[2,2,4,128]{3,2,1,0:T(4,128)S(1)}, f32[2,2,4,128]{3,2,1,0:T(4,128)S(1)}, u32[]{:S(2)}, u32[]{:S(2)}) collective-permute-start(f32[2,2,4,128]{3,2,1,0:T(4,128)S(1)} %pad_maximum_fusion.2), channel_id=1, source_target_pairs={{0,8},{8,16},{16,24},{24,0},{1,9},{9,17},{17,25},{25,1},{2,10},{10... | collective-permute-start | bytes 24584 | tf_op jit(solution)/shard_map/ppermute | solution.py:376
  4.2 2.1 %collective-permute-start.1 = (f32[2,2,4,128]{3,2,1,0:T(4,128)S(1)}, f32[2,2,4,128]{3,2,1,0:T(4,128)S(1)}, u32[]{:S(2)}, u32[]{:S(2)}) collective-permute-start(f32[2,2,4,128]{3,2,1,0:T(4,128)S(1)} %pad_maximum_fusion.2), channel_id=1, source_target_pairs={{0,24},{8,0},{16,8},{24,16},{1,25},{9,1},{17,9},{25,17},{2,26},{10... | collective-permute-start | bytes 24584 | tf_op jit(solution)/shard_map/ppermute | solution.py:376
  6.3 1.0 collective-permute-done
  7.3 0.0 collective-permute-done.1
  7.3 2.9 %collective-permute-start.2 = (f32[4,2,4,128]{3,2,1,0:T(4,128)S(1)}, f32[4,2,4,128]{3,2,1,0:T(4,128)S(1)}, u32[]{:S(2)}, u32[]{:S(2)}) collective-permute-start(f32[4,2,4,128]{3,2,1,0:T(4,128)S(1)} %pad_maximum_fusion.1.strip_ref), channel_id=1, source_target_pairs={{0,1},{1,2},{2,3},{3,4},{4,5},{5,6},{6,7},{7,0},{8,9},{9,10},{10,1... | collective-permute-start | bytes 49160 | tf_op jit(solution)/shard_map/ppermute | solution.py:376
  10.2 0.0 collective-permute-start.3
  10.2 0.6 pad_add_fusion.me_ref
  10.8 0.7 copy.12
  11.5 0.0 collective-permute-done.2.below_ref
  11.5 1.9 %collective-permute-done.3.above_ref = f32[4,2,4,128]{3,2,1,0:T(4,128)S(1)} collective-permute-done((f32[4,2,4,128]{3,2,1,0:T(4,128)S(1)}, f32[4,2,4,128]{3,2,1,0:T(4,128)S(1)}, u32[]{:S(2)}, u32[]{:S(2)}) %collective-permute-start.3) | collective-permute-done | bytes 16416 | tf_op jit(solution)/shard_map/ppermute | solution.py:376
  13.4 0.6 broadcast_in_dim.15.force_ref
  14.0 41.9 %shard_map.95 = (f32[2,4,4,7,16,128]{5,4,3,2,1,0:T(8,128)}, f32[2,4,4,7,16,128]{5,4,3,2,1,0:T(8,128)}) custom-call(s32[4,8]{1,0:T(4,128)} %bitcast.105, s32[4,8]{1,0:T(4,128)} %bitcast.106, s32[4]{0:T(128)} %pad_add_fusion.me_ref, f32[4,2,4,128]{3,2,1,0:T(4,128)} %copy-done.6, f32[4,2,4,128]{3,2,1,0:T(4,128)} %copy-done.7, f32[4,2,4,128]{3,2,1,0:T(4,128)} %copy-done.8, ...), custom_call_target="tpu_custom_call" | custom-call | tf_op jit(solution)/shard_map/pallas_call | solution.py:261
  55.9 1.4 %slice_bitcast_fusion.1 = f32[4,4,7,16,128]{4,3,2,1,0:T(8,128)S(1)} fusion(f32[2,4,4,7,16,128]{5,4,3,2,1,0:T(8,128)} %get-tuple-element.10), kind=kLoop, calls=%fused_computation.3 | loop fusion | bytes 1835008 | tf_op jit(solution)/shard_map/squeeze | solution.py:384
  57.3 0.1 collective-permute-start.4
  57.4 0.3 copy-done.4
  57.6 0.1 slice_bitcast_fusion
  57.7 0.3 collective-permute-start.14
  58.0 1.8 %collective-permute-done.4 = f32[4,4,7,16,128]{4,3,2,1,0:T(8,128)S(1)} collective-permute-done((f32[4,4,7,16,128]{4,3,2,1,0:T(8,128)S(1)}, f32[4,4,7,16,128]{4,3,2,1,0:T(8,128)S(1)}, u32[]{:S(2)}, u32[]{:S(2)}) %collective-permute-start.4) | collective-permute-done | bytes 917536 | tf_op jit(solution)/shard_map/ppermute | solution.py:380
  59.8 0.1 bitcast_add_fusion.1
  60.0 0.1 slice_bitcast_fusion.8
  60.0 0.4 collective-permute-start.5
  60.5 2.3 %collective-permute-start.7 = (f32[4,7,16,128]{3,2,1,0:T(8,128)S(1)}, f32[4,7,16,128]{3,2,1,0:T(8,128)S(1)}, u32[]{:S(2)}, u32[]{:S(2)}) collective-permute-start(f32[4,7,16,128]{3,2,1,0:T(8,128)S(1)} %get-tuple-element.19), channel_id=1, source_target_pairs={{0,6},{1,7},{2,4},{3,5},{4,2},{5,3},{6,0},{7,1},{8,14},{9,15},{10,... | collective-permute-start | bytes 688136 | tf_op jit(solution)/shard_map/ppermute | solution.py:380
  62.7 0.0 collective-permute-done.14
  62.7 0.1 bitcast_add_fusion
  62.9 0.4 collective-permute-start.15
  63.4 0.0 collective-permute-start.16
  63.4 3.8 %collective-permute-done.5 = f32[4,7,16,128]{3,2,1,0:T(8,128)S(1)} collective-permute-done((f32[4,7,16,128]{3,2,1,0:T(8,128)S(1)}, f32[4,7,16,128]{3,2,1,0:T(8,128)S(1)}, u32[]{:S(2)}, u32[]{:S(2)}) %collective-permute-start.5) | collective-permute-done | bytes 229408 | tf_op jit(solution)/shard_map/ppermute | solution.py:380
  67.2 5.0 %collective-permute-done.6 = f32[4,7,16,128]{3,2,1,0:T(8,128)S(1)} collective-permute-done((f32[4,7,16,128]{3,2,1,0:T(8,128)S(1)}, f32[4,7,16,128]{3,2,1,0:T(8,128)S(1)}, u32[]{:S(2)}, u32[]{:S(2)}) %collective-permute-start.6) | collective-permute-done | bytes 229408 | tf_op jit(solution)/shard_map/ppermute | solution.py:380
  72.1 0.0 collective-permute-done.7
  72.1 0.1 fusion.5
  72.2 3.7 %collective-permute-start.10 = (f32[7,16,128]{2,1,0:T(8,128)S(1)}, f32[7,16,128]{2,1,0:T(8,128)S(1)}, u32[]{:S(2)}, u32[]{:S(2)}) collective-permute-start(f32[7,16,128]{2,1,0:T(8,128)S(1)} %get-tuple-element.25), channel_id=1, source_target_pairs={{0,24},{8,16},{16,8},{24,0},{1,25},{9,17},{17,9},{25,1},{2,26},{10... | collective-permute-start | bytes 172040 | tf_op jit(solution)/shard_map/ppermute | solution.py:380
  76.0 1.1 collective-permute-done.15
  77.0 0.0 collective-permute-start.9
  77.1 4.9 %collective-permute-done.16 = f32[4,7,16,128]{3,2,1,0:T(8,128)S(1)} collective-permute-done((f32[4,7,16,128]{3,2,1,0:T(8,128)S(1)}, f32[4,7,16,128]{3,2,1,0:T(8,128)S(1)}, u32[]{:S(2)}, u32[]{:S(2)}) %collective-permute-start.16) | collective-permute-done | bytes 229408 | tf_op jit(solution)/shard_map/ppermute | solution.py:380
  82.0 0.1 fusion.2
  82.1 2.6 %collective-permute-start.18 = (f32[7,16,128]{2,1,0:T(8,128)S(1)}, f32[7,16,128]{2,1,0:T(8,128)S(1)}, u32[]{:S(2)}, u32[]{:S(2)}) collective-permute-start(f32[7,16,128]{2,1,0:T(8,128)S(1)} %get-tuple-element.27), channel_id=1, source_target_pairs={{0,8},{8,0},{16,24},{24,16},{1,9},{9,1},{17,25},{25,17},{2,10},{10... | collective-permute-start | bytes 172040 | tf_op jit(solution)/shard_map/ppermute | solution.py:380
  84.7 1.4 %collective-permute-start.19 = (f32[7,16,128]{2,1,0:T(8,128)S(1)}, f32[7,16,128]{2,1,0:T(8,128)S(1)}, u32[]{:S(2)}, u32[]{:S(2)}) collective-permute-start(f32[7,16,128]{2,1,0:T(8,128)S(1)} %get-tuple-element.29), channel_id=1, source_target_pairs={{0,16},{8,24},{16,0},{24,8},{1,17},{9,25},{17,1},{25,9},{2,18},{10... | collective-permute-start | bytes 172040 | tf_op jit(solution)/shard_map/ppermute | solution.py:380
  86.1 0.8 collective-permute-start.20
  86.8 0.0 collective-permute-done.8
  86.8 0.0 collective-permute-done.9
  86.9 0.6 collective-permute-start.11
  87.4 2.3 %collective-permute-start.12 = (f32[7,16,128]{2,1,0:T(8,128)S(1)}, f32[7,16,128]{2,1,0:T(8,128)S(1)}, u32[]{:S(2)}, u32[]{:S(2)}) collective-permute-start(f32[7,16,128]{2,1,0:T(8,128)S(1)} %fusion.11), channel_id=1, source_target_pairs={{0,16},{8,24},{16,0},{24,8},{1,17},{9,25},{17,1},{25,9},{2,18},{10... | collective-permute-start | bytes 172040 | tf_op jit(solution)/shard_map/ppermute | solution.py:380
  89.7 0.0 collective-permute-done.18
  89.7 0.8 collective-permute-start.13
  90.5 0.4 collective-permute-done.20
  90.9 0.6 collective-permute-start.21
  91.5 1.8 %collective-permute-start.22 = (f32[7,16,128]{2,1,0:T(8,128)S(1)}, f32[7,16,128]{2,1,0:T(8,128)S(1)}, u32[]{:S(2)}, u32[]{:S(2)}) collective-permute-start(f32[7,16,128]{2,1,0:T(8,128)S(1)} %fusion.8), channel_id=1, source_target_pairs={{0,16},{8,24},{16,0},{24,8},{1,17},{9,25},{17,1},{25,9},{2,18},{10... | collective-permute-start | bytes 172040 | tf_op jit(solution)/shard_map/ppermute | solution.py:380
  93.4 0.0 collective-permute-done.11
  93.4 1.2 collective-permute-start.23
  94.6 0.0 collective-permute-done.12
  94.6 0.5 collective-permute-done.13
  95.1 0.0 collective-permute-done.21
  95.1 4.0 %collective-permute-done.22 = f32[7,16,128]{2,1,0:T(8,128)S(1)} collective-permute-done((f32[7,16,128]{2,1,0:T(8,128)S(1)}, f32[7,16,128]{2,1,0:T(8,128)S(1)}, u32[]{:S(2)}, u32[]{:S(2)}) %collective-permute-start.22) | collective-permute-done | bytes 57376 | tf_op jit(solution)/shard_map/ppermute | solution.py:380
  99.3 0.8 shard_map.96
  100.0 1.2 %collective-permute-start.24 = (f32[6,64,128]{2,1,0:T(8,128)S(1)}, f32[6,64,128]{2,1,0:T(8,128)S(1)}, u32[]{:S(2)}, u32[]{:S(2)}) collective-permute-start(f32[6,64,128]{2,1,0:T(8,128)S(1)} %get-tuple-element.13), channel_id=1, source_target_pairs={{0,2},{1,3},{2,0},{3,1},{4,6},{5,7},{6,4},{7,5},{8,10},{9,11},{10,... | collective-permute-start | bytes 589832 | tf_op jit(solution)/shard_map/ppermute | solution.py:380
  101.2 0.3 collective-permute-start.25
  101.5 1.2 %collective-permute-start.26 = (f32[3,64,128]{2,1,0:T(8,128)S(1)}, f32[3,64,128]{2,1,0:T(8,128)S(1)}, u32[]{:S(2)}, u32[]{:S(2)}) collective-permute-start(f32[3,64,128]{2,1,0:T(8,128)S(1)} %get-tuple-element.15), channel_id=1, source_target_pairs={{0,6},{1,7},{2,4},{3,5},{4,2},{5,3},{6,0},{7,1},{8,14},{9,15},{10,... | collective-permute-start | bytes 294920 | tf_op jit(solution)/shard_map/ppermute | solution.py:380
  102.8 1.8 %collective-permute-done.24 = f32[6,64,128]{2,1,0:T(8,128)S(1)} collective-permute-done((f32[6,64,128]{2,1,0:T(8,128)S(1)}, f32[6,64,128]{2,1,0:T(8,128)S(1)}, u32[]{:S(2)}, u32[]{:S(2)}) %collective-permute-start.24) | collective-permute-done | bytes 196640 | tf_op jit(solution)/shard_map/ppermute | solution.py:380
  104.6 2.2 %collective-permute-done.25 = f32[6,64,128]{2,1,0:T(8,128)S(1)} collective-permute-done((f32[6,64,128]{2,1,0:T(8,128)S(1)}, f32[6,64,128]{2,1,0:T(8,128)S(1)}, u32[]{:S(2)}, u32[]{:S(2)}) %collective-permute-start.25) | collective-permute-done | bytes 196640 | tf_op jit(solution)/shard_map/ppermute | solution.py:380
  106.9 7.4 %collective-permute-start.27 = (f32[29,64,128]{2,1,0:T(8,128)S(1)}, f32[29,64,128]{2,1,0:T(8,128)S(1)}, u32[]{:S(2)}, u32[]{:S(2)}) collective-permute-start(f32[29,64,128]{2,1,0:T(8,128)S(1)} %constant_dynamic-update-slice_fusion.mine_ref), channel_id=1, source_target_pairs={{0,1},{1,0},{2,3},{3,2},{4,5},{5,4},{6,7},{7,6},{8,9},{9,8},{10,11... | collective-permute-start | bytes 2850824 | tf_op jit(solution)/shard_map/ppermute | solution.py:380
  114.3 2.1 %collective-permute-done.27.other_ref = f32[29,64,128]{2,1,0:T(8,128)S(1)} collective-permute-done((f32[29,64,128]{2,1,0:T(8,128)S(1)}, f32[29,64,128]{2,1,0:T(8,128)S(1)}, u32[]{:S(2)}, u32[]{:S(2)}) %collective-permute-start.27) | collective-permute-done | bytes 950304 | tf_op jit(solution)/shard_map/ppermute | solution.py:380
  116.4 3.2 %shard_map.97 = (f32[192,1536]{1,0:T(8,128)}, f32[1,192]{1,0:T(1,128)}) custom-call(s32[4]{0:T(128)S(1)} %copy-done, s32[8,36]{1,0:T(8,128)S(1)} %copy-done.1, s32[8]{0:T(128)S(1)} %copy-done.3, f32[29,64,128]{2,1,0:T(8,128)S(1)} %constant_dynamic-update-slice_fusion.mine_ref, f32[29,64,128]{2,1,0:T(8,128)S(1)} %collective-permute-done.27.other_ref), custom_call_target="tpu_custom_call" | custom-call | tf_op jit(solution)/shard_map/pallas_call | solution.py:354
  (42 shorter events, 0.3 us)
Async XLA Ops:
  2.0 5.2 %collective-permute-start = (f32[2,2,4,128]{3,2,1,0:T(4,128)S(1)}, f32[2,2,4,128]{3,2,1,0:T(4,128)S(1)}, u32[]{:S(2)}, u32[]{:S(2)}) collective-permute-start(f32[2,2,4,128]{3,2,1,0:T(4,128)S(1)} %pad_maximum_fusion.2), channel_id=1, source_target_pairs={{0,8},{8,16},{16,24},{24,0},{1,9},{9,17},{17,25},{25,1},{2,10},{10... | collective-permute-start | bytes 24584 | tf_op jit(solution)/shard_map/ppermute | solution.py:376
  4.2 3.1 %collective-permute-start.1 = (f32[2,2,4,128]{3,2,1,0:T(4,128)S(1)}, f32[2,2,4,128]{3,2,1,0:T(4,128)S(1)}, u32[]{:S(2)}, u32[]{:S(2)}) collective-permute-start(f32[2,2,4,128]{3,2,1,0:T(4,128)S(1)} %pad_maximum_fusion.2), channel_id=1, source_target_pairs={{0,24},{8,0},{16,8},{24,16},{1,25},{9,1},{17,9},{25,17},{2,26},{10... | collective-permute-start | bytes 24584 | tf_op jit(solution)/shard_map/ppermute | solution.py:376
  7.3 6.7 %copy-start.6 = (f32[4,2,4,128]{3,2,1,0:T(4,128)}, f32[4,2,4,128]{3,2,1,0:T(4,128)S(1)}, u32[]{:S(2)}) copy-start(f32[4,2,4,128]{3,2,1,0:T(4,128)S(1)} %pad_maximum_fusion.1.strip_ref) | copy-start | bytes 49156
  7.3 4.2 %collective-permute-start.2 = (f32[4,2,4,128]{3,2,1,0:T(4,128)S(1)}, f32[4,2,4,128]{3,2,1,0:T(4,128)S(1)}, u32[]{:S(2)}, u32[]{:S(2)}) collective-permute-start(f32[4,2,4,128]{3,2,1,0:T(4,128)S(1)} %pad_maximum_fusion.1.strip_ref), channel_id=1, source_target_pairs={{0,1},{1,2},{2,3},{3,4},{4,5},{5,6},{6,7},{7,0},{8,9},{9,10},{10,1... | collective-permute-start | bytes 49160 | tf_op jit(solution)/shard_map/ppermute | solution.py:376
  10.2 3.2 %collective-permute-start.3 = (f32[4,2,4,128]{3,2,1,0:T(4,128)S(1)}, f32[4,2,4,128]{3,2,1,0:T(4,128)S(1)}, u32[]{:S(2)}, u32[]{:S(2)}) collective-permute-start(f32[4,2,4,128]{3,2,1,0:T(4,128)S(1)} %pad_maximum_fusion.1.strip_ref), channel_id=1, source_target_pairs={{0,7},{1,0},{2,1},{3,2},{4,3},{5,4},{6,5},{7,6},{8,15},{9,8},{10,9... | collective-permute-start | bytes 49160 | tf_op jit(solution)/shard_map/ppermute | solution.py:376
  11.5 2.5 %copy-start.7 = (f32[4,2,4,128]{3,2,1,0:T(4,128)}, f32[4,2,4,128]{3,2,1,0:T(4,128)S(1)}, u32[]{:S(2)}) copy-start(f32[4,2,4,128]{3,2,1,0:T(4,128)S(1)} %collective-permute-done.2.below_ref) | copy-start | bytes 49156
  13.4 0.6 copy-start.8
  55.9 1.8 %copy-start.4 = (f32[2,4,4,7,16,128]{5,4,3,2,1,0:T(8,128)S(1)}, f32[2,4,4,7,16,128]{5,4,3,2,1,0:T(8,128)}, u32[]{:S(2)}) copy-start(f32[2,4,4,7,16,128]{5,4,3,2,1,0:T(8,128)} %get-tuple-element.11) | copy-start | bytes 5505028
  55.9 4.0 %copy-start.5 = (f32[2,4,4,7,16,128]{5,4,3,2,1,0:T(8,128)S(1)}, f32[2,4,4,7,16,128]{5,4,3,2,1,0:T(8,128)}, u32[]{:S(2)}) copy-start(f32[2,4,4,7,16,128]{5,4,3,2,1,0:T(8,128)} %get-tuple-element.10) | copy-start | bytes 5505028
  57.3 2.5 %collective-permute-start.4 = (f32[4,4,7,16,128]{4,3,2,1,0:T(8,128)S(1)}, f32[4,4,7,16,128]{4,3,2,1,0:T(8,128)S(1)}, u32[]{:S(2)}, u32[]{:S(2)}) collective-permute-start(f32[4,4,7,16,128]{4,3,2,1,0:T(8,128)S(1)} %slice_bitcast_fusion.1), channel_id=1, source_target_pairs={{0,1},{1,0},{2,3},{3,2},{4,5},{5,4},{6,7},{7,6},{8,9},{9,8},{10,11... | collective-permute-start | bytes 2752520 | tf_op jit(solution)/shard_map/ppermute | solution.py:380
  57.7 5.0 %collective-permute-start.14 = (f32[4,4,7,16,128]{4,3,2,1,0:T(8,128)S(1)}, f32[4,4,7,16,128]{4,3,2,1,0:T(8,128)S(1)}, u32[]{:S(2)}, u32[]{:S(2)}) collective-permute-start(f32[4,4,7,16,128]{4,3,2,1,0:T(8,128)S(1)} %slice_bitcast_fusion), channel_id=1, source_target_pairs={{0,1},{1,0},{2,3},{3,2},{4,5},{5,4},{6,7},{7,6},{8,9},{9,8},{10,11... | collective-permute-start | bytes 2752520 | tf_op jit(solution)/shard_map/ppermute | solution.py:380
  60.0 7.1 %collective-permute-start.5 = (f32[4,7,16,128]{3,2,1,0:T(8,128)S(1)}, f32[4,7,16,128]{3,2,1,0:T(8,128)S(1)}, u32[]{:S(2)}, u32[]{:S(2)}) collective-permute-start(f32[4,7,16,128]{3,2,1,0:T(8,128)S(1)} %get-tuple-element.18), channel_id=1, source_target_pairs={{0,2},{1,3},{2,0},{3,1},{4,6},{5,7},{6,4},{7,5},{8,10},{9,11},{10,... | collective-permute-start | bytes 688136 | tf_op jit(solution)/shard_map/ppermute | solution.py:380
  60.5 11.7 %collective-permute-start.6 = (f32[4,7,16,128]{3,2,1,0:T(8,128)S(1)}, f32[4,7,16,128]{3,2,1,0:T(8,128)S(1)}, u32[]{:S(2)}, u32[]{:S(2)}) collective-permute-start(f32[4,7,16,128]{3,2,1,0:T(8,128)S(1)} %get-tuple-element.20), channel_id=1, source_target_pairs={{0,4},{1,5},{2,6},{3,7},{4,0},{5,1},{6,2},{7,3},{8,12},{9,13},{10,... | collective-permute-start | bytes 688136 | tf_op jit(solution)/shard_map/ppermute | solution.py:380
  60.5 11.7 %collective-permute-start.7 = (f32[4,7,16,128]{3,2,1,0:T(8,128)S(1)}, f32[4,7,16,128]{3,2,1,0:T(8,128)S(1)}, u32[]{:S(2)}, u32[]{:S(2)}) collective-permute-start(f32[4,7,16,128]{3,2,1,0:T(8,128)S(1)} %get-tuple-element.19), channel_id=1, source_target_pairs={{0,6},{1,7},{2,4},{3,5},{4,2},{5,3},{6,0},{7,1},{8,14},{9,15},{10,... | collective-permute-start | bytes 688136 | tf_op jit(solution)/shard_map/ppermute | solution.py:380
  62.9 14.1 %collective-permute-start.15 = (f32[4,7,16,128]{3,2,1,0:T(8,128)S(1)}, f32[4,7,16,128]{3,2,1,0:T(8,128)S(1)}, u32[]{:S(2)}, u32[]{:S(2)}) collective-permute-start(f32[4,7,16,128]{3,2,1,0:T(8,128)S(1)} %get-tuple-element.21), channel_id=1, source_target_pairs={{0,2},{1,3},{2,0},{3,1},{4,6},{5,7},{6,4},{7,5},{8,10},{9,11},{10,... | collective-permute-start | bytes 688136 | tf_op jit(solution)/shard_map/ppermute | solution.py:380
  63.4 18.6 %collective-permute-start.16 = (f32[4,7,16,128]{3,2,1,0:T(8,128)S(1)}, f32[4,7,16,128]{3,2,1,0:T(8,128)S(1)}, u32[]{:S(2)}, u32[]{:S(2)}) collective-permute-start(f32[4,7,16,128]{3,2,1,0:T(8,128)S(1)} %get-tuple-element.23), channel_id=1, source_target_pairs={{0,4},{1,5},{2,6},{3,7},{4,0},{5,1},{6,2},{7,3},{8,12},{9,13},{10,... | collective-permute-start | bytes 688136 | tf_op jit(solution)/shard_map/ppermute | solution.py:380
  67.2 14.8 %collective-permute-start.17 = (f32[4,7,16,128]{3,2,1,0:T(8,128)S(1)}, f32[4,7,16,128]{3,2,1,0:T(8,128)S(1)}, u32[]{:S(2)}, u32[]{:S(2)}) collective-permute-start(f32[4,7,16,128]{3,2,1,0:T(8,128)S(1)} %get-tuple-element.22), channel_id=1, source_target_pairs={{0,6},{1,7},{2,4},{3,5},{4,2},{5,3},{6,0},{7,1},{8,14},{9,15},{10,... | collective-permute-start | bytes 688136 | tf_op jit(solution)/shard_map/ppermute | solution.py:380
  72.2 13.9 %collective-permute-start.10 = (f32[7,16,128]{2,1,0:T(8,128)S(1)}, f32[7,16,128]{2,1,0:T(8,128)S(1)}, u32[]{:S(2)}, u32[]{:S(2)}) collective-permute-start(f32[7,16,128]{2,1,0:T(8,128)S(1)} %get-tuple-element.25), channel_id=1, source_target_pairs={{0,24},{8,16},{16,8},{24,0},{1,25},{9,17},{17,9},{25,1},{2,26},{10... | collective-permute-start | bytes 172040 | tf_op jit(solution)/shard_map/ppermute | solution.py:380
  76.0 10.9 %collective-permute-start.8 = (f32[7,16,128]{2,1,0:T(8,128)S(1)}, f32[7,16,128]{2,1,0:T(8,128)S(1)}, u32[]{:S(2)}, u32[]{:S(2)}) collective-permute-start(f32[7,16,128]{2,1,0:T(8,128)S(1)} %get-tuple-element.24), channel_id=1, source_target_pairs={{0,8},{8,0},{16,24},{24,16},{1,9},{9,1},{17,25},{25,17},{2,10},{10... | collective-permute-start | bytes 172040 | tf_op jit(solution)/shard_map/ppermute | solution.py:380
  77.0 22.2 %copy-start = (s32[4]{0:T(128)S(1)}, s32[4]{0:T(128)}, u32[]{:S(2)}) copy-start(s32[4]{0:T(128)} %pad_add_fusion.me_ref) | copy-start | bytes 52
  77.0 22.2 %copy-start.2 = (s32[4,15]{1,0:T(4,128)S(1)}, s32[4,15]{1,0:T(4,128)}, u32[]{:S(2)}) copy-start(s32[4,15]{1,0:T(4,128)} %constant.38.clone.send_ref) | copy-start | bytes 724
  77.0 9.8 %collective-permute-start.9 = (f32[7,16,128]{2,1,0:T(8,128)S(1)}, f32[7,16,128]{2,1,0:T(8,128)S(1)}, u32[]{:S(2)}, u32[]{:S(2)}) collective-permute-start(f32[7,16,128]{2,1,0:T(8,128)S(1)} %get-tuple-element.26), channel_id=1, source_target_pairs={{0,16},{8,24},{16,0},{24,8},{1,17},{9,25},{17,1},{25,9},{2,18},{10... | collective-permute-start | bytes 172040 | tf_op jit(solution)/shard_map/ppermute | solution.py:380
  82.1 7.7 %collective-permute-start.18 = (f32[7,16,128]{2,1,0:T(8,128)S(1)}, f32[7,16,128]{2,1,0:T(8,128)S(1)}, u32[]{:S(2)}, u32[]{:S(2)}) collective-permute-start(f32[7,16,128]{2,1,0:T(8,128)S(1)} %get-tuple-element.27), channel_id=1, source_target_pairs={{0,8},{8,0},{16,24},{24,16},{1,9},{9,1},{17,25},{25,17},{2,10},{10... | collective-permute-start | bytes 172040 | tf_op jit(solution)/shard_map/ppermute | solution.py:380
  84.7 5.8 %collective-permute-start.19 = (f32[7,16,128]{2,1,0:T(8,128)S(1)}, f32[7,16,128]{2,1,0:T(8,128)S(1)}, u32[]{:S(2)}, u32[]{:S(2)}) collective-permute-start(f32[7,16,128]{2,1,0:T(8,128)S(1)} %get-tuple-element.29), channel_id=1, source_target_pairs={{0,16},{8,24},{16,0},{24,8},{1,17},{9,25},{17,1},{25,9},{2,18},{10... | collective-permute-start | bytes 172040 | tf_op jit(solution)/shard_map/ppermute | solution.py:380
  86.1 4.8 %collective-permute-start.20 = (f32[7,16,128]{2,1,0:T(8,128)S(1)}, f32[7,16,128]{2,1,0:T(8,128)S(1)}, u32[]{:S(2)}, u32[]{:S(2)}) collective-permute-start(f32[7,16,128]{2,1,0:T(8,128)S(1)} %get-tuple-element.28), channel_id=1, source_target_pairs={{0,24},{8,16},{16,8},{24,0},{1,25},{9,17},{17,9},{25,1},{2,26},{10... | collective-permute-start | bytes 172040 | tf_op jit(solution)/shard_map/ppermute | solution.py:380
  86.9 6.5 %collective-permute-start.11 = (f32[7,16,128]{2,1,0:T(8,128)S(1)}, f32[7,16,128]{2,1,0:T(8,128)S(1)}, u32[]{:S(2)}, u32[]{:S(2)}) collective-permute-start(f32[7,16,128]{2,1,0:T(8,128)S(1)} %fusion.11), channel_id=1, source_target_pairs={{0,8},{8,0},{16,24},{24,16},{1,9},{9,1},{17,25},{25,17},{2,10},{10... | collective-permute-start | bytes 172040 | tf_op jit(solution)/shard_map/ppermute | solution.py:380
  87.4 7.1 %collective-permute-start.12 = (f32[7,16,128]{2,1,0:T(8,128)S(1)}, f32[7,16,128]{2,1,0:T(8,128)S(1)}, u32[]{:S(2)}, u32[]{:S(2)}) collective-permute-start(f32[7,16,128]{2,1,0:T(8,128)S(1)} %fusion.11), channel_id=1, source_target_pairs={{0,16},{8,24},{16,0},{24,8},{1,17},{9,25},{17,1},{25,9},{2,18},{10... | collective-permute-start | bytes 172040 | tf_op jit(solution)/shard_map/ppermute | solution.py:380
  89.7 5.4 %collective-permute-start.13 = (f32[7,16,128]{2,1,0:T(8,128)S(1)}, f32[7,16,128]{2,1,0:T(8,128)S(1)}, u32[]{:S(2)}, u32[]{:S(2)}) collective-permute-start(f32[7,16,128]{2,1,0:T(8,128)S(1)} %fusion.11), channel_id=1, source_target_pairs={{0,24},{8,16},{16,8},{24,0},{1,25},{9,17},{17,9},{25,1},{2,26},{10... | collective-permute-start | bytes 172040 | tf_op jit(solution)/shard_map/ppermute | solution.py:380
  90.9 4.2 %collective-permute-start.21 = (f32[7,16,128]{2,1,0:T(8,128)S(1)}, f32[7,16,128]{2,1,0:T(8,128)S(1)}, u32[]{:S(2)}, u32[]{:S(2)}) collective-permute-start(f32[7,16,128]{2,1,0:T(8,128)S(1)} %fusion.8), channel_id=1, source_target_pairs={{0,8},{8,0},{16,24},{24,16},{1,9},{9,1},{17,25},{25,17},{2,10},{10... | collective-permute-start | bytes 172040 | tf_op jit(solution)/shard_map/ppermute | solution.py:380
  91.5 7.6 %collective-permute-start.22 = (f32[7,16,128]{2,1,0:T(8,128)S(1)}, f32[7,16,128]{2,1,0:T(8,128)S(1)}, u32[]{:S(2)}, u32[]{:S(2)}) collective-permute-start(f32[7,16,128]{2,1,0:T(8,128)S(1)} %fusion.8), channel_id=1, source_target_pairs={{0,16},{8,24},{16,0},{24,8},{1,17},{9,25},{17,1},{25,9},{2,18},{10... | collective-permute-start | bytes 172040 | tf_op jit(solution)/shard_map/ppermute | solution.py:380
  93.4 5.8 %collective-permute-start.23 = (f32[7,16,128]{2,1,0:T(8,128)S(1)}, f32[7,16,128]{2,1,0:T(8,128)S(1)}, u32[]{:S(2)}, u32[]{:S(2)}) collective-permute-start(f32[7,16,128]{2,1,0:T(8,128)S(1)} %fusion.8), channel_id=1, source_target_pairs={{0,24},{8,16},{16,8},{24,0},{1,25},{9,17},{17,9},{25,1},{2,26},{10... | collective-permute-start | bytes 172040 | tf_op jit(solution)/shard_map/ppermute | solution.py:380
  99.2 17.2 %copy-start.1 = (s32[8,36]{1,0:T(8,128)S(1)}, s32[8,36]{1,0:T(8,128)}, u32[]{:S(2)}) copy-start(s32[8,36]{1,0:T(8,128)} %constant.39.clone.table_ref) | copy-start | bytes 3460
  99.2 17.2 %copy-start.3 = (s32[8]{0:T(128)S(1)}, s32[8]{0:T(128)}, u32[]{:S(2)}) copy-start(s32[8]{0:T(128)} %constant.40.clone.rhs_at_ref) | copy-start | bytes 100
  100.0 4.6 %collective-permute-start.24 = (f32[6,64,128]{2,1,0:T(8,128)S(1)}, f32[6,64,128]{2,1,0:T(8,128)S(1)}, u32[]{:S(2)}, u32[]{:S(2)}) collective-permute-start(f32[6,64,128]{2,1,0:T(8,128)S(1)} %get-tuple-element.13), channel_id=1, source_target_pairs={{0,2},{1,3},{2,0},{3,1},{4,6},{5,7},{6,4},{7,5},{8,10},{9,11},{10,... | collective-permute-start | bytes 589832 | tf_op jit(solution)/shard_map/ppermute | solution.py:380
  101.2 5.6 %collective-permute-start.25 = (f32[6,64,128]{2,1,0:T(8,128)S(1)}, f32[6,64,128]{2,1,0:T(8,128)S(1)}, u32[]{:S(2)}, u32[]{:S(2)}) collective-permute-start(f32[6,64,128]{2,1,0:T(8,128)S(1)} %get-tuple-element.14), channel_id=1, source_target_pairs={{0,4},{1,5},{2,6},{3,7},{4,0},{5,1},{6,2},{7,3},{8,12},{9,13},{10,... | collective-permute-start | bytes 589832 | tf_op jit(solution)/shard_map/ppermute | solution.py:380
  101.5 5.3 %collective-permute-start.26 = (f32[3,64,128]{2,1,0:T(8,128)S(1)}, f32[3,64,128]{2,1,0:T(8,128)S(1)}, u32[]{:S(2)}, u32[]{:S(2)}) collective-permute-start(f32[3,64,128]{2,1,0:T(8,128)S(1)} %get-tuple-element.15), channel_id=1, source_target_pairs={{0,6},{1,7},{2,4},{3,5},{4,2},{5,3},{6,0},{7,1},{8,14},{9,15},{10,... | collective-permute-start | bytes 294920 | tf_op jit(solution)/shard_map/ppermute | solution.py:380
  106.9 9.5 %collective-permute-start.27 = (f32[29,64,128]{2,1,0:T(8,128)S(1)}, f32[29,64,128]{2,1,0:T(8,128)S(1)}, u32[]{:S(2)}, u32[]{:S(2)}) collective-permute-start(f32[29,64,128]{2,1,0:T(8,128)S(1)} %constant_dynamic-update-slice_fusion.mine_ref), channel_id=1, source_target_pairs={{0,1},{1,0},{2,3},{3,2},{4,5},{5,4},{6,7},{7,6},{8,9},{9,8},{10,11... | collective-permute-start | bytes 2850824 | tf_op jit(solution)/shard_map/ppermute | solution.py:380

commit v5 on v4

--- a/solution.py
+++ b/solution.py
@@ -87,23 +87,22 @@
                         self.table[d, u * TILES + c] = -1
 
 
-def gram_tiles(me_ref, force_ref, rows_s, left_s, outs, plan):
+def gram_tiles(me_ref, force_ref, rows_s, left_s, upper, lower, plan):
     def put(tile, value):
         g, s = plan.place[tile]
-        out = outs[s // plan.slots]
         for h in range(2):
             for z in range(plan.size_x):
                 at = h * HALF // 2 + z * plan.part
-                out[h ^ me_ref[0], g ^ me_ref[1], z ^ me_ref[2], s % plan.slots] = value[at:at + plan.part]
+                out = (upper, lower)[h][s // plan.slots]
+                out[g ^ me_ref[1], z ^ me_ref[2], s % plan.slots] = value[at:at + plan.part]
 
     used = {(g, s) for g, s in plan.place.values()}
     for g in range(plan.pairs):
         for s in range(plan.room):
             if (g, s) not in used:
-                plan_tile = jnp.zeros((plan.part, HALF), jnp.float32)
-                for h in range(2):
+                for out in (upper, lower):
                     for z in range(plan.size_x):
-                        outs[s // plan.slots][h ^ me_ref[0], g ^ me_ref[1], z ^ me_ref[2], s % plan.slots] = plan_tile
+                        out[s // plan.slots][g ^ me_ref[1], z ^ me_ref[2], s % plan.slots] = jnp.zeros((plan.part, HALF), jnp.float32)
     for p in range(PAIRS):
         left_s[...] = rows_s[:, p * K:(p + 1) * K].T
         for q in range(p, PAIRS):
@@ -120,8 +119,8 @@
 
 
 def design_kernel(off_ref, mask_ref, me_ref, strip_ref, below_ref, above_ref, force_ref, *refs, plan, by_blocks, beads, slots, groups):
-    outs = refs[:CHUNKS]
-    pos_s, lt_s, code_s, w_s, res_s, rows_s, left_s, near_s, col_s, list_s = refs[CHUNKS:]
+    outs = refs[:2 * CHUNKS]
+    pos_s, lt_s, code_s, w_s, res_s, rows_s, left_s, near_s, col_s, list_s = refs[2 * CHUNKS:]
     b = pl.program_id(0)
     bx = b // by_blocks
     by = b % by_blocks
@@ -202,22 +201,9 @@
             both.append(lax.dot_general(w, g, (((1,), (1,)), ((), ())), preferred_element_type=jnp.float32))
         res_s[pl.ds(pl.multiple_of(at * 72, 8), 72), :] = jnp.concatenate(both, axis=1)
 
-    for n in range(1, slots + 1):
-        @pl.when(live == n)
-        def _(n=n):
-            def body(g, carry):
-                for q in range(8 * groups):
-                    couple((g * groups + q // 8) * 16 + q % 8, (g * groups + q // 8) * 8 + q % 8, n)
-                return carry
-            lax.fori_loop(0, beads // (16 * groups), body, 0)
-
-    @pl.when(live == 0)
-    def _():
-        res_s[...] = jnp.zeros_like(res_s)
-
     cut = lane % 64
 
-    def unfold(g, carry):
+    def unfold(g):
         i0 = g * 16
         kt16 = jnp.broadcast_to(col_s[pl.ds(pl.multiple_of(i0, 16), 16), 3:4], (16, 128))
         is_t = [kt16 == float(t) for t in range(3)]
@@ -245,19 +231,38 @@
                     if lo_t != hi_t:
                         x = jnp.where(is_t[hi_t], d[lo_t][v], x)
                     rows_s[pl.ds(pl.multiple_of((b * 3 + a) * beads + i0, 16), 16), p * K + v * 128:p * K + (v + 1) * 128] = x.astype(jnp.bfloat16)
-        return carry
-    lax.fori_loop(0, beads // 16, unfold, 0)
+    for n in range(1, slots + 1):
+        @pl.when(live == n)
+        def _(n=n):
+            step = groups if n > slots // 2 else 1
+
+            def body(g, carry):
+                for q in range(step):
+                    for k in range(8):
+                        couple((g * step + q) * 16 + k, (g * step + q) * 8 + k, n)
+                    if q > 0:
+                        unfold(g * step + q - 1)
+                unfold(g * step + step - 1)
+                return carry
+            lax.fori_loop(0, beads // (16 * step), body, 0)
+
+    @pl.when(live == 0)
+    def _():
+        rows_s[pl.ds(pl.multiple_of(b * 3 * beads, 16), 3 * beads), :] = jnp.zeros((3 * beads, PAIRS * K), jnp.bfloat16)
 
     @pl.when(b == pl.num_programs(0) - 1)
     def _():
-        gram_tiles(me_ref, force_ref, rows_s, left_s, outs, plan)
-
-
-def design(off, mask, me, strip, below, above, force, plan, groups=2):
+        for core in range(2):
+            @pl.when(me_ref[0] == core)
+            def _(core=core):
+                gram_tiles(me_ref, force_ref, rows_s, left_s, outs[core::2], outs[1 - core::2], plan)
+
+
+def design(off, mask, me, strip, below, above, force, plan, groups=4):
     nb, slots = off.shape
     x_rows, by_blocks, _, beads = strip.shape
     total = nb * 3 * beads
-    share = (2, plan.pairs, plan.size_x, plan.slots, plan.part, HALF)
+    share = (plan.pairs, plan.size_x, plan.slots, plan.part, HALF)
     return pl.pallas_call(
         functools.partial(design_kernel, plan=plan, by_blocks=by_blocks, beads=beads, slots=slots, groups=groups),
         grid_spec=pltpu.PrefetchScalarGridSpec(
@@ -265,7 +270,7 @@
             grid=(nb,),
             in_specs=[pl.BlockSpec(strip.shape, lambda b, *_: (0, 0, 0, 0))] * 3
             + [pl.BlockSpec((16, total), lambda b, *_: (0, 0))],
-            out_specs=[pl.BlockSpec(share, lambda b, *_: (0,) * 6)] * CHUNKS,
+            out_specs=[pl.BlockSpec(share, lambda b, *_: (0,) * 5)] * (2 * CHUNKS),
             scratch_shapes=[
                 pltpu.VMEM((slots, beads, beads), jnp.float32),
                 pltpu.VMEM((slots, beads, beads), jnp.float32),
@@ -279,7 +284,7 @@
                 pltpu.SMEM((slots + 1,), jnp.int32),
             ],
         ),
-        out_shape=[jax.ShapeDtypeStruct(share, jnp.float32)] * CHUNKS,
+        out_shape=[jax.ShapeDtypeStruct(share, jnp.float32)] * (2 * CHUNKS),
         compiler_params=pltpu.CompilerParams(vmem_limit_bytes=56 * 1024 * 1024),
     )(off, mask, me, strip, below, above, force)
 
@@ -380,8 +385,8 @@
     return lax.ppermute(x, axis, [(i, i ^ flip) for i in range(lax.axis_size(axis))])
 
 
-def summed(x, plan):
-    x = x[0] + swap(x[1], "gy", 1)
+def summed(x, away, plan):
+    x = x + swap(away, "gy", 1)
     got = [swap(x[k], "gy", 2 * k) for k in range(1, plan.pairs)]
     x = functools.reduce(jnp.add, got, x[0])
     got = [swap(x[k], "gx", k) for k in range(1, plan.size_x)]
@@ -415,7 +420,7 @@
         jnp.broadcast_to(force, (16, nb * 3 * beads)),
         plan,
     )
-    parts = jnp.stack([summed(x, plan) for x in chunks])
+    parts = jnp.stack([summed(*chunks[2 * c:2 * c + 2], plan) for c in range(CHUNKS)])
     own, *messages = pack(me, parts, plan, 1.0 / frame_rows)
     got = [swap(m, "gy", 2 * k) for k, m in enumerate(messages, 1)]
     mine = jnp.concatenate([own] + got)

time: 119 us -> 118 us (level); the launches traced: 120 us -> 117 us
  Pallas kernels: 45.8 us -> 39.1 us
  waiting for transfers between devices: 30.6 us -> 35 us
  local copies, waits for them, and re-layouts: 4.02 us -> 2.26 us
    pallas_call x1, Pallas kernels: 41.9 us -> 35.2 us  [design(): pl.pallas_call(functools.partial(design_kernel, plan=plan, by_blocks=by_b...]
    ppermute x24, waiting for transfers between devices: 27.7 us -> 30.6 us  [swap(): lax.ppermute(x, axis, [(i, i ^ flip) for i in range(lax.axis_size(axis))])]
    ppermute x4, waiting for transfers between devices: 2.86 us -> 4.39 us  [shifted(): lax.ppermute(x, axis, [(i, (i + step) % count) for i in range(count)])]
    squeeze x2 -> x0, local copies, waits for them, and re-layouts: 1.48 us -> none  [summed(): x = x[0] + swap(x[1], 'gy', 1)]
  transfers between devices with their start and end apart: 28 -> 28, of which waited for: 13 -> 13; matrix products, arithmetic and copies ran while one was open for 2% -> 3% of each run, Pallas kernels for 0% -> 0%
where the time goes in v5:
time: 118 us; the launch traced here: 117 us
  Pallas kernels  39.1 us (33%)
  starting transfers between devices  36.5 us (31%)
  waiting for transfers between devices  35 us (30%)
  other arithmetic  2.92 us (2%)
  local copies, waits for them, and re-layouts  2.26 us (2%)
    pallas_call x1, Pallas kernels, design(): pl.pallas_call(functools.partial(design_kernel, plan=plan, by_blocks=by_b...  35.2 us
    ppermute x24, waiting for transfers between devices, swap(): lax.ppermute(x, axis, [(i, i ^ flip) for i in range(lax.axis_size(axis))])  30.6 us
    ppermute x24, starting transfers between devices, swap(): lax.ppermute(x, axis, [(i, i ^ flip) for i in range(lax.axis_size(axis))])  28.9 us
    ppermute x4, starting transfers between devices, shifted(): lax.ppermute(x, axis, [(i, (i + step) % count) for i in range(count)])  7.52 us
    ppermute x4, waiting for transfers between devices, shifted(): lax.ppermute(x, axis, [(i, (i + step) % count) for i in range(count)])  4.39 us
    pallas_call x1, Pallas kernels, place(): pl.pallas_call(functools.partial(place_kernel, plan=plan), grid_spec=pltp...  3.19 us
  transfers between devices with their start and end apart: 28, of which 13 were waited for; matrix products, arithmetic and copies ran while one was open for 3% of the time, Pallas kernels for 0%

profile of v5, /device:TPU:1, one launch (start us, length us, event | category | flops | bytes accessed | tf_op | source)
XLA Modules:
  0.0 116.7 jit_solution(7523242956530287212)
XLA Ops:
  0.6 0.7 convert_element_type.3
  1.3 0.7 copy.14
  2.0 4.2 %collective-permute-start.1 = (f32[2,2,4,128]{3,2,1,0:T(4,128)S(1)}, f32[2,2,4,128]{3,2,1,0:T(4,128)S(1)}, u32[]{:S(2)}, u32[]{:S(2)}) collective-permute-start(f32[2,2,4,128]{3,2,1,0:T(4,128)S(1)} %pad_maximum_fusion.2), channel_id=1, source_target_pairs={{0,24},{8,0},{16,8},{24,16},{1,25},{9,1},{17,9},{25,17},{2,26},{10... | collective-permute-start | bytes 24584 | tf_op jit(solution)/shard_map/ppermute | solution.py:381
  6.2 0.0 collective-permute-start
  6.2 0.8 collective-permute-done.1
  7.0 3.5 %collective-permute-done = f32[2,2,4,128]{3,2,1,0:T(4,128)S(1)} collective-permute-done((f32[2,2,4,128]{3,2,1,0:T(4,128)S(1)}, f32[2,2,4,128]{3,2,1,0:T(4,128)S(1)}, u32[]{:S(2)}, u32[]{:S(2)}) %collective-permute-start) | collective-permute-done | bytes 8224 | tf_op jit(solution)/shard_map/ppermute | solution.py:381
  10.5 2.2 %collective-permute-start.3 = (f32[4,2,4,128]{3,2,1,0:T(4,128)S(1)}, f32[4,2,4,128]{3,2,1,0:T(4,128)S(1)}, u32[]{:S(2)}, u32[]{:S(2)}) collective-permute-start(f32[4,2,4,128]{3,2,1,0:T(4,128)S(1)} %pad_maximum_fusion.1.strip_ref), channel_id=1, source_target_pairs={{0,7},{1,0},{2,1},{3,2},{4,3},{5,4},{6,5},{7,6},{8,15},{9,8},{10,9... | collective-permute-start | bytes 49160 | tf_op jit(solution)/shard_map/ppermute | solution.py:381
  12.7 1.2 collective-permute-start.2
  13.9 0.6 pad_add_fusion.me_ref
  14.4 0.7 copy.12
  15.1 0.1 collective-permute-done.3.above_ref
  15.2 0.0 collective-permute-done.2.below_ref
  15.2 0.6 broadcast_in_dim.15.force_ref
  15.9 35.2 %shard_map.95 = (f32[4,4,7,16,128]{4,3,2,1,0:T(8,128)}, f32[4,4,7,16,128]{4,3,2,1,0:T(8,128)}, f32[4,4,7,16,128]{4,3,2,1,0:T(8,128)}, f32[4,4,7,16,128]{4,3,2,1,0:T(8,128)}) custom-call(s32[4,8]{1,0:T(4,128)} %bitcast.97, s32[4,8]{1,0:T(4,128)} %bitcast.98, s32[4]{0:T(128)} %pad_add_fusion.me_ref, f32[4,2,4,128]{3,2,1,0:T(4,128)} %copy-done.5, ...), custom_call_target="tpu_custom_call" | custom-call | tf_op jit(solution)/shard_map/pallas_call | solution.py:266
  51.1 1.9 %collective-permute-start.4 = (f32[4,4,7,16,128]{4,3,2,1,0:T(8,128)}, f32[4,4,7,16,128]{4,3,2,1,0:T(8,128)S(1)}, u32[]{:S(2)}, u32[]{:S(2)}) collective-permute-start(f32[4,4,7,16,128]{4,3,2,1,0:T(8,128)} %get-tuple-element.13), channel_id=1, source_target_pairs={{0,1},{1,0},{2,3},{3,2},{4,5},{5,4},{6,7},{7,6},{8,9},{9,8},{10,11... | collective-permute-start | bytes 2752520 | tf_op jit(solution)/shard_map/ppermute | solution.py:385
  53.0 0.0 collective-permute-start.14
  53.0 2.3 %collective-permute-done.4 = f32[4,4,7,16,128]{4,3,2,1,0:T(8,128)S(1)} collective-permute-done((f32[4,4,7,16,128]{4,3,2,1,0:T(8,128)}, f32[4,4,7,16,128]{4,3,2,1,0:T(8,128)S(1)}, u32[]{:S(2)}, u32[]{:S(2)}) %collective-permute-start.4) | collective-permute-done | bytes 917536 | tf_op jit(solution)/shard_map/ppermute | solution.py:385
  55.3 1.3 %add.48 = f32[4,4,7,16,128]{4,3,2,1,0:T(8,128)S(1)} add(f32[4,4,7,16,128]{4,3,2,1,0:T(8,128)} %get-tuple-element.12, f32[4,4,7,16,128]{4,3,2,1,0:T(8,128)S(1)} %collective-permute-done.4) | non-fusion elementwise | flops 229376 | bytes 2752512 | tf_op jit(solution)/shard_map/add | solution.py:389
  56.7 0.8 collective-permute-start.5
  57.5 2.6 %collective-permute-start.7 = (f32[4,7,16,128]{3,2,1,0:T(8,128)S(1)}, f32[4,7,16,128]{3,2,1,0:T(8,128)S(1)}, u32[]{:S(2)}, u32[]{:S(2)}) collective-permute-start(f32[4,7,16,128]{3,2,1,0:T(8,128)S(1)} %get-tuple-element.23), channel_id=1, source_target_pairs={{0,6},{1,7},{2,4},{3,5},{4,2},{5,3},{6,0},{7,1},{8,14},{9,15},{10,... | collective-permute-start | bytes 688136 | tf_op jit(solution)/shard_map/ppermute | solution.py:385
  60.0 0.0 collective-permute-start.6
  60.0 0.0 collective-permute-done.14
  60.0 0.1 add.55
  60.2 0.3 collective-permute-start.15
  60.6 2.4 %collective-permute-start.17 = (f32[4,7,16,128]{3,2,1,0:T(8,128)S(1)}, f32[4,7,16,128]{3,2,1,0:T(8,128)S(1)}, u32[]{:S(2)}, u32[]{:S(2)}) collective-permute-start(f32[4,7,16,128]{3,2,1,0:T(8,128)S(1)} %get-tuple-element.26), channel_id=1, source_target_pairs={{0,6},{1,7},{2,4},{3,5},{4,2},{5,3},{6,0},{7,1},{8,14},{9,15},{10,... | collective-permute-start | bytes 688136 | tf_op jit(solution)/shard_map/ppermute | solution.py:385
  63.0 0.6 collective-permute-done.5
  63.6 2.1 %collective-permute-start.16 = (f32[4,7,16,128]{3,2,1,0:T(8,128)S(1)}, f32[4,7,16,128]{3,2,1,0:T(8,128)S(1)}, u32[]{:S(2)}, u32[]{:S(2)}) collective-permute-start(f32[4,7,16,128]{3,2,1,0:T(8,128)S(1)} %get-tuple-element.27), channel_id=1, source_target_pairs={{0,4},{1,5},{2,6},{3,7},{4,0},{5,1},{6,2},{7,3},{8,12},{9,13},{10,... | collective-permute-start | bytes 688136 | tf_op jit(solution)/shard_map/ppermute | solution.py:385
  65.7 4.7 %collective-permute-done.7 = f32[4,7,16,128]{3,2,1,0:T(8,128)S(1)} collective-permute-done((f32[4,7,16,128]{3,2,1,0:T(8,128)S(1)}, f32[4,7,16,128]{3,2,1,0:T(8,128)S(1)}, u32[]{:S(2)}, u32[]{:S(2)}) %collective-permute-start.7) | collective-permute-done | bytes 229408 | tf_op jit(solution)/shard_map/ppermute | solution.py:385
  70.3 0.0 collective-permute-done.6
  70.4 0.1 fusion.5
  70.4 0.1 collective-permute-start.8
  70.5 0.2 collective-permute-start.10
  70.7 2.7 %collective-permute-done.15 = f32[4,7,16,128]{3,2,1,0:T(8,128)S(1)} collective-permute-done((f32[4,7,16,128]{3,2,1,0:T(8,128)S(1)}, f32[4,7,16,128]{3,2,1,0:T(8,128)S(1)}, u32[]{:S(2)}, u32[]{:S(2)}) %collective-permute-start.15) | collective-permute-done | bytes 229408 | tf_op jit(solution)/shard_map/ppermute | solution.py:385
  73.4 0.0 collective-permute-start.9
  73.4 6.8 %collective-permute-done.17 = f32[4,7,16,128]{3,2,1,0:T(8,128)S(1)} collective-permute-done((f32[4,7,16,128]{3,2,1,0:T(8,128)S(1)}, f32[4,7,16,128]{3,2,1,0:T(8,128)S(1)}, u32[]{:S(2)}, u32[]{:S(2)}) %collective-permute-start.17) | collective-permute-done | bytes 229408 | tf_op jit(solution)/shard_map/ppermute | solution.py:385
  80.2 0.0 collective-permute-done.16
  80.2 0.1 fusion.2
  80.3 0.1 collective-permute-start.18
  80.4 0.2 collective-permute-start.20
  80.6 0.0 collective-permute-done.8
  80.6 2.5 %collective-permute-start.19 = (f32[7,16,128]{2,1,0:T(8,128)S(1)}, f32[7,16,128]{2,1,0:T(8,128)S(1)}, u32[]{:S(2)}, u32[]{:S(2)}) collective-permute-start(f32[7,16,128]{2,1,0:T(8,128)S(1)} %get-tuple-element.33), channel_id=1, source_target_pairs={{0,16},{8,24},{16,0},{24,8},{1,17},{9,25},{17,1},{25,9},{2,18},{10... | collective-permute-start | bytes 172040 | tf_op jit(solution)/shard_map/ppermute | solution.py:385
  83.0 0.0 collective-permute-done.10
  83.1 1.0 collective-permute-start.13
  84.1 1.2 %collective-permute-start.12 = (f32[7,16,128]{2,1,0:T(8,128)S(1)}, f32[7,16,128]{2,1,0:T(8,128)S(1)}, u32[]{:S(2)}, u32[]{:S(2)}) collective-permute-start(f32[7,16,128]{2,1,0:T(8,128)S(1)} %fusion.11), channel_id=1, source_target_pairs={{0,16},{8,24},{16,0},{24,8},{1,17},{9,25},{17,1},{25,9},{2,18},{10... | collective-permute-start | bytes 172040 | tf_op jit(solution)/shard_map/ppermute | solution.py:385
  85.3 1.4 %collective-permute-start.11 = (f32[7,16,128]{2,1,0:T(8,128)S(1)}, f32[7,16,128]{2,1,0:T(8,128)S(1)}, u32[]{:S(2)}, u32[]{:S(2)}) collective-permute-start(f32[7,16,128]{2,1,0:T(8,128)S(1)} %fusion.11), channel_id=1, source_target_pairs={{0,8},{8,0},{16,24},{24,16},{1,9},{9,1},{17,25},{25,17},{2,10},{10... | collective-permute-start | bytes 172040 | tf_op jit(solution)/shard_map/ppermute | solution.py:385
  86.7 1.8 %collective-permute-start.23 = (f32[7,16,128]{2,1,0:T(8,128)S(1)}, f32[7,16,128]{2,1,0:T(8,128)S(1)}, u32[]{:S(2)}, u32[]{:S(2)}) collective-permute-start(f32[7,16,128]{2,1,0:T(8,128)S(1)} %fusion.8), channel_id=1, source_target_pairs={{0,24},{8,16},{16,8},{24,0},{1,25},{9,17},{17,9},{25,1},{2,26},{10... | collective-permute-start | bytes 172040 | tf_op jit(solution)/shard_map/ppermute | solution.py:385
  88.5 0.0 collective-permute-start.22
  88.5 0.0 collective-permute-done.13
  88.6 1.7 %collective-permute-start.21 = (f32[7,16,128]{2,1,0:T(8,128)S(1)}, f32[7,16,128]{2,1,0:T(8,128)S(1)}, u32[]{:S(2)}, u32[]{:S(2)}) collective-permute-start(f32[7,16,128]{2,1,0:T(8,128)S(1)} %fusion.8), channel_id=1, source_target_pairs={{0,8},{8,0},{16,24},{24,16},{1,9},{9,1},{17,25},{25,17},{2,10},{10... | collective-permute-start | bytes 172040 | tf_op jit(solution)/shard_map/ppermute | solution.py:385
  90.3 3.5 %collective-permute-done.12 = f32[7,16,128]{2,1,0:T(8,128)S(1)} collective-permute-done((f32[7,16,128]{2,1,0:T(8,128)S(1)}, f32[7,16,128]{2,1,0:T(8,128)S(1)}, u32[]{:S(2)}, u32[]{:S(2)}) %collective-permute-start.12) | collective-permute-done | bytes 57376 | tf_op jit(solution)/shard_map/ppermute | solution.py:385
  93.8 0.0 collective-permute-done.11
  93.9 0.0 collective-permute-done.23
  93.9 2.4 %collective-permute-done.22 = f32[7,16,128]{2,1,0:T(8,128)S(1)} collective-permute-done((f32[7,16,128]{2,1,0:T(8,128)S(1)}, f32[7,16,128]{2,1,0:T(8,128)S(1)}, u32[]{:S(2)}, u32[]{:S(2)}) %collective-permute-start.22) | collective-permute-done | bytes 57376 | tf_op jit(solution)/shard_map/ppermute | solution.py:385
  96.4 0.0 copy-start.1
  96.4 0.0 copy-start.3
  96.4 0.8 shard_map.96
  97.2 1.7 %collective-permute-start.24 = (f32[6,64,128]{2,1,0:T(8,128)S(1)}, f32[6,64,128]{2,1,0:T(8,128)S(1)}, u32[]{:S(2)}, u32[]{:S(2)}) collective-permute-start(f32[6,64,128]{2,1,0:T(8,128)S(1)} %get-tuple-element.17), channel_id=1, source_target_pairs={{0,2},{1,3},{2,0},{3,1},{4,6},{5,7},{6,4},{7,5},{8,10},{9,11},{10,... | collective-permute-start | bytes 589832 | tf_op jit(solution)/shard_map/ppermute | solution.py:385
  98.9 1.1 collective-permute-start.26
  100.0 0.2 collective-permute-start.25
  100.2 1.9 %collective-permute-done.24 = f32[6,64,128]{2,1,0:T(8,128)S(1)} collective-permute-done((f32[6,64,128]{2,1,0:T(8,128)S(1)}, f32[6,64,128]{2,1,0:T(8,128)S(1)}, u32[]{:S(2)}, u32[]{:S(2)}) %collective-permute-start.24) | collective-permute-done | bytes 196640 | tf_op jit(solution)/shard_map/ppermute | solution.py:385
  102.1 3.5 %collective-permute-done.25 = f32[6,64,128]{2,1,0:T(8,128)S(1)} collective-permute-done((f32[6,64,128]{2,1,0:T(8,128)S(1)}, f32[6,64,128]{2,1,0:T(8,128)S(1)}, u32[]{:S(2)}, u32[]{:S(2)}) %collective-permute-start.25) | collective-permute-done | bytes 196640 | tf_op jit(solution)/shard_map/ppermute | solution.py:385
  105.6 5.7 %collective-permute-start.27 = (f32[29,64,128]{2,1,0:T(8,128)S(1)}, f32[29,64,128]{2,1,0:T(8,128)S(1)}, u32[]{:S(2)}, u32[]{:S(2)}) collective-permute-start(f32[29,64,128]{2,1,0:T(8,128)S(1)} %constant_dynamic-update-slice_fusion.mine_ref), channel_id=1, source_target_pairs={{0,1},{1,0},{2,3},{3,2},{4,5},{5,4},{6,7},{7,6},{8,9},{9,8},{10,11... | collective-permute-start | bytes 2850824 | tf_op jit(solution)/shard_map/ppermute | solution.py:385
  111.3 2.1 %collective-permute-done.27.other_ref = f32[29,64,128]{2,1,0:T(8,128)S(1)} collective-permute-done((f32[29,64,128]{2,1,0:T(8,128)S(1)}, f32[29,64,128]{2,1,0:T(8,128)S(1)}, u32[]{:S(2)}, u32[]{:S(2)}) %collective-permute-start.27) | collective-permute-done | bytes 950304 | tf_op jit(solution)/shard_map/ppermute | solution.py:385
  113.5 3.2 %shard_map.97 = (f32[192,1536]{1,0:T(8,128)}, f32[1,192]{1,0:T(1,128)}) custom-call(s32[4]{0:T(128)S(1)} %copy-done, s32[8,36]{1,0:T(8,128)S(1)} %copy-done.1, s32[8]{0:T(128)S(1)} %copy-done.3, f32[29,64,128]{2,1,0:T(8,128)S(1)} %constant_dynamic-update-slice_fusion.mine_ref, f32[29,64,128]{2,1,0:T(8,128)S(1)} %collective-permute-done.27.other_ref), custom_call_target="tpu_custom_call" | custom-call | tf_op jit(solution)/shard_map/pallas_call | solution.py:359
  (38 shorter events, 0.4 us)
Async XLA Ops:
  2.0 5.0 %collective-permute-start.1 = (f32[2,2,4,128]{3,2,1,0:T(4,128)S(1)}, f32[2,2,4,128]{3,2,1,0:T(4,128)S(1)}, u32[]{:S(2)}, u32[]{:S(2)}) collective-permute-start(f32[2,2,4,128]{3,2,1,0:T(4,128)S(1)} %pad_maximum_fusion.2), channel_id=1, source_target_pairs={{0,24},{8,0},{16,8},{24,16},{1,25},{9,1},{17,9},{25,17},{2,26},{10... | collective-permute-start | bytes 24584 | tf_op jit(solution)/shard_map/ppermute | solution.py:381
  6.2 4.3 %collective-permute-start = (f32[2,2,4,128]{3,2,1,0:T(4,128)S(1)}, f32[2,2,4,128]{3,2,1,0:T(4,128)S(1)}, u32[]{:S(2)}, u32[]{:S(2)}) collective-permute-start(f32[2,2,4,128]{3,2,1,0:T(4,128)S(1)} %pad_maximum_fusion.2), channel_id=1, source_target_pairs={{0,8},{8,16},{16,24},{24,0},{1,9},{9,17},{17,25},{25,1},{2,10},{10... | collective-permute-start | bytes 24584 | tf_op jit(solution)/shard_map/ppermute | solution.py:381
  10.5 5.3 %copy-start.5 = (f32[4,2,4,128]{3,2,1,0:T(4,128)}, f32[4,2,4,128]{3,2,1,0:T(4,128)S(1)}, u32[]{:S(2)}) copy-start(f32[4,2,4,128]{3,2,1,0:T(4,128)S(1)} %pad_maximum_fusion.1.strip_ref) | copy-start | bytes 49156
  10.5 4.7 %collective-permute-start.3 = (f32[4,2,4,128]{3,2,1,0:T(4,128)S(1)}, f32[4,2,4,128]{3,2,1,0:T(4,128)S(1)}, u32[]{:S(2)}, u32[]{:S(2)}) collective-permute-start(f32[4,2,4,128]{3,2,1,0:T(4,128)S(1)} %pad_maximum_fusion.1.strip_ref), channel_id=1, source_target_pairs={{0,7},{1,0},{2,1},{3,2},{4,3},{5,4},{6,5},{7,6},{8,15},{9,8},{10,9... | collective-permute-start | bytes 49160 | tf_op jit(solution)/shard_map/ppermute | solution.py:381
  12.7 2.5 %collective-permute-start.2 = (f32[4,2,4,128]{3,2,1,0:T(4,128)S(1)}, f32[4,2,4,128]{3,2,1,0:T(4,128)S(1)}, u32[]{:S(2)}, u32[]{:S(2)}) collective-permute-start(f32[4,2,4,128]{3,2,1,0:T(4,128)S(1)} %pad_maximum_fusion.1.strip_ref), channel_id=1, source_target_pairs={{0,1},{1,2},{2,3},{3,4},{4,5},{5,6},{6,7},{7,0},{8,9},{9,10},{10,1... | collective-permute-start | bytes 49160 | tf_op jit(solution)/shard_map/ppermute | solution.py:381
  15.2 0.6 copy-start.6
  15.2 0.6 copy-start.7
  51.1 4.3 %collective-permute-start.4 = (f32[4,4,7,16,128]{4,3,2,1,0:T(8,128)}, f32[4,4,7,16,128]{4,3,2,1,0:T(8,128)S(1)}, u32[]{:S(2)}, u32[]{:S(2)}) collective-permute-start(f32[4,4,7,16,128]{4,3,2,1,0:T(8,128)} %get-tuple-element.13), channel_id=1, source_target_pairs={{0,1},{1,0},{2,3},{3,2},{4,5},{5,4},{6,7},{7,6},{8,9},{9,8},{10,11... | collective-permute-start | bytes 2752520 | tf_op jit(solution)/shard_map/ppermute | solution.py:385
  53.0 7.0 %collective-permute-start.14 = (f32[4,4,7,16,128]{4,3,2,1,0:T(8,128)}, f32[4,4,7,16,128]{4,3,2,1,0:T(8,128)S(1)}, u32[]{:S(2)}, u32[]{:S(2)}) collective-permute-start(f32[4,4,7,16,128]{4,3,2,1,0:T(8,128)} %get-tuple-element.15), channel_id=1, source_target_pairs={{0,1},{1,0},{2,3},{3,2},{4,5},{5,4},{6,7},{7,6},{8,9},{9,8},{10,11... | collective-permute-start | bytes 2752520 | tf_op jit(solution)/shard_map/ppermute | solution.py:385
  56.6 3.4 %copy-start.4 = (f32[4,4,7,16,128]{4,3,2,1,0:T(8,128)S(1)}, f32[4,4,7,16,128]{4,3,2,1,0:T(8,128)}, u32[]{:S(2)}) copy-start(f32[4,4,7,16,128]{4,3,2,1,0:T(8,128)} %get-tuple-element.14) | copy-start | bytes 2752516
  56.7 6.9 %collective-permute-start.5 = (f32[4,7,16,128]{3,2,1,0:T(8,128)S(1)}, f32[4,7,16,128]{3,2,1,0:T(8,128)S(1)}, u32[]{:S(2)}, u32[]{:S(2)}) collective-permute-start(f32[4,7,16,128]{3,2,1,0:T(8,128)S(1)} %get-tuple-element.22), channel_id=1, source_target_pairs={{0,2},{1,3},{2,0},{3,1},{4,6},{5,7},{6,4},{7,5},{8,10},{9,11},{10,... | collective-permute-start | bytes 688136 | tf_op jit(solution)/shard_map/ppermute | solution.py:385
  57.5 12.9 %collective-permute-start.7 = (f32[4,7,16,128]{3,2,1,0:T(8,128)S(1)}, f32[4,7,16,128]{3,2,1,0:T(8,128)S(1)}, u32[]{:S(2)}, u32[]{:S(2)}) collective-permute-start(f32[4,7,16,128]{3,2,1,0:T(8,128)S(1)} %get-tuple-element.23), channel_id=1, source_target_pairs={{0,6},{1,7},{2,4},{3,5},{4,2},{5,3},{6,0},{7,1},{8,14},{9,15},{10,... | collective-permute-start | bytes 688136 | tf_op jit(solution)/shard_map/ppermute | solution.py:385
  60.0 10.3 %collective-permute-start.6 = (f32[4,7,16,128]{3,2,1,0:T(8,128)S(1)}, f32[4,7,16,128]{3,2,1,0:T(8,128)S(1)}, u32[]{:S(2)}, u32[]{:S(2)}) collective-permute-start(f32[4,7,16,128]{3,2,1,0:T(8,128)S(1)} %get-tuple-element.24), channel_id=1, source_target_pairs={{0,4},{1,5},{2,6},{3,7},{4,0},{5,1},{6,2},{7,3},{8,12},{9,13},{10,... | collective-permute-start | bytes 688136 | tf_op jit(solution)/shard_map/ppermute | solution.py:385
  60.2 13.2 %collective-permute-start.15 = (f32[4,7,16,128]{3,2,1,0:T(8,128)S(1)}, f32[4,7,16,128]{3,2,1,0:T(8,128)S(1)}, u32[]{:S(2)}, u32[]{:S(2)}) collective-permute-start(f32[4,7,16,128]{3,2,1,0:T(8,128)S(1)} %get-tuple-element.25), channel_id=1, source_target_pairs={{0,2},{1,3},{2,0},{3,1},{4,6},{5,7},{6,4},{7,5},{8,10},{9,11},{10,... | collective-permute-start | bytes 688136 | tf_op jit(solution)/shard_map/ppermute | solution.py:385
  60.6 19.6 %collective-permute-start.17 = (f32[4,7,16,128]{3,2,1,0:T(8,128)S(1)}, f32[4,7,16,128]{3,2,1,0:T(8,128)S(1)}, u32[]{:S(2)}, u32[]{:S(2)}) collective-permute-start(f32[4,7,16,128]{3,2,1,0:T(8,128)S(1)} %get-tuple-element.26), channel_id=1, source_target_pairs={{0,6},{1,7},{2,4},{3,5},{4,2},{5,3},{6,0},{7,1},{8,14},{9,15},{10,... | collective-permute-start | bytes 688136 | tf_op jit(solution)/shard_map/ppermute | solution.py:385
  63.6 16.7 %collective-permute-start.16 = (f32[4,7,16,128]{3,2,1,0:T(8,128)S(1)}, f32[4,7,16,128]{3,2,1,0:T(8,128)S(1)}, u32[]{:S(2)}, u32[]{:S(2)}) collective-permute-start(f32[4,7,16,128]{3,2,1,0:T(8,128)S(1)} %get-tuple-element.27), channel_id=1, source_target_pairs={{0,4},{1,5},{2,6},{3,7},{4,0},{5,1},{6,2},{7,3},{8,12},{9,13},{10,... | collective-permute-start | bytes 688136 | tf_op jit(solution)/shard_map/ppermute | solution.py:385
  70.4 10.1 %collective-permute-start.8 = (f32[7,16,128]{2,1,0:T(8,128)S(1)}, f32[7,16,128]{2,1,0:T(8,128)S(1)}, u32[]{:S(2)}, u32[]{:S(2)}) collective-permute-start(f32[7,16,128]{2,1,0:T(8,128)S(1)} %get-tuple-element.28), channel_id=1, source_target_pairs={{0,8},{8,0},{16,24},{24,16},{1,9},{9,1},{17,25},{25,17},{2,10},{10... | collective-permute-start | bytes 172040 | tf_op jit(solution)/shard_map/ppermute | solution.py:385
  70.5 12.5 %collective-permute-start.10 = (f32[7,16,128]{2,1,0:T(8,128)S(1)}, f32[7,16,128]{2,1,0:T(8,128)S(1)}, u32[]{:S(2)}, u32[]{:S(2)}) collective-permute-start(f32[7,16,128]{2,1,0:T(8,128)S(1)} %get-tuple-element.29), channel_id=1, source_target_pairs={{0,24},{8,16},{16,8},{24,0},{1,25},{9,17},{17,9},{25,1},{2,26},{10... | collective-permute-start | bytes 172040 | tf_op jit(solution)/shard_map/ppermute | solution.py:385
  73.4 9.6 %collective-permute-start.9 = (f32[7,16,128]{2,1,0:T(8,128)S(1)}, f32[7,16,128]{2,1,0:T(8,128)S(1)}, u32[]{:S(2)}, u32[]{:S(2)}) collective-permute-start(f32[7,16,128]{2,1,0:T(8,128)S(1)} %get-tuple-element.30), channel_id=1, source_target_pairs={{0,16},{8,24},{16,0},{24,8},{1,17},{9,25},{17,1},{25,9},{2,18},{10... | collective-permute-start | bytes 172040 | tf_op jit(solution)/shard_map/ppermute | solution.py:385
  80.3 5.0 %collective-permute-start.18 = (f32[7,16,128]{2,1,0:T(8,128)S(1)}, f32[7,16,128]{2,1,0:T(8,128)S(1)}, u32[]{:S(2)}, u32[]{:S(2)}) collective-permute-start(f32[7,16,128]{2,1,0:T(8,128)S(1)} %get-tuple-element.31), channel_id=1, source_target_pairs={{0,8},{8,0},{16,24},{24,16},{1,9},{9,1},{17,25},{25,17},{2,10},{10... | collective-permute-start | bytes 172040 | tf_op jit(solution)/shard_map/ppermute | solution.py:385
  80.4 6.3 %collective-permute-start.20 = (f32[7,16,128]{2,1,0:T(8,128)S(1)}, f32[7,16,128]{2,1,0:T(8,128)S(1)}, u32[]{:S(2)}, u32[]{:S(2)}) collective-permute-start(f32[7,16,128]{2,1,0:T(8,128)S(1)} %get-tuple-element.32), channel_id=1, source_target_pairs={{0,24},{8,16},{16,8},{24,0},{1,25},{9,17},{17,9},{25,1},{2,26},{10... | collective-permute-start | bytes 172040 | tf_op jit(solution)/shard_map/ppermute | solution.py:385
  80.6 15.8 %copy-start = (s32[4]{0:T(128)S(1)}, s32[4]{0:T(128)}, u32[]{:S(2)}) copy-start(s32[4]{0:T(128)} %pad_add_fusion.me_ref) | copy-start | bytes 52
  80.6 15.8 %copy-start.2 = (s32[4,15]{1,0:T(4,128)S(1)}, s32[4,15]{1,0:T(4,128)}, u32[]{:S(2)}) copy-start(s32[4,15]{1,0:T(4,128)} %constant.38.clone.send_ref) | copy-start | bytes 724
  80.6 6.1 %collective-permute-start.19 = (f32[7,16,128]{2,1,0:T(8,128)S(1)}, f32[7,16,128]{2,1,0:T(8,128)S(1)}, u32[]{:S(2)}, u32[]{:S(2)}) collective-permute-start(f32[7,16,128]{2,1,0:T(8,128)S(1)} %get-tuple-element.33), channel_id=1, source_target_pairs={{0,16},{8,24},{16,0},{24,8},{1,17},{9,25},{17,1},{25,9},{2,18},{10... | collective-permute-start | bytes 172040 | tf_op jit(solution)/shard_map/ppermute | solution.py:385
  83.1 5.5 %collective-permute-start.13 = (f32[7,16,128]{2,1,0:T(8,128)S(1)}, f32[7,16,128]{2,1,0:T(8,128)S(1)}, u32[]{:S(2)}, u32[]{:S(2)}) collective-permute-start(f32[7,16,128]{2,1,0:T(8,128)S(1)} %fusion.11), channel_id=1, source_target_pairs={{0,24},{8,16},{16,8},{24,0},{1,25},{9,17},{17,9},{25,1},{2,26},{10... | collective-permute-start | bytes 172040 | tf_op jit(solution)/shard_map/ppermute | solution.py:385
  84.1 9.7 %collective-permute-start.12 = (f32[7,16,128]{2,1,0:T(8,128)S(1)}, f32[7,16,128]{2,1,0:T(8,128)S(1)}, u32[]{:S(2)}, u32[]{:S(2)}) collective-permute-start(f32[7,16,128]{2,1,0:T(8,128)S(1)} %fusion.11), channel_id=1, source_target_pairs={{0,16},{8,24},{16,0},{24,8},{1,17},{9,25},{17,1},{25,9},{2,18},{10... | collective-permute-start | bytes 172040 | tf_op jit(solution)/shard_map/ppermute | solution.py:385
  85.3 8.6 %collective-permute-start.11 = (f32[7,16,128]{2,1,0:T(8,128)S(1)}, f32[7,16,128]{2,1,0:T(8,128)S(1)}, u32[]{:S(2)}, u32[]{:S(2)}) collective-permute-start(f32[7,16,128]{2,1,0:T(8,128)S(1)} %fusion.11), channel_id=1, source_target_pairs={{0,8},{8,0},{16,24},{24,16},{1,9},{9,1},{17,25},{25,17},{2,10},{10... | collective-permute-start | bytes 172040 | tf_op jit(solution)/shard_map/ppermute | solution.py:385
  86.7 7.2 %collective-permute-start.23 = (f32[7,16,128]{2,1,0:T(8,128)S(1)}, f32[7,16,128]{2,1,0:T(8,128)S(1)}, u32[]{:S(2)}, u32[]{:S(2)}) collective-permute-start(f32[7,16,128]{2,1,0:T(8,128)S(1)} %fusion.8), channel_id=1, source_target_pairs={{0,24},{8,16},{16,8},{24,0},{1,25},{9,17},{17,9},{25,1},{2,26},{10... | collective-permute-start | bytes 172040 | tf_op jit(solution)/shard_map/ppermute | solution.py:385
  88.5 7.8 %collective-permute-start.22 = (f32[7,16,128]{2,1,0:T(8,128)S(1)}, f32[7,16,128]{2,1,0:T(8,128)S(1)}, u32[]{:S(2)}, u32[]{:S(2)}) collective-permute-start(f32[7,16,128]{2,1,0:T(8,128)S(1)} %fusion.8), channel_id=1, source_target_pairs={{0,16},{8,24},{16,0},{24,8},{1,17},{9,25},{17,1},{25,9},{2,18},{10... | collective-permute-start | bytes 172040 | tf_op jit(solution)/shard_map/ppermute | solution.py:385
  88.6 7.7 %collective-permute-start.21 = (f32[7,16,128]{2,1,0:T(8,128)S(1)}, f32[7,16,128]{2,1,0:T(8,128)S(1)}, u32[]{:S(2)}, u32[]{:S(2)}) collective-permute-start(f32[7,16,128]{2,1,0:T(8,128)S(1)} %fusion.8), channel_id=1, source_target_pairs={{0,8},{8,0},{16,24},{24,16},{1,9},{9,1},{17,25},{25,17},{2,10},{10... | collective-permute-start | bytes 172040 | tf_op jit(solution)/shard_map/ppermute | solution.py:385
  96.4 17.1 %copy-start.1 = (s32[8,36]{1,0:T(8,128)S(1)}, s32[8,36]{1,0:T(8,128)}, u32[]{:S(2)}) copy-start(s32[8,36]{1,0:T(8,128)} %constant.39.clone.table_ref) | copy-start | bytes 3460
  96.4 17.1 %copy-start.3 = (s32[8]{0:T(128)S(1)}, s32[8]{0:T(128)}, u32[]{:S(2)}) copy-start(s32[8]{0:T(128)} %constant.40.clone.rhs_at_ref) | copy-start | bytes 100
  97.2 4.9 %collective-permute-start.24 = (f32[6,64,128]{2,1,0:T(8,128)S(1)}, f32[6,64,128]{2,1,0:T(8,128)S(1)}, u32[]{:S(2)}, u32[]{:S(2)}) collective-permute-start(f32[6,64,128]{2,1,0:T(8,128)S(1)} %get-tuple-element.17), channel_id=1, source_target_pairs={{0,2},{1,3},{2,0},{3,1},{4,6},{5,7},{6,4},{7,5},{8,10},{9,11},{10,... | collective-permute-start | bytes 589832 | tf_op jit(solution)/shard_map/ppermute | solution.py:385
  98.9 6.7 %collective-permute-start.26 = (f32[3,64,128]{2,1,0:T(8,128)S(1)}, f32[3,64,128]{2,1,0:T(8,128)S(1)}, u32[]{:S(2)}, u32[]{:S(2)}) collective-permute-start(f32[3,64,128]{2,1,0:T(8,128)S(1)} %get-tuple-element.19), channel_id=1, source_target_pairs={{0,6},{1,7},{2,4},{3,5},{4,2},{5,3},{6,0},{7,1},{8,14},{9,15},{10,... | collective-permute-start | bytes 294920 | tf_op jit(solution)/shard_map/ppermute | solution.py:385
  100.0 5.6 %collective-permute-start.25 = (f32[6,64,128]{2,1,0:T(8,128)S(1)}, f32[6,64,128]{2,1,0:T(8,128)S(1)}, u32[]{:S(2)}, u32[]{:S(2)}) collective-permute-start(f32[6,64,128]{2,1,0:T(8,128)S(1)} %get-tuple-element.18), channel_id=1, source_target_pairs={{0,4},{1,5},{2,6},{3,7},{4,0},{5,1},{6,2},{7,3},{8,12},{9,13},{10,... | collective-permute-start | bytes 589832 | tf_op jit(solution)/shard_map/ppermute | solution.py:385
  105.6 7.8 %collective-permute-start.27 = (f32[29,64,128]{2,1,0:T(8,128)S(1)}, f32[29,64,128]{2,1,0:T(8,128)S(1)}, u32[]{:S(2)}, u32[]{:S(2)}) collective-permute-start(f32[29,64,128]{2,1,0:T(8,128)S(1)} %constant_dynamic-update-slice_fusion.mine_ref), channel_id=1, source_target_pairs={{0,1},{1,0},{2,3},{3,2},{4,5},{5,4},{6,7},{7,6},{8,9},{9,8},{10,11... | collective-permute-start | bytes 2850824 | tf_op jit(solution)/shard_map/ppermute | solution.py:385

commit v6 on v5

--- a/solution.py
+++ b/solution.py
@@ -87,22 +87,23 @@
                         self.table[d, u * TILES + c] = -1
 
 
-def gram_tiles(me_ref, force_ref, rows_s, left_s, upper, lower, plan):
+def gram_tiles(me_ref, force_ref, rows_s, left_s, outs, plan):
     def put(tile, value):
         g, s = plan.place[tile]
+        out = outs[s // plan.slots]
         for h in range(2):
             for z in range(plan.size_x):
                 at = h * HALF // 2 + z * plan.part
-                out = (upper, lower)[h][s // plan.slots]
-                out[g ^ me_ref[1], z ^ me_ref[2], s % plan.slots] = value[at:at + plan.part]
+                out[h ^ me_ref[0], g ^ me_ref[1], z ^ me_ref[2], s % plan.slots] = value[at:at + plan.part]
 
     used = {(g, s) for g, s in plan.place.values()}
     for g in range(plan.pairs):
         for s in range(plan.room):
             if (g, s) not in used:
-                for out in (upper, lower):
+                plan_tile = jnp.zeros((plan.part, HALF), jnp.float32)
+                for h in range(2):
                     for z in range(plan.size_x):
-                        out[s // plan.slots][g ^ me_ref[1], z ^ me_ref[2], s % plan.slots] = jnp.zeros((plan.part, HALF), jnp.float32)
+                        outs[s // plan.slots][h ^ me_ref[0], g ^ me_ref[1], z ^ me_ref[2], s % plan.slots] = plan_tile
     for p in range(PAIRS):
         left_s[...] = rows_s[:, p * K:(p + 1) * K].T
         for q in range(p, PAIRS):
@@ -119,8 +120,8 @@
 
 
 def design_kernel(off_ref, mask_ref, me_ref, strip_ref, below_ref, above_ref, force_ref, *refs, plan, by_blocks, beads, slots, groups):
-    outs = refs[:2 * CHUNKS]
-    pos_s, lt_s, code_s, w_s, res_s, rows_s, left_s, near_s, col_s, list_s = refs[2 * CHUNKS:]
+    outs = refs[:CHUNKS]
+    pos_s, lt_s, code_s, w_s, res_s, rows_s, left_s, near_s, col_s, list_s = refs[CHUNKS:]
     b = pl.program_id(0)
     bx = b // by_blocks
     by = b % by_blocks
@@ -252,17 +253,14 @@
 
     @pl.when(b == pl.num_programs(0) - 1)
     def _():
-        for core in range(2):
-            @pl.when(me_ref[0] == core)
-            def _(core=core):
-                gram_tiles(me_ref, force_ref, rows_s, left_s, outs[core::2], outs[1 - core::2], plan)
+        gram_tiles(me_ref, force_ref, rows_s, left_s, outs, plan)
 
 
 def design(off, mask, me, strip, below, above, force, plan, groups=4):
     nb, slots = off.shape
     x_rows, by_blocks, _, beads = strip.shape
     total = nb * 3 * beads
-    share = (plan.pairs, plan.size_x, plan.slots, plan.part, HALF)
+    share = (2, plan.pairs, plan.size_x, plan.slots, plan.part, HALF)
     return pl.pallas_call(
         functools.partial(design_kernel, plan=plan, by_blocks=by_blocks, beads=beads, slots=slots, groups=groups),
         grid_spec=pltpu.PrefetchScalarGridSpec(
@@ -270,7 +268,7 @@
             grid=(nb,),
             in_specs=[pl.BlockSpec(strip.shape, lambda b, *_: (0, 0, 0, 0))] * 3
             + [pl.BlockSpec((16, total), lambda b, *_: (0, 0))],
-            out_specs=[pl.BlockSpec(share, lambda b, *_: (0,) * 5)] * (2 * CHUNKS),
+            out_specs=[pl.BlockSpec(share, lambda b, *_: (0,) * 6)] * CHUNKS,
             scratch_shapes=[
                 pltpu.VMEM((slots, beads, beads), jnp.float32),
                 pltpu.VMEM((slots, beads, beads), jnp.float32),
@@ -284,7 +282,7 @@
                 pltpu.SMEM((slots + 1,), jnp.int32),
             ],
         ),
-        out_shape=[jax.ShapeDtypeStruct(share, jnp.float32)] * (2 * CHUNKS),
+        out_shape=[jax.ShapeDtypeStruct(share, jnp.float32)] * CHUNKS,
         compiler_params=pltpu.CompilerParams(vmem_limit_bytes=56 * 1024 * 1024),
     )(off, mask, me, strip, below, above, force)
 
@@ -385,8 +383,8 @@
     return lax.ppermute(x, axis, [(i, i ^ flip) for i in range(lax.axis_size(axis))])
 
 
-def summed(x, away, plan):
-    x = x + swap(away, "gy", 1)
+def summed(x, plan):
+    x = x[0] + swap(x[1], "gy", 1)
     got = [swap(x[k], "gy", 2 * k) for k in range(1, plan.pairs)]
     x = functools.reduce(jnp.add, got, x[0])
     got = [swap(x[k], "gx", k) for k in range(1, plan.size_x)]
@@ -420,7 +418,7 @@
         jnp.broadcast_to(force, (16, nb * 3 * beads)),
         plan,
     )
-    parts = jnp.stack([summed(*chunks[2 * c:2 * c + 2], plan) for c in range(CHUNKS)])
+    parts = jnp.stack([summed(x, plan) for x in chunks])
     own, *messages = pack(me, parts, plan, 1.0 / frame_rows)
     got = [swap(m, "gy", 2 * k) for k, m in enumerate(messages, 1)]
     mine = jnp.concatenate([own] + got)

time: 118 us -> 114 us (0.966)
  waiting for transfers between devices: 35 us -> 27.2 us
  starting transfers between devices: 36.5 us -> 39.5 us
  local copies, waits for them, and re-layouts: 2.26 us -> 4.02 us
    ppermute x24, waiting for transfers between devices: 30.6 us -> 24.3 us  [swap(): lax.ppermute(x, axis, [(i, i ^ flip) for i in range(lax.axis_size(axis))])]
    ppermute x24, starting transfers between devices: 28.9 us -> 32.3 us  [swap(): lax.ppermute(x, axis, [(i, i ^ flip) for i in range(lax.axis_size(axis))])]
    ppermute x4, waiting for transfers between devices: 4.39 us -> 2.86 us  [shifted(): lax.ppermute(x, axis, [(i, (i + step) % count) for i in range(count)])]
    squeeze x0 -> x2, local copies, waits for them, and re-layouts: none -> 1.48 us  [summed(): x = x[0] + swap(x[1], 'gy', 1)]
  transfers between devices with their start and end apart: 28 -> 28, of which waited for: 13 -> 13; matrix products, arithmetic and copies ran while one was open for 3% -> 2% of each run, Pallas kernels for 0% -> 0%
where the time goes in v6:
time: 114 us; the launch traced here: 113 us
  Pallas kernels  39.9 us (35%)
  starting transfers between devices  39.5 us (35%)
  waiting for transfers between devices  27.2 us (24%)
  local copies, waits for them, and re-layouts  4.02 us (4%)
  other arithmetic  1.75 us (2%)
    pallas_call x1, Pallas kernels, design(): pl.pallas_call(functools.partial(design_kernel, plan=plan, by_blocks=by_b...  35.9 us
    ppermute x24, starting transfers between devices, swap(): lax.ppermute(x, axis, [(i, i ^ flip) for i in range(lax.axis_size(axis))])  32.3 us
    ppermute x24, waiting for transfers between devices, swap(): lax.ppermute(x, axis, [(i, i ^ flip) for i in range(lax.axis_size(axis))])  24.3 us
    ppermute x4, starting transfers between devices, shifted(): lax.ppermute(x, axis, [(i, (i + step) % count) for i in range(count)])  7.18 us
    pallas_call x1, Pallas kernels, place(): pl.pallas_call(functools.partial(place_kernel, plan=plan), grid_spec=pltp...  3.19 us
    ppermute x4, waiting for transfers between devices, shifted(): lax.ppermute(x, axis, [(i, (i + step) % count) for i in range(count)])  2.86 us
  transfers between devices with their start and end apart: 28, of which 13 were waited for; matrix products, arithmetic and copies ran while one was open for 2% of the time, Pallas kernels for 0%

profile of v6, /device:TPU:1, one launch (start us, length us, event | category | flops | bytes accessed | tf_op | source)
XLA Modules:
  0.0 113.2 jit_solution(596571196956987403)
XLA Ops:
  0.6 0.7 copy.14
  1.3 0.7 convert_element_type.3
  2.0 2.2 %collective-permute-start = (f32[2,2,4,128]{3,2,1,0:T(4,128)S(1)}, f32[2,2,4,128]{3,2,1,0:T(4,128)S(1)}, u32[]{:S(2)}, u32[]{:S(2)}) collective-permute-start(f32[2,2,4,128]{3,2,1,0:T(4,128)S(1)} %pad_maximum_fusion.2), channel_id=1, source_target_pairs={{0,8},{8,16},{16,24},{24,0},{1,9},{9,17},{17,25},{25,1},{2,10},{10... | collective-permute-start | bytes 24584 | tf_op jit(solution)/shard_map/ppermute | solution.py:379
  4.2 2.1 %collective-permute-start.1 = (f32[2,2,4,128]{3,2,1,0:T(4,128)S(1)}, f32[2,2,4,128]{3,2,1,0:T(4,128)S(1)}, u32[]{:S(2)}, u32[]{:S(2)}) collective-permute-start(f32[2,2,4,128]{3,2,1,0:T(4,128)S(1)} %pad_maximum_fusion.2), channel_id=1, source_target_pairs={{0,24},{8,0},{16,8},{24,16},{1,25},{9,1},{17,9},{25,17},{2,26},{10... | collective-permute-start | bytes 24584 | tf_op jit(solution)/shard_map/ppermute | solution.py:379
  6.3 1.0 collective-permute-done
  7.3 0.0 collective-permute-done.1
  7.3 2.9 %collective-permute-start.2 = (f32[4,2,4,128]{3,2,1,0:T(4,128)S(1)}, f32[4,2,4,128]{3,2,1,0:T(4,128)S(1)}, u32[]{:S(2)}, u32[]{:S(2)}) collective-permute-start(f32[4,2,4,128]{3,2,1,0:T(4,128)S(1)} %pad_maximum_fusion.1.strip_ref), channel_id=1, source_target_pairs={{0,1},{1,2},{2,3},{3,4},{4,5},{5,6},{6,7},{7,0},{8,9},{9,10},{10,1... | collective-permute-start | bytes 49160 | tf_op jit(solution)/shard_map/ppermute | solution.py:379
  10.2 0.6 pad_add_fusion.me_ref
  10.8 0.7 copy.12
  11.5 0.0 collective-permute-done.2.below_ref
  11.5 1.9 %collective-permute-done.3.above_ref = f32[4,2,4,128]{3,2,1,0:T(4,128)S(1)} collective-permute-done((f32[4,2,4,128]{3,2,1,0:T(4,128)S(1)}, f32[4,2,4,128]{3,2,1,0:T(4,128)S(1)}, u32[]{:S(2)}, u32[]{:S(2)}) %collective-permute-start.3) | collective-permute-done | bytes 16416 | tf_op jit(solution)/shard_map/ppermute | solution.py:379
  13.4 0.6 broadcast_in_dim.15.force_ref
  14.0 35.9 %shard_map.95 = (f32[2,4,4,7,16,128]{5,4,3,2,1,0:T(8,128)}, f32[2,4,4,7,16,128]{5,4,3,2,1,0:T(8,128)}) custom-call(s32[4,8]{1,0:T(4,128)} %bitcast.105, s32[4,8]{1,0:T(4,128)} %bitcast.106, s32[4]{0:T(128)} %pad_add_fusion.me_ref, f32[4,2,4,128]{3,2,1,0:T(4,128)} %copy-done.6, f32[4,2,4,128]{3,2,1,0:T(4,128)} %copy-done.7, f32[4,2,4,128]{3,2,1,0:T(4,128)} %copy-done.8, ...), custom_call_target="tpu_custom_call" | custom-call | tf_op jit(solution)/shard_map/pallas_call | solution.py:264
  50.0 1.4 %slice_bitcast_fusion.1 = f32[4,4,7,16,128]{4,3,2,1,0:T(8,128)S(1)} fusion(f32[2,4,4,7,16,128]{5,4,3,2,1,0:T(8,128)} %get-tuple-element.10), kind=kLoop, calls=%fused_computation.3 | loop fusion | bytes 1835008 | tf_op jit(solution)/shard_map/squeeze | solution.py:387
  51.4 0.1 collective-permute-start.4
  51.5 0.3 copy-done.4
  51.7 0.1 slice_bitcast_fusion
  51.8 0.3 collective-permute-start.14
  52.1 1.8 %collective-permute-done.4 = f32[4,4,7,16,128]{4,3,2,1,0:T(8,128)S(1)} collective-permute-done((f32[4,4,7,16,128]{4,3,2,1,0:T(8,128)S(1)}, f32[4,4,7,16,128]{4,3,2,1,0:T(8,128)S(1)}, u32[]{:S(2)}, u32[]{:S(2)}) %collective-permute-start.4) | collective-permute-done | bytes 917536 | tf_op jit(solution)/shard_map/ppermute | solution.py:383
  53.9 0.1 bitcast_add_fusion.1
  54.1 0.1 slice_bitcast_fusion.8
  54.1 2.6 %collective-permute-start.5 = (f32[4,7,16,128]{3,2,1,0:T(8,128)S(1)}, f32[4,7,16,128]{3,2,1,0:T(8,128)S(1)}, u32[]{:S(2)}, u32[]{:S(2)}) collective-permute-start(f32[4,7,16,128]{3,2,1,0:T(8,128)S(1)} %get-tuple-element.18), channel_id=1, source_target_pairs={{0,2},{1,3},{2,0},{3,1},{4,6},{5,7},{6,4},{7,5},{8,10},{9,11},{10,... | collective-permute-start | bytes 688136 | tf_op jit(solution)/shard_map/ppermute | solution.py:383
  56.7 0.1 collective-permute-start.6
  56.8 1.2 %collective-permute-start.7 = (f32[4,7,16,128]{3,2,1,0:T(8,128)S(1)}, f32[4,7,16,128]{3,2,1,0:T(8,128)S(1)}, u32[]{:S(2)}, u32[]{:S(2)}) collective-permute-start(f32[4,7,16,128]{3,2,1,0:T(8,128)S(1)} %get-tuple-element.19), channel_id=1, source_target_pairs={{0,6},{1,7},{2,4},{3,5},{4,2},{5,3},{6,0},{7,1},{8,14},{9,15},{10,... | collective-permute-start | bytes 688136 | tf_op jit(solution)/shard_map/ppermute | solution.py:383
  58.0 0.0 collective-permute-done.14
  58.0 0.1 bitcast_add_fusion
  58.2 1.4 %collective-permute-start.15 = (f32[4,7,16,128]{3,2,1,0:T(8,128)S(1)}, f32[4,7,16,128]{3,2,1,0:T(8,128)S(1)}, u32[]{:S(2)}, u32[]{:S(2)}) collective-permute-start(f32[4,7,16,128]{3,2,1,0:T(8,128)S(1)} %get-tuple-element.21), channel_id=1, source_target_pairs={{0,2},{1,3},{2,0},{3,1},{4,6},{5,7},{6,4},{7,5},{8,10},{9,11},{10,... | collective-permute-start | bytes 688136 | tf_op jit(solution)/shard_map/ppermute | solution.py:383
  59.6 0.1 collective-permute-start.16
  59.7 2.9 %collective-permute-done.5 = f32[4,7,16,128]{3,2,1,0:T(8,128)S(1)} collective-permute-done((f32[4,7,16,128]{3,2,1,0:T(8,128)S(1)}, f32[4,7,16,128]{3,2,1,0:T(8,128)S(1)}, u32[]{:S(2)}, u32[]{:S(2)}) %collective-permute-start.5) | collective-permute-done | bytes 229408 | tf_op jit(solution)/shard_map/ppermute | solution.py:383
  62.6 1.0 collective-permute-start.17
  63.6 4.8 %collective-permute-done.6 = f32[4,7,16,128]{3,2,1,0:T(8,128)S(1)} collective-permute-done((f32[4,7,16,128]{3,2,1,0:T(8,128)S(1)}, f32[4,7,16,128]{3,2,1,0:T(8,128)S(1)}, u32[]{:S(2)}, u32[]{:S(2)}) %collective-permute-start.6) | collective-permute-done | bytes 229408 | tf_op jit(solution)/shard_map/ppermute | solution.py:383
  68.4 0.0 collective-permute-done.7
  68.4 0.1 fusion.5
  68.5 4.0 %collective-permute-start.10 = (f32[7,16,128]{2,1,0:T(8,128)S(1)}, f32[7,16,128]{2,1,0:T(8,128)S(1)}, u32[]{:S(2)}, u32[]{:S(2)}) collective-permute-start(f32[7,16,128]{2,1,0:T(8,128)S(1)} %get-tuple-element.25), channel_id=1, source_target_pairs={{0,24},{8,16},{16,8},{24,0},{1,25},{9,17},{17,9},{25,1},{2,26},{10... | collective-permute-start | bytes 172040 | tf_op jit(solution)/shard_map/ppermute | solution.py:383
  72.5 0.0 copy-start.2
  72.5 2.4 %collective-permute-start.9 = (f32[7,16,128]{2,1,0:T(8,128)S(1)}, f32[7,16,128]{2,1,0:T(8,128)S(1)}, u32[]{:S(2)}, u32[]{:S(2)}) collective-permute-start(f32[7,16,128]{2,1,0:T(8,128)S(1)} %get-tuple-element.26), channel_id=1, source_target_pairs={{0,16},{8,24},{16,0},{24,8},{1,17},{9,25},{17,1},{25,9},{2,18},{10... | collective-permute-start | bytes 172040 | tf_op jit(solution)/shard_map/ppermute | solution.py:383
  74.9 3.3 %collective-permute-done.16 = f32[4,7,16,128]{3,2,1,0:T(8,128)S(1)} collective-permute-done((f32[4,7,16,128]{3,2,1,0:T(8,128)S(1)}, f32[4,7,16,128]{3,2,1,0:T(8,128)S(1)}, u32[]{:S(2)}, u32[]{:S(2)}) %collective-permute-start.16) | collective-permute-done | bytes 229408 | tf_op jit(solution)/shard_map/ppermute | solution.py:383
  78.2 0.0 collective-permute-done.17
  78.2 0.1 fusion.2
  78.3 1.0 collective-permute-start.18
  79.3 3.3 %collective-permute-start.19 = (f32[7,16,128]{2,1,0:T(8,128)S(1)}, f32[7,16,128]{2,1,0:T(8,128)S(1)}, u32[]{:S(2)}, u32[]{:S(2)}) collective-permute-start(f32[7,16,128]{2,1,0:T(8,128)S(1)} %get-tuple-element.29), channel_id=1, source_target_pairs={{0,16},{8,24},{16,0},{24,8},{1,17},{9,25},{17,1},{25,9},{2,18},{10... | collective-permute-start | bytes 172040 | tf_op jit(solution)/shard_map/ppermute | solution.py:383
  82.6 0.0 collective-permute-done.9
  82.6 0.3 collective-permute-start.11
  83.0 3.3 %collective-permute-start.12 = (f32[7,16,128]{2,1,0:T(8,128)S(1)}, f32[7,16,128]{2,1,0:T(8,128)S(1)}, u32[]{:S(2)}, u32[]{:S(2)}) collective-permute-start(f32[7,16,128]{2,1,0:T(8,128)S(1)} %fusion.11), channel_id=1, source_target_pairs={{0,16},{8,24},{16,0},{24,8},{1,17},{9,25},{17,1},{25,9},{2,18},{10... | collective-permute-start | bytes 172040 | tf_op jit(solution)/shard_map/ppermute | solution.py:383
  86.2 0.0 collective-permute-done.18
  86.2 0.0 collective-permute-start.13
  86.2 0.0 collective-permute-done.19
  86.2 1.2 %collective-permute-done.20 = f32[7,16,128]{2,1,0:T(8,128)S(1)} collective-permute-done((f32[7,16,128]{2,1,0:T(8,128)S(1)}, f32[7,16,128]{2,1,0:T(8,128)S(1)}, u32[]{:S(2)}, u32[]{:S(2)}) %collective-permute-start.20) | collective-permute-done | bytes 57376 | tf_op jit(solution)/shard_map/ppermute | solution.py:383
  87.5 0.1 collective-permute-start.21
  87.5 2.3 %collective-permute-start.22 = (f32[7,16,128]{2,1,0:T(8,128)S(1)}, f32[7,16,128]{2,1,0:T(8,128)S(1)}, u32[]{:S(2)}, u32[]{:S(2)}) collective-permute-start(f32[7,16,128]{2,1,0:T(8,128)S(1)} %fusion.8), channel_id=1, source_target_pairs={{0,16},{8,24},{16,0},{24,8},{1,17},{9,25},{17,1},{25,9},{2,18},{10... | collective-permute-start | bytes 172040 | tf_op jit(solution)/shard_map/ppermute | solution.py:383
  89.9 0.0 collective-permute-done.11
  89.9 1.2 %collective-permute-start.23 = (f32[7,16,128]{2,1,0:T(8,128)S(1)}, f32[7,16,128]{2,1,0:T(8,128)S(1)}, u32[]{:S(2)}, u32[]{:S(2)}) collective-permute-start(f32[7,16,128]{2,1,0:T(8,128)S(1)} %fusion.8), channel_id=1, source_target_pairs={{0,24},{8,16},{16,8},{24,0},{1,25},{9,17},{17,9},{25,1},{2,26},{10... | collective-permute-start | bytes 172040 | tf_op jit(solution)/shard_map/ppermute | solution.py:383
  91.1 0.7 collective-permute-done.13
  91.8 3.3 %collective-permute-done.22 = f32[7,16,128]{2,1,0:T(8,128)S(1)} collective-permute-done((f32[7,16,128]{2,1,0:T(8,128)S(1)}, f32[7,16,128]{2,1,0:T(8,128)S(1)}, u32[]{:S(2)}, u32[]{:S(2)}) %collective-permute-start.22) | collective-permute-done | bytes 57376 | tf_op jit(solution)/shard_map/ppermute | solution.py:383
  95.1 0.2 collective-permute-done.23
  95.4 0.8 shard_map.96
  96.2 1.1 collective-permute-start.24
  97.3 0.8 collective-permute-start.25
  98.1 0.8 collective-permute-start.26
  98.9 1.8 %collective-permute-done.24 = f32[6,64,128]{2,1,0:T(8,128)S(1)} collective-permute-done((f32[6,64,128]{2,1,0:T(8,128)S(1)}, f32[6,64,128]{2,1,0:T(8,128)S(1)}, u32[]{:S(2)}, u32[]{:S(2)}) %collective-permute-start.24) | collective-permute-done | bytes 196640 | tf_op jit(solution)/shard_map/ppermute | solution.py:383
  100.8 2.1 %collective-permute-done.25 = f32[6,64,128]{2,1,0:T(8,128)S(1)} collective-permute-done((f32[6,64,128]{2,1,0:T(8,128)S(1)}, f32[6,64,128]{2,1,0:T(8,128)S(1)}, u32[]{:S(2)}, u32[]{:S(2)}) %collective-permute-start.25) | collective-permute-done | bytes 196640 | tf_op jit(solution)/shard_map/ppermute | solution.py:383
  102.9 5.0 %collective-permute-start.27 = (f32[29,64,128]{2,1,0:T(8,128)S(1)}, f32[29,64,128]{2,1,0:T(8,128)S(1)}, u32[]{:S(2)}, u32[]{:S(2)}) collective-permute-start(f32[29,64,128]{2,1,0:T(8,128)S(1)} %constant_dynamic-update-slice_fusion.mine_ref), channel_id=1, source_target_pairs={{0,1},{1,0},{2,3},{3,2},{4,5},{5,4},{6,7},{7,6},{8,9},{9,8},{10,11... | collective-permute-start | bytes 2850824 | tf_op jit(solution)/shard_map/ppermute | solution.py:383
  107.9 2.1 %collective-permute-done.27.other_ref = f32[29,64,128]{2,1,0:T(8,128)S(1)} collective-permute-done((f32[29,64,128]{2,1,0:T(8,128)S(1)}, f32[29,64,128]{2,1,0:T(8,128)S(1)}, u32[]{:S(2)}, u32[]{:S(2)}) %collective-permute-start.27) | collective-permute-done | bytes 950304 | tf_op jit(solution)/shard_map/ppermute | solution.py:383
  110.1 3.2 %shard_map.97 = (f32[192,1536]{1,0:T(8,128)}, f32[1,192]{1,0:T(1,128)}) custom-call(s32[4]{0:T(128)S(1)} %copy-done, s32[8,36]{1,0:T(8,128)S(1)} %copy-done.1, s32[8]{0:T(128)S(1)} %copy-done.3, f32[29,64,128]{2,1,0:T(8,128)S(1)} %constant_dynamic-update-slice_fusion.mine_ref, f32[29,64,128]{2,1,0:T(8,128)S(1)} %collective-permute-done.27.other_ref), custom_call_target="tpu_custom_call" | custom-call | tf_op jit(solution)/shard_map/pallas_call | solution.py:357
  (42 shorter events, 0.3 us)
Async XLA Ops:
  2.0 5.2 %collective-permute-start = (f32[2,2,4,128]{3,2,1,0:T(4,128)S(1)}, f32[2,2,4,128]{3,2,1,0:T(4,128)S(1)}, u32[]{:S(2)}, u32[]{:S(2)}) collective-permute-start(f32[2,2,4,128]{3,2,1,0:T(4,128)S(1)} %pad_maximum_fusion.2), channel_id=1, source_target_pairs={{0,8},{8,16},{16,24},{24,0},{1,9},{9,17},{17,25},{25,1},{2,10},{10... | collective-permute-start | bytes 24584 | tf_op jit(solution)/shard_map/ppermute | solution.py:379
  4.2 3.1 %collective-permute-start.1 = (f32[2,2,4,128]{3,2,1,0:T(4,128)S(1)}, f32[2,2,4,128]{3,2,1,0:T(4,128)S(1)}, u32[]{:S(2)}, u32[]{:S(2)}) collective-permute-start(f32[2,2,4,128]{3,2,1,0:T(4,128)S(1)} %pad_maximum_fusion.2), channel_id=1, source_target_pairs={{0,24},{8,0},{16,8},{24,16},{1,25},{9,1},{17,9},{25,17},{2,26},{10... | collective-permute-start | bytes 24584 | tf_op jit(solution)/shard_map/ppermute | solution.py:379
  7.3 6.7 %copy-start.6 = (f32[4,2,4,128]{3,2,1,0:T(4,128)}, f32[4,2,4,128]{3,2,1,0:T(4,128)S(1)}, u32[]{:S(2)}) copy-start(f32[4,2,4,128]{3,2,1,0:T(4,128)S(1)} %pad_maximum_fusion.1.strip_ref) | copy-start | bytes 49156
  7.3 4.2 %collective-permute-start.2 = (f32[4,2,4,128]{3,2,1,0:T(4,128)S(1)}, f32[4,2,4,128]{3,2,1,0:T(4,128)S(1)}, u32[]{:S(2)}, u32[]{:S(2)}) collective-permute-start(f32[4,2,4,128]{3,2,1,0:T(4,128)S(1)} %pad_maximum_fusion.1.strip_ref), channel_id=1, source_target_pairs={{0,1},{1,2},{2,3},{3,4},{4,5},{5,6},{6,7},{7,0},{8,9},{9,10},{10,1... | collective-permute-start | bytes 49160 | tf_op jit(solution)/shard_map/ppermute | solution.py:379
  10.2 3.2 %collective-permute-start.3 = (f32[4,2,4,128]{3,2,1,0:T(4,128)S(1)}, f32[4,2,4,128]{3,2,1,0:T(4,128)S(1)}, u32[]{:S(2)}, u32[]{:S(2)}) collective-permute-start(f32[4,2,4,128]{3,2,1,0:T(4,128)S(1)} %pad_maximum_fusion.1.strip_ref), channel_id=1, source_target_pairs={{0,7},{1,0},{2,1},{3,2},{4,3},{5,4},{6,5},{7,6},{8,15},{9,8},{10,9... | collective-permute-start | bytes 49160 | tf_op jit(solution)/shard_map/ppermute | solution.py:379
  11.5 2.5 %copy-start.7 = (f32[4,2,4,128]{3,2,1,0:T(4,128)}, f32[4,2,4,128]{3,2,1,0:T(4,128)S(1)}, u32[]{:S(2)}) copy-start(f32[4,2,4,128]{3,2,1,0:T(4,128)S(1)} %collective-permute-done.2.below_ref) | copy-start | bytes 49156
  13.4 0.6 copy-start.8
  50.0 1.8 %copy-start.4 = (f32[2,4,4,7,16,128]{5,4,3,2,1,0:T(8,128)S(1)}, f32[2,4,4,7,16,128]{5,4,3,2,1,0:T(8,128)}, u32[]{:S(2)}) copy-start(f32[2,4,4,7,16,128]{5,4,3,2,1,0:T(8,128)} %get-tuple-element.11) | copy-start | bytes 5505028
  50.0 4.0 %copy-start.5 = (f32[2,4,4,7,16,128]{5,4,3,2,1,0:T(8,128)S(1)}, f32[2,4,4,7,16,128]{5,4,3,2,1,0:T(8,128)}, u32[]{:S(2)}) copy-start(f32[2,4,4,7,16,128]{5,4,3,2,1,0:T(8,128)} %get-tuple-element.10) | copy-start | bytes 5505028
  51.4 2.5 %collective-permute-start.4 = (f32[4,4,7,16,128]{4,3,2,1,0:T(8,128)S(1)}, f32[4,4,7,16,128]{4,3,2,1,0:T(8,128)S(1)}, u32[]{:S(2)}, u32[]{:S(2)}) collective-permute-start(f32[4,4,7,16,128]{4,3,2,1,0:T(8,128)S(1)} %slice_bitcast_fusion.1), channel_id=1, source_target_pairs={{0,1},{1,0},{2,3},{3,2},{4,5},{5,4},{6,7},{7,6},{8,9},{9,8},{10,11... | collective-permute-start | bytes 2752520 | tf_op jit(solution)/shard_map/ppermute | solution.py:383
  51.8 6.2 %collective-permute-start.14 = (f32[4,4,7,16,128]{4,3,2,1,0:T(8,128)S(1)}, f32[4,4,7,16,128]{4,3,2,1,0:T(8,128)S(1)}, u32[]{:S(2)}, u32[]{:S(2)}) collective-permute-start(f32[4,4,7,16,128]{4,3,2,1,0:T(8,128)S(1)} %slice_bitcast_fusion), channel_id=1, source_target_pairs={{0,1},{1,0},{2,3},{3,2},{4,5},{5,4},{6,7},{7,6},{8,9},{9,8},{10,11... | collective-permute-start | bytes 2752520 | tf_op jit(solution)/shard_map/ppermute | solution.py:383
  54.1 8.5 %collective-permute-start.5 = (f32[4,7,16,128]{3,2,1,0:T(8,128)S(1)}, f32[4,7,16,128]{3,2,1,0:T(8,128)S(1)}, u32[]{:S(2)}, u32[]{:S(2)}) collective-permute-start(f32[4,7,16,128]{3,2,1,0:T(8,128)S(1)} %get-tuple-element.18), channel_id=1, source_target_pairs={{0,2},{1,3},{2,0},{3,1},{4,6},{5,7},{6,4},{7,5},{8,10},{9,11},{10,... | collective-permute-start | bytes 688136 | tf_op jit(solution)/shard_map/ppermute | solution.py:383
  56.7 11.7 %collective-permute-start.6 = (f32[4,7,16,128]{3,2,1,0:T(8,128)S(1)}, f32[4,7,16,128]{3,2,1,0:T(8,128)S(1)}, u32[]{:S(2)}, u32[]{:S(2)}) collective-permute-start(f32[4,7,16,128]{3,2,1,0:T(8,128)S(1)} %get-tuple-element.20), channel_id=1, source_target_pairs={{0,4},{1,5},{2,6},{3,7},{4,0},{5,1},{6,2},{7,3},{8,12},{9,13},{10,... | collective-permute-start | bytes 688136 | tf_op jit(solution)/shard_map/ppermute | solution.py:383
  56.8 11.6 %collective-permute-start.7 = (f32[4,7,16,128]{3,2,1,0:T(8,128)S(1)}, f32[4,7,16,128]{3,2,1,0:T(8,128)S(1)}, u32[]{:S(2)}, u32[]{:S(2)}) collective-permute-start(f32[4,7,16,128]{3,2,1,0:T(8,128)S(1)} %get-tuple-element.19), channel_id=1, source_target_pairs={{0,6},{1,7},{2,4},{3,5},{4,2},{5,3},{6,0},{7,1},{8,14},{9,15},{10,... | collective-permute-start | bytes 688136 | tf_op jit(solution)/shard_map/ppermute | solution.py:383
  58.2 14.3 %collective-permute-start.15 = (f32[4,7,16,128]{3,2,1,0:T(8,128)S(1)}, f32[4,7,16,128]{3,2,1,0:T(8,128)S(1)}, u32[]{:S(2)}, u32[]{:S(2)}) collective-permute-start(f32[4,7,16,128]{3,2,1,0:T(8,128)S(1)} %get-tuple-element.21), channel_id=1, source_target_pairs={{0,2},{1,3},{2,0},{3,1},{4,6},{5,7},{6,4},{7,5},{8,10},{9,11},{10,... | collective-permute-start | bytes 688136 | tf_op jit(solution)/shard_map/ppermute | solution.py:383
  59.6 18.6 %collective-permute-start.16 = (f32[4,7,16,128]{3,2,1,0:T(8,128)S(1)}, f32[4,7,16,128]{3,2,1,0:T(8,128)S(1)}, u32[]{:S(2)}, u32[]{:S(2)}) collective-permute-start(f32[4,7,16,128]{3,2,1,0:T(8,128)S(1)} %get-tuple-element.23), channel_id=1, source_target_pairs={{0,4},{1,5},{2,6},{3,7},{4,0},{5,1},{6,2},{7,3},{8,12},{9,13},{10,... | collective-permute-start | bytes 688136 | tf_op jit(solution)/shard_map/ppermute | solution.py:383
  62.6 15.7 %collective-permute-start.17 = (f32[4,7,16,128]{3,2,1,0:T(8,128)S(1)}, f32[4,7,16,128]{3,2,1,0:T(8,128)S(1)}, u32[]{:S(2)}, u32[]{:S(2)}) collective-permute-start(f32[4,7,16,128]{3,2,1,0:T(8,128)S(1)} %get-tuple-element.22), channel_id=1, source_target_pairs={{0,6},{1,7},{2,4},{3,5},{4,2},{5,3},{6,0},{7,1},{8,14},{9,15},{10,... | collective-permute-start | bytes 688136 | tf_op jit(solution)/shard_map/ppermute | solution.py:383
  68.5 14.1 %collective-permute-start.10 = (f32[7,16,128]{2,1,0:T(8,128)S(1)}, f32[7,16,128]{2,1,0:T(8,128)S(1)}, u32[]{:S(2)}, u32[]{:S(2)}) collective-permute-start(f32[7,16,128]{2,1,0:T(8,128)S(1)} %get-tuple-element.25), channel_id=1, source_target_pairs={{0,24},{8,16},{16,8},{24,0},{1,25},{9,17},{17,9},{25,1},{2,26},{10... | collective-permute-start | bytes 172040 | tf_op jit(solution)/shard_map/ppermute | solution.py:383
  72.5 10.1 %collective-permute-start.8 = (f32[7,16,128]{2,1,0:T(8,128)S(1)}, f32[7,16,128]{2,1,0:T(8,128)S(1)}, u32[]{:S(2)}, u32[]{:S(2)}) collective-permute-start(f32[7,16,128]{2,1,0:T(8,128)S(1)} %get-tuple-element.24), channel_id=1, source_target_pairs={{0,8},{8,0},{16,24},{24,16},{1,9},{9,1},{17,25},{25,17},{2,10},{10... | collective-permute-start | bytes 172040 | tf_op jit(solution)/shard_map/ppermute | solution.py:383
  72.5 22.9 %copy-start = (s32[4]{0:T(128)S(1)}, s32[4]{0:T(128)}, u32[]{:S(2)}) copy-start(s32[4]{0:T(128)} %pad_add_fusion.me_ref) | copy-start | bytes 52
  72.5 22.9 %copy-start.2 = (s32[4,15]{1,0:T(4,128)S(1)}, s32[4,15]{1,0:T(4,128)}, u32[]{:S(2)}) copy-start(s32[4,15]{1,0:T(4,128)} %constant.38.clone.send_ref) | copy-start | bytes 724
  72.5 10.1 %collective-permute-start.9 = (f32[7,16,128]{2,1,0:T(8,128)S(1)}, f32[7,16,128]{2,1,0:T(8,128)S(1)}, u32[]{:S(2)}, u32[]{:S(2)}) collective-permute-start(f32[7,16,128]{2,1,0:T(8,128)S(1)} %get-tuple-element.26), channel_id=1, source_target_pairs={{0,16},{8,24},{16,0},{24,8},{1,17},{9,25},{17,1},{25,9},{2,18},{10... | collective-permute-start | bytes 172040 | tf_op jit(solution)/shard_map/ppermute | solution.py:383
  78.3 7.9 %collective-permute-start.18 = (f32[7,16,128]{2,1,0:T(8,128)S(1)}, f32[7,16,128]{2,1,0:T(8,128)S(1)}, u32[]{:S(2)}, u32[]{:S(2)}) collective-permute-start(f32[7,16,128]{2,1,0:T(8,128)S(1)} %get-tuple-element.27), channel_id=1, source_target_pairs={{0,8},{8,0},{16,24},{24,16},{1,9},{9,1},{17,25},{25,17},{2,10},{10... | collective-permute-start | bytes 172040 | tf_op jit(solution)/shard_map/ppermute | solution.py:383
  79.3 6.9 %collective-permute-start.19 = (f32[7,16,128]{2,1,0:T(8,128)S(1)}, f32[7,16,128]{2,1,0:T(8,128)S(1)}, u32[]{:S(2)}, u32[]{:S(2)}) collective-permute-start(f32[7,16,128]{2,1,0:T(8,128)S(1)} %get-tuple-element.29), channel_id=1, source_target_pairs={{0,16},{8,24},{16,0},{24,8},{1,17},{9,25},{17,1},{25,9},{2,18},{10... | collective-permute-start | bytes 172040 | tf_op jit(solution)/shard_map/ppermute | solution.py:383
  82.6 4.9 %collective-permute-start.20 = (f32[7,16,128]{2,1,0:T(8,128)S(1)}, f32[7,16,128]{2,1,0:T(8,128)S(1)}, u32[]{:S(2)}, u32[]{:S(2)}) collective-permute-start(f32[7,16,128]{2,1,0:T(8,128)S(1)} %get-tuple-element.28), channel_id=1, source_target_pairs={{0,24},{8,16},{16,8},{24,0},{1,25},{9,17},{17,9},{25,1},{2,26},{10... | collective-permute-start | bytes 172040 | tf_op jit(solution)/shard_map/ppermute | solution.py:383
  82.6 7.2 %collective-permute-start.11 = (f32[7,16,128]{2,1,0:T(8,128)S(1)}, f32[7,16,128]{2,1,0:T(8,128)S(1)}, u32[]{:S(2)}, u32[]{:S(2)}) collective-permute-start(f32[7,16,128]{2,1,0:T(8,128)S(1)} %fusion.11), channel_id=1, source_target_pairs={{0,8},{8,0},{16,24},{24,16},{1,9},{9,1},{17,25},{25,17},{2,10},{10... | collective-permute-start | bytes 172040 | tf_op jit(solution)/shard_map/ppermute | solution.py:383
  83.0 8.1 %collective-permute-start.12 = (f32[7,16,128]{2,1,0:T(8,128)S(1)}, f32[7,16,128]{2,1,0:T(8,128)S(1)}, u32[]{:S(2)}, u32[]{:S(2)}) collective-permute-start(f32[7,16,128]{2,1,0:T(8,128)S(1)} %fusion.11), channel_id=1, source_target_pairs={{0,16},{8,24},{16,0},{24,8},{1,17},{9,25},{17,1},{25,9},{2,18},{10... | collective-permute-start | bytes 172040 | tf_op jit(solution)/shard_map/ppermute | solution.py:383
  86.2 5.6 %collective-permute-start.13 = (f32[7,16,128]{2,1,0:T(8,128)S(1)}, f32[7,16,128]{2,1,0:T(8,128)S(1)}, u32[]{:S(2)}, u32[]{:S(2)}) collective-permute-start(f32[7,16,128]{2,1,0:T(8,128)S(1)} %fusion.11), channel_id=1, source_target_pairs={{0,24},{8,16},{16,8},{24,0},{1,25},{9,17},{17,9},{25,1},{2,26},{10... | collective-permute-start | bytes 172040 | tf_op jit(solution)/shard_map/ppermute | solution.py:383
  87.5 4.3 %collective-permute-start.21 = (f32[7,16,128]{2,1,0:T(8,128)S(1)}, f32[7,16,128]{2,1,0:T(8,128)S(1)}, u32[]{:S(2)}, u32[]{:S(2)}) collective-permute-start(f32[7,16,128]{2,1,0:T(8,128)S(1)} %fusion.8), channel_id=1, source_target_pairs={{0,8},{8,0},{16,24},{24,16},{1,9},{9,1},{17,25},{25,17},{2,10},{10... | collective-permute-start | bytes 172040 | tf_op jit(solution)/shard_map/ppermute | solution.py:383
  87.5 7.6 %collective-permute-start.22 = (f32[7,16,128]{2,1,0:T(8,128)S(1)}, f32[7,16,128]{2,1,0:T(8,128)S(1)}, u32[]{:S(2)}, u32[]{:S(2)}) collective-permute-start(f32[7,16,128]{2,1,0:T(8,128)S(1)} %fusion.8), channel_id=1, source_target_pairs={{0,16},{8,24},{16,0},{24,8},{1,17},{9,25},{17,1},{25,9},{2,18},{10... | collective-permute-start | bytes 172040 | tf_op jit(solution)/shard_map/ppermute | solution.py:383
  89.9 5.4 %collective-permute-start.23 = (f32[7,16,128]{2,1,0:T(8,128)S(1)}, f32[7,16,128]{2,1,0:T(8,128)S(1)}, u32[]{:S(2)}, u32[]{:S(2)}) collective-permute-start(f32[7,16,128]{2,1,0:T(8,128)S(1)} %fusion.8), channel_id=1, source_target_pairs={{0,24},{8,16},{16,8},{24,0},{1,25},{9,17},{17,9},{25,1},{2,26},{10... | collective-permute-start | bytes 172040 | tf_op jit(solution)/shard_map/ppermute | solution.py:383
  95.3 14.7 %copy-start.1 = (s32[8,36]{1,0:T(8,128)S(1)}, s32[8,36]{1,0:T(8,128)}, u32[]{:S(2)}) copy-start(s32[8,36]{1,0:T(8,128)} %constant.39.clone.table_ref) | copy-start | bytes 3460
  95.3 14.7 %copy-start.3 = (s32[8]{0:T(128)S(1)}, s32[8]{0:T(128)}, u32[]{:S(2)}) copy-start(s32[8]{0:T(128)} %constant.40.clone.rhs_at_ref) | copy-start | bytes 100
  96.2 4.6 %collective-permute-start.24 = (f32[6,64,128]{2,1,0:T(8,128)S(1)}, f32[6,64,128]{2,1,0:T(8,128)S(1)}, u32[]{:S(2)}, u32[]{:S(2)}) collective-permute-start(f32[6,64,128]{2,1,0:T(8,128)S(1)} %get-tuple-element.13), channel_id=1, source_target_pairs={{0,2},{1,3},{2,0},{3,1},{4,6},{5,7},{6,4},{7,5},{8,10},{9,11},{10,... | collective-permute-start | bytes 589832 | tf_op jit(solution)/shard_map/ppermute | solution.py:383
  97.3 5.6 %collective-permute-start.25 = (f32[6,64,128]{2,1,0:T(8,128)S(1)}, f32[6,64,128]{2,1,0:T(8,128)S(1)}, u32[]{:S(2)}, u32[]{:S(2)}) collective-permute-start(f32[6,64,128]{2,1,0:T(8,128)S(1)} %get-tuple-element.14), channel_id=1, source_target_pairs={{0,4},{1,5},{2,6},{3,7},{4,0},{5,1},{6,2},{7,3},{8,12},{9,13},{10,... | collective-permute-start | bytes 589832 | tf_op jit(solution)/shard_map/ppermute | solution.py:383
  98.1 4.8 %collective-permute-start.26 = (f32[3,64,128]{2,1,0:T(8,128)S(1)}, f32[3,64,128]{2,1,0:T(8,128)S(1)}, u32[]{:S(2)}, u32[]{:S(2)}) collective-permute-start(f32[3,64,128]{2,1,0:T(8,128)S(1)} %get-tuple-element.15), channel_id=1, source_target_pairs={{0,6},{1,7},{2,4},{3,5},{4,2},{5,3},{6,0},{7,1},{8,14},{9,15},{10,... | collective-permute-start | bytes 294920 | tf_op jit(solution)/shard_map/ppermute | solution.py:383
  102.9 7.2 %collective-permute-start.27 = (f32[29,64,128]{2,1,0:T(8,128)S(1)}, f32[29,64,128]{2,1,0:T(8,128)S(1)}, u32[]{:S(2)}, u32[]{:S(2)}) collective-permute-start(f32[29,64,128]{2,1,0:T(8,128)S(1)} %constant_dynamic-update-slice_fusion.mine_ref), channel_id=1, source_target_pairs={{0,1},{1,0},{2,3},{3,2},{4,5},{5,4},{6,7},{7,6},{8,9},{9,8},{10,11... | collective-permute-start | bytes 2850824 | tf_op jit(solution)/shard_map/ppermute | solution.py:383
